TPU v7x, 32 devices: a whole 2x2x4 slice. The times are simulated.
32 devices in a mesh: dp: 4 (over z), tr: 4 (over x, core), tc: 2 (over y).
Axes of the slice: x: 2, y: 2, z: 4, core: 2. Of those that a mesh axis runs over, the one named last changes fastest.
Arguments:
- layer_input: bfloat16 [8192, 1152], P(('dp', 'tr'), 'tc'), may hold values from -6 to 6
- picture: int32 [8192], P('dp'), may hold values from 0 to 7, as said below
- token_kept: int32 [8192], P('dp'), may hold values from 0 to 1, as said below
- ln1_gain: float32 [1152], P('tc'), may hold values from 0.5 to 1.5
- ln1_bias: float32 [1152], P('tc'), may hold values from -1.75 to 1.75
- w_query: bfloat16 [1152, 1152], P('tc', 'tr'), may hold values from -0.1875 to 0.1875
- b_query: float32 [1152], P(('tr', 'tc')), may hold values from -3 to 3
- w_key: bfloat16 [1152, 1152], P('tc', 'tr'), may hold values from -0.1875 to 0.1875
- w_value: bfloat16 [1152, 1152], P('tc', 'tr'), may hold values from -0.1875 to 0.1875
- b_value: float32 [1152], P(('tr', 'tc')), may hold values from -0.3125 to 0.3125
- w_out: bfloat16 [1152, 1152], P('tr', 'tc'), may hold values from -3 to 3
- b_out: float32 [1152], P('tc'), may hold values from -1.75 to 1.75
- ln2_gain: float32 [1152], P('tc'), may hold values from 0.5 to 1.5
- ln2_bias: float32 [1152], P('tc'), may hold values from -1.75 to 1.75
- w_up: bfloat16 [1152, 4304], P('tc', 'tr'), may hold values from -0.1875 to 0.1875
- b_up: float32 [4304], P(('tr', 'tc')), may hold values from -3 to 3
- w_down: bfloat16 [4304, 1152], P('tr', 'tc'), may hold values from -0.09375 to 0.09375
- b_down: float32 [1152], P('tc'), may hold values from -1.75 to 1.75
- grad_out: bfloat16 [8192, 1152], P(('dp', 'tr'), 'tc'), may hold values from -6 to 6
Outputs:
- result: bfloat16 [8192, 1152], P(('dp', 'tr'), 'tc')
- grad_layer_input: bfloat16 [8192, 1152], P(('dp', 'tr'), 'tc')
- grad_ln1_gain: float32 [1152], P('tc')
- grad_ln1_bias: float32 [1152], P('tc')
- grad_w_query: float32 [1152, 1152], P('tc', 'tr')
- grad_b_query: float32 [1152], P(('tr', 'tc'))
- grad_w_key: float32 [1152, 1152], P('tc', 'tr')
- grad_w_value: float32 [1152, 1152], P('tc', 'tr')
- grad_b_value: float32 [1152], P(('tr', 'tc'))
- grad_w_out: float32 [1152, 1152], P('tr', 'tc')
- grad_b_out: float32 [1152], P('tc')
- grad_ln2_gain: float32 [1152], P('tc')
- grad_ln2_bias: float32 [1152], P('tc')
- grad_w_up: float32 [1152, 4304], P('tc', 'tr')
- grad_b_up: float32 [4304], P(('tr', 'tc'))
- grad_w_down: float32 [4304, 1152], P('tr', 'tc')
- grad_b_down: float32 [1152], P('tc')
Inputs may be any that keep to these rules, and one draw needn't show every extreme that they name: Within each packed row of 2048 tokens the picture numbers run 0 to 7 in order, each picture a contiguous run. `token_kept`: padding stands at the end of each packed row, at least one token and at most 128 of them, inside the row's last picture.
All inputs are finite; a program needn't handle non-finite values.
Results may differ from a plain program's by a relative error of at most 0.015.
Values may be sent and summed in bfloat16 or wider, within the bound.
No kernel may reach another device: no remote copies, remote signals or barrier semaphores. Data moves between devices by JAX's collectives and lax.ppermute only.
A program may use at most 128 MiB of HBM per device.

v0:
```python
import jax
import jax.numpy as jnp
from jax import lax
from jax.sharding import PartitionSpec as P

DH = 72
SEQ = 2048
BLOCK = 512


EPSILON = 1e-06
GELU_C = 0.7978845608028654
GELU_A = 0.044715
MASKED = -1e30


def row_sums(first, second):
    return lax.psum((first, second), "tc")


def norm_forward(values, gains, biases):
    row_width = values.shape[1] * lax.axis_size("tc")
    totals, squares = row_sums(jnp.sum(values, axis=1), jnp.sum(values * values, axis=1))
    means = totals / row_width
    inv_root = lax.rsqrt(squares / row_width - means * means + EPSILON)[:, None]
    normed = (values - means[:, None]) * inv_root
    return (normed, inv_root, normed * gains + biases)


def norm_backward(gradient, normed, inv_root, gains):
    row_width = gradient.shape[1] * lax.axis_size("tc")
    weighted = gradient * gains
    totals, along = row_sums(jnp.sum(weighted, axis=1), jnp.sum(weighted * normed, axis=1))
    grad_in = inv_root * (
        weighted - totals[:, None] / row_width - normed * (along[:, None] / row_width)
    )
    return (grad_in, jnp.sum(gradient * normed, axis=0), jnp.sum(gradient, axis=0))


def rows_in(values):
    return lax.all_gather(values, "tr", axis=0, tiled=True)


def cols_in(values):
    return lax.all_gather(values, "tc", axis=1, tiled=True)


def rows_out(term_fn, row_count):
    return lax.psum_scatter(
        term_fn(jnp.int32(0), row_count * lax.axis_size("tr")),
        "tr",
        scatter_dimension=0,
        tiled=True,
    )


def grad_rows_in(values):
    return lax.all_gather(values, "tr", axis=0, tiled=True)


def grad_cols_out(terms):
    return lax.psum_scatter(terms, "tc", scatter_dimension=1, tiled=True)


def grad_rows_out(term_fn, row_count):
    return lax.psum_scatter(
        term_fn(jnp.int32(0), row_count * lax.axis_size("tr")),
        "tr",
        scatter_dimension=0,
        tiled=True,
    )


def slice_rows(values, first_row, row_count):
    return lax.dynamic_slice_in_dim(values, first_row, row_count, 0)


def contract_rows(left, right):
    return lax.dot_general(
        left, right, (((0,), (0,)), ((), ())), preferred_element_type=jnp.float32
    )


def right_transposed(left, right):
    return lax.dot_general(
        left, right, (((1,), (1,)), ((), ())), preferred_element_type=jnp.float32
    )


def gelu_value(upper):
    return 0.5 * upper * (1.0 + jnp.tanh(GELU_C * (upper + GELU_A * upper * upper * upper)))


def gelu_slope(upper):
    tangent = jnp.tanh(GELU_C * (upper + GELU_A * upper * upper * upper))
    return 0.5 * (1.0 + tangent) + 0.5 * upper * (1.0 - tangent * tangent) * GELU_C * (
        1.0 + 3.0 * GELU_A * upper * upper
    )


def block_scores(query_block, key_rows, picture_query, picture_keys, kept_keys, query_offset):
    raw = jnp.einsum(
        "qhd,khd->hqk", query_block, key_rows, preferred_element_type=jnp.float32
    ) * DH ** (-0.5)
    query_places = query_offset + jnp.arange(query_block.shape[0], dtype=jnp.int32)
    key_places = jnp.arange(key_rows.shape[0], dtype=jnp.int32)
    same = (picture_query[:, None] == picture_keys[None, :]) & (kept_keys[None, :] == 1)
    allowed = same | (query_places[:, None] == key_places[None, :])
    return jnp.where(allowed[None], raw, MASKED)


def block_inputs(queries, keys, values, picture, kept_flags, block_index):
    first_row = block_index * BLOCK
    seq_start = first_row // SEQ * SEQ
    query_block = slice_rows(queries, first_row, BLOCK)
    key_rows = slice_rows(keys, seq_start, SEQ)
    value_rows = slice_rows(values, seq_start, SEQ)
    scores = block_scores(
        query_block,
        key_rows,
        slice_rows(picture, first_row, BLOCK),
        slice_rows(picture, seq_start, SEQ),
        slice_rows(kept_flags, seq_start, SEQ),
        first_row - seq_start,
    )
    return (first_row, seq_start, query_block, key_rows, value_rows, scores)


def attend_forward(queries, keys, values, picture, kept_flags):
    block_count = queries.shape[0] // BLOCK

    def one_block(block_index):
        first_row, seq_start, query_block, key_rows, value_rows, scores = block_inputs(
            queries, keys, values, picture, kept_flags, block_index
        )
        highest = jnp.max(scores, axis=2, keepdims=True)
        weights = jnp.exp(scores - highest)
        totals = jnp.sum(weights, axis=2, keepdims=True)
        probs = (weights / totals).astype(jnp.bfloat16)
        attended = jnp.einsum("hqk,khd->qhd", probs, value_rows, preferred_element_type=jnp.float32)
        return (attended, (highest + jnp.log(totals))[:, :, 0])

    attended, log_totals = lax.map(one_block, jnp.arange(block_count, dtype=jnp.int32))
    return (attended.reshape(queries.shape[0], -1), log_totals)


def attend_backward(queries, keys, values, log_totals, grad_attended, picture, kept_flags):
    block_count = queries.shape[0] // BLOCK
    factor = DH ** (-0.5)

    def one_block(carry, block_index):
        grad_keys, grad_values = carry
        first_row, seq_start, query_block, key_rows, value_rows, scores = block_inputs(
            queries, keys, values, picture, kept_flags, block_index
        )
        probs = jnp.exp(scores - log_totals[block_index][:, :, None])
        grad_block = slice_rows(grad_attended, first_row, BLOCK)
        part_values = jnp.einsum(
            "hqk,qhd->khd",
            probs.astype(jnp.bfloat16),
            grad_block,
            preferred_element_type=jnp.float32,
        )
        grad_probs = jnp.einsum(
            "qhd,khd->hqk", grad_block, value_rows, preferred_element_type=jnp.float32
        )
        delta = jnp.sum(probs * grad_probs, axis=2, keepdims=True)
        grad_scores = (probs * (grad_probs - delta)).astype(jnp.bfloat16)
        grad_query = (
            jnp.einsum("hqk,khd->qhd", grad_scores, key_rows, preferred_element_type=jnp.float32)
            * factor
        )
        part_keys = (
            jnp.einsum("hqk,qhd->khd", grad_scores, query_block, preferred_element_type=jnp.float32)
            * factor
        )
        grad_keys = slice_rows(grad_keys, seq_start, SEQ) + part_keys
        grad_values = slice_rows(grad_values, seq_start, SEQ) + part_values
        return ((grad_keys, grad_values), grad_query)

    zeros = jnp.zeros(queries.shape, jnp.float32)
    (grad_keys, grad_values), grad_queries = lax.scan(
        one_block, (zeros, zeros), jnp.arange(block_count, dtype=jnp.int32)
    )
    return (grad_queries.reshape(queries.shape), grad_keys, grad_values)


def local(
    layer_input,
    picture,
    token_kept,
    ln1_gain,
    ln1_bias,
    w_query,
    b_query,
    w_key,
    w_value,
    b_value,
    w_out,
    b_out,
    ln2_gain,
    ln2_bias,
    w_up,
    b_up,
    w_down,
    b_down,
    grad_out,
):
    local_rows = layer_input.shape[0]
    residual = layer_input.astype(jnp.float32)
    normed1, root1, pre1 = norm_forward(residual, ln1_gain, ln1_bias)
    hidden1 = rows_in(pre1.astype(jnp.bfloat16))
    token_count = hidden1.shape[0]
    stacked = jnp.stack((w_query, w_key, w_value), axis=1)
    projected = lax.psum_scatter(
        jnp.einsum("td,dcf->tcf", hidden1, stacked, preferred_element_type=jnp.float32),
        "tc",
        scatter_dimension=2,
        tiled=True,
    )
    head_width = projected.shape[2]
    local_heads = head_width // DH
    queries = (projected[:, 0] + b_query).astype(jnp.bfloat16).reshape(token_count, local_heads, DH)
    keys = projected[:, 1].astype(jnp.bfloat16).reshape(token_count, local_heads, DH)
    values = (projected[:, 2] + b_value).astype(jnp.bfloat16).reshape(token_count, local_heads, DH)
    attended, log_totals = attend_forward(queries, keys, values, picture, token_kept)
    heads_all = cols_in(attended.astype(jnp.bfloat16))

    def attn_terms(first_row, row_count):
        return jnp.dot(
            slice_rows(heads_all, first_row, row_count), w_out, preferred_element_type=jnp.float32
        )

    mixed = residual + rows_out(attn_terms, local_rows) + b_out
    normed2, root2, pre2 = norm_forward(mixed, ln2_gain, ln2_bias)
    hidden2 = rows_in(pre2.astype(jnp.bfloat16))
    upper = (
        lax.psum_scatter(
            jnp.dot(hidden2, w_up, preferred_element_type=jnp.float32),
            "tc",
            scatter_dimension=1,
            tiled=True,
        )
        + b_up
    )
    activated = cols_in(gelu_value(upper).astype(jnp.bfloat16))

    def down_terms(first_row, row_count):
        return jnp.dot(
            slice_rows(activated, first_row, row_count), w_down, preferred_element_type=jnp.float32
        )

    result = mixed + rows_out(down_terms, local_rows) + b_down
    grad_result = grad_out.astype(jnp.float32)
    grad_b_down = jnp.sum(grad_result, axis=0)
    grad_full = grad_rows_in(grad_out)
    grad_w_down = contract_rows(activated, grad_full)
    grad_activated = grad_cols_out(right_transposed(grad_full, w_down))
    grad_upper = (grad_activated * gelu_slope(upper)).astype(jnp.bfloat16)
    grad_b_up = jnp.sum(grad_upper, axis=0, dtype=jnp.float32)
    grad_upper_all = lax.all_gather(grad_upper, "tc", axis=1, tiled=True)
    grad_w_up = contract_rows(hidden2, grad_upper_all)

    def norm2_terms(first_row, row_count):
        return right_transposed(slice_rows(grad_upper_all, first_row, row_count), w_up)

    grad_hidden2 = grad_rows_out(norm2_terms, local_rows)
    grad_mix_norm, grad_ln2_gain, grad_ln2_bias = norm_backward(
        grad_hidden2, normed2, root2, ln2_gain
    )
    grad_mixed = grad_result + grad_mix_norm
    grad_b_out = jnp.sum(grad_mixed, axis=0)
    grad_mixed_all = grad_rows_in(grad_mixed.astype(jnp.bfloat16))
    grad_w_out = contract_rows(heads_all, grad_mixed_all)
    grad_heads = grad_cols_out(right_transposed(grad_mixed_all, w_out)).astype(jnp.bfloat16)
    grad_queries, grad_keys, grad_values = attend_backward(
        queries,
        keys,
        values,
        log_totals,
        grad_heads.reshape(token_count, local_heads, DH),
        picture,
        token_kept,
    )
    grad_stack = jnp.stack(
        (
            grad_queries.reshape(token_count, head_width),
            grad_keys.reshape(token_count, head_width),
            grad_values.reshape(token_count, head_width),
        ),
        axis=1,
    ).astype(jnp.bfloat16)
    grad_b_query = jnp.sum(grad_stack[:, 0], axis=0, dtype=jnp.float32)
    grad_b_value = jnp.sum(grad_stack[:, 2], axis=0, dtype=jnp.float32)
    grad_stack_all = lax.all_gather(grad_stack, "tc", axis=2, tiled=True)
    grad_w_stack = jnp.einsum(
        "td,tcf->dcf", hidden1, grad_stack_all, preferred_element_type=jnp.float32
    )

    def norm1_terms(first_row, row_count):
        return jnp.einsum(
            "tcf,dcf->td",
            slice_rows(grad_stack_all, first_row, row_count),
            stacked,
            preferred_element_type=jnp.float32,
        )

    grad_hidden1 = grad_rows_out(norm1_terms, local_rows)
    grad_in_norm, grad_ln1_gain, grad_ln1_bias = norm_backward(
        grad_hidden1, normed1, root1, ln1_gain
    )
    grad_total_in = (grad_mixed + grad_in_norm).astype(jnp.bfloat16)
    weight_totals = (
        lax.psum(grad_w_stack[:, 0].astype(jnp.bfloat16), "dp").astype(jnp.float32),
        lax.psum(grad_w_stack[:, 1].astype(jnp.bfloat16), "dp").astype(jnp.float32),
        lax.psum(grad_w_stack[:, 2].astype(jnp.bfloat16), "dp").astype(jnp.float32),
        lax.psum(grad_w_out.astype(jnp.bfloat16), "dp").astype(jnp.float32),
        lax.psum(grad_w_up.astype(jnp.bfloat16), "dp").astype(jnp.float32),
        lax.psum(grad_w_down.astype(jnp.bfloat16), "dp").astype(jnp.float32),
        lax.psum(grad_b_query.astype(jnp.bfloat16), "dp").astype(jnp.float32),
        lax.psum(grad_b_value.astype(jnp.bfloat16), "dp").astype(jnp.float32),
        lax.psum(grad_b_up.astype(jnp.bfloat16), "dp").astype(jnp.float32),
    )
    small_totals = lax.psum(
        (grad_ln1_gain, grad_ln1_bias, grad_b_out, grad_ln2_gain, grad_ln2_bias, grad_b_down),
        ("dp", "tr"),
    )
    return (
        result.astype(jnp.bfloat16),
        grad_total_in,
        small_totals[0],
        small_totals[1],
        weight_totals[0],
        weight_totals[6],
        weight_totals[1],
        weight_totals[2],
        weight_totals[7],
        weight_totals[3],
        small_totals[2],
        small_totals[3],
        small_totals[4],
        weight_totals[4],
        weight_totals[8],
        weight_totals[5],
        small_totals[5],
    )


def solution(mesh):
    placed = (
        P(("dp", "tr"), "tc"),
        P("dp"),
        P("dp"),
        P("tc"),
        P("tc"),
        P("tc", "tr"),
        P(("tr", "tc")),
        P("tc", "tr"),
        P("tc", "tr"),
        P(("tr", "tc")),
        P("tr", "tc"),
        P("tc"),
        P("tc"),
        P("tc"),
        P("tc", "tr"),
        P(("tr", "tc")),
        P("tr", "tc"),
        P("tc"),
        P(("dp", "tr"), "tc"),
    )
    return jax.shard_map(
        local,
        mesh=mesh,
        in_specs=placed,
        out_specs=(
            P(("dp", "tr"), "tc"),
            P(("dp", "tr"), "tc"),
            P("tc"),
            P("tc"),
            P("tc", "tr"),
            P(("tr", "tc")),
            P("tc", "tr"),
            P("tc", "tr"),
            P(("tr", "tc")),
            P("tr", "tc"),
            P("tc"),
            P("tc"),
            P("tc"),
            P("tc", "tr"),
            P(("tr", "tc")),
            P("tr", "tc"),
            P("tc"),
        ),
        check_vma=False,
    )
```

profile of v0, /device:TPU:0, one launch (start us, length us, event | category | flops | bytes accessed | tf_op | source)
XLA Modules:
  0.0 1278.6 jit_solution(12101578684816493014)
XLA Ops:
  8.7 5.9 all-reduce.8
  16.8 25.9 %all-gather.11.cloned.1.call-done = bf16[2048,576]{0,1:T(8,128)(2,1)} async-done(((bf16[512,576]{0,1:T(8,128)(2,1)}), bf16[2048,576]{0,1:T(8,128)(2,1)}) %all-gather.11.cloned.1.call-update) | async-done | bytes 2359312 | tf_op jit(solution)/shard_map/all_gather | solution.py:41
  42.8 6.6 fusion.49
  50.2 85.0 %reduce-scatter.11.cloned.1.call-done = f32[2048,3,144]{0,2,1:T(8,128)} async-done(((f32[2048,3,288]{0,2,1:T(8,128)}), f32[2048,3,144]{0,2,1:T(8,128)}) %reduce-scatter.11.cloned.1.call-update) | async-done | bytes 3538960 | tf_op jit(solution)/shard_map/reduce_scatter | solution.py:215
  139.4 43.9 %while.31 = (s32[]{:T(128)}, bf16[4,512,2,72]{1,3,2,0:T(8,128)(2,1)}, f32[4,2,512]{2,1,0:T(2,128)S(1)}, s32[4]{0:T(128)S(1)}, s32[2048]{0:T(1024)S(1)}, /*index=...) while((s32[]{:T(128)}, ...), condition=%wide.region_8.9_spmd, body=%wide.region_5.8_spmd.sunk | while | flops 633341440 | bytes 35764680 | solution.py:143
  144.2 2.6 fusion.137
  146.8 2.7 fusion.138
  155.2 2.6 fusion.137
  157.8 2.7 fusion.138
  166.2 2.6 fusion.137
  168.7 2.7 fusion.138
  177.1 2.6 fusion.137
  179.7 2.7 fusion.138
  186.0 22.9 %all-gather.13.cloned.1.call-done = bf16[2048,288]{0,1:T(8,128)(2,1)} async-done(((bf16[2048,144]{0,1:T(8,128)(2,1)}), bf16[2048,288]{0,1:T(8,128)(2,1)}) %all-gather.13.cloned.1.call-update) | async-done | bytes 1179664 | tf_op jit(solution)/shard_map/all_gather | solution.py:45
  208.9 4.8 fusion.80
  214.4 47.3 %reduce-scatter.13.cloned.1.call-done = f32[512,576]{0,1:T(8,128)} async-done(((f32[2048,576]{0,1:T(8,128)}), f32[512,576]{0,1:T(8,128)}) %reduce-scatter.13.cloned.1.call-update) | async-done | bytes 1179664 | tf_op jit(solution)/shard_map/reduce_scatter | solution.py:49
  264.3 4.9 all-reduce.7
  271.9 15.3 %all-gather.17.cloned.1.call-done = bf16[2048,576]{0,1:T(8,128)(2,1)} async-done(((bf16[512,576]{0,1:T(8,128)(2,1)}), bf16[2048,576]{0,1:T(8,128)(2,1)}) %all-gather.17.cloned.1.call-update) | async-done | bytes 2359312 | tf_op jit(solution)/shard_map/all_gather | solution.py:58
  287.3 9.1 fusion.83
  296.4 17.0 %all-gather.15.cloned.1.call-done = bf16[2048,576]{0,1:T(8,128)(2,1)} async-done(((bf16[512,576]{0,1:T(8,128)(2,1)}), bf16[2048,576]{0,1:T(8,128)(2,1)}) %all-gather.15.cloned.1.call-update) | async-done | bytes 2359312 | tf_op jit(solution)/shard_map/all_gather | solution.py:41
  313.4 8.7 fusion.81
  322.1 205.3 %fusion.73 = (f32[2048,544]{0,1:T(8,128)}, f32[2048,544]{0,1:T(8,128)}) fusion(f32[2048,1076]{0,1:T(8,128)} %fusion.81, f32[2048,1076]{0,1:T(8,128)} %fusion.83), kind=kCustom, calls=%all-reduce-scatter.2 | all-reduce-scatter fusion | flops 4456449 | bytes 26542592
  528.2 3.4 collective-permute-start.1
  535.0 13.3 %concatenate.1 = f32[2048,550]{0,1:T(8,128)} concatenate(f32[2048,6]{0,1:T(8,128)S(1)} %collective-permute-done.1, f32[2048,544]{0,1:T(8,128)} %get-tuple-element.408), dimensions={1} | concatenate | bytes 9011200
  548.3 13.2 %concatenate = f32[2048,550]{0,1:T(8,128)} concatenate(f32[2048,6]{0,1:T(8,128)S(1)} %collective-permute-done, f32[2048,544]{0,1:T(8,128)} %get-tuple-element.407), dimensions={1} | concatenate | bytes 9011200
  561.5 8.0 fusion.74
  569.6 5.5 fusion.51
  575.6 53.3 %all-gather.25.cloned.1.call-done = bf16[2,538,2048]{2,1,0:T(8,128)(2,1)} async-done(((bf16[1,538,2048]{2,1,0:T(8,128)(2,1)}), bf16[2,538,2048]{2,1,0:T(8,128)(2,1)}) %all-gather.25.cloned.1.call-update) | async-done | bytes 4407312 | tf_op jit(solution)/shard_map/all_gather | solution.py:261
  629.0 5.1 reshape.265
  634.1 7.1 fusion.84
  641.3 49.5 %all-gather.23.cloned.1.call-done = bf16[2,538,2048]{2,1,0:T(8,128)(2,1)} async-done(((bf16[1,538,2048]{2,1,0:T(8,128)(2,1)}), bf16[2,538,2048]{2,1,0:T(8,128)(2,1)}) %all-gather.23.cloned.1.call-update) | async-done | bytes 4407312 | tf_op jit(solution)/shard_map/all_gather | solution.py:45
  690.8 5.2 reshape.263
  696.0 7.1 fusion.82
  703.3 38.0 %reduce-scatter.17.cloned.1.call-done = f32[512,576]{0,1:T(8,128)} async-done(((f32[2048,576]{0,1:T(8,128)}), f32[512,576]{0,1:T(8,128)}) %reduce-scatter.17.cloned.1.call-update) | async-done | bytes 1179664 | tf_op jit(solution)/shard_map/reduce_scatter | solution.py:66
  743.0 4.9 all-reduce.6
  748.0 43.7 %reduce-scatter.15.cloned.1.call-done = f32[512,576]{0,1:T(8,128)} async-done(((f32[2048,576]{0,1:T(8,128)}), f32[512,576]{0,1:T(8,128)}) %reduce-scatter.15.cloned.1.call-update) | async-done | bytes 1179664 | tf_op jit(solution)/shard_map/reduce_scatter | solution.py:49
  791.7 3.0 fusion.77
  796.7 24.2 %all-gather.19.cloned.1.call-done = bf16[2048,576]{0,1:T(8,128)(2,1)} async-done(((bf16[512,576]{0,1:T(8,128)(2,1)}), bf16[2048,576]{0,1:T(8,128)(2,1)}) %all-gather.19.cloned.1.call-update) | async-done | bytes 2359312 | tf_op jit(solution)/shard_map/all_gather | solution.py:58
  820.8 4.2 fusion.85
  825.3 34.6 %reduce-scatter.19.cloned.1.call-done = f32[2048,144]{0,1:T(8,128)} async-done(((f32[2048,288]{0,1:T(8,128)}), f32[2048,144]{0,1:T(8,128)}) %reduce-scatter.19.cloned.1.call-update) | async-done | bytes 1179664 | tf_op jit(solution)/shard_map/reduce_scatter | solution.py:62
  862.9 74.7 %while.32 = (s32[]{:T(128)}, f32[2048,2,72]{0,2,1:T(8,128)S(1)}, f32[2048,2,72]{0,2,1:T(8,128)}, bf16[4,512,2,72]{1,3,2,0:T(8,128)(2,1)}, s32[4]{0:T(128)S(1)}, ...) while((s32[]{:T(128)}, f32[2048,2,72]{0,2,1:T(8,128)S(1)}, ...), condition=%wide.region_25.26_spmd.clone, body=%wide.region_23.25_spmd.clone.sunk | while | flops 1547150848 | bytes 81619520 | solution.py:182
  868.9 3.6 fusion.151
  872.4 3.1 multiply_reduce_fusion.7
  875.6 2.6 multiply_convert_fusion.3
  886.6 4.8 fusion.151
  891.4 3.1 multiply_reduce_fusion.7
  894.5 2.6 multiply_convert_fusion.3
  905.5 4.8 fusion.151
  910.3 3.1 multiply_reduce_fusion.7
  913.5 2.6 multiply_convert_fusion.3
  924.5 4.8 fusion.151
  929.3 3.1 multiply_reduce_fusion.7
  932.4 2.6 multiply_convert_fusion.3
  942.6 7.4 convolution_convert_fusion.1
  950.1 7.3 convolution_convert_fusion
  959.2 32.9 %all-gather.21.cloned.1.call-done = bf16[2048,3,288]{0,2,1:T(8,128)(2,1)} async-done(((bf16[2048,3,144]{0,2,1:T(8,128)(2,1)}), bf16[2048,3,288]{0,2,1:T(8,128)(2,1)}) %all-gather.21.cloned.1.call-update) | async-done | bytes 3538960 | tf_op jit(solution)/shard_map/all_gather | solution.py:295
  992.1 5.7 fusion.52
  1000.0 6.8 convolution_bitcast_fusion
  1008.2 12.3 all-reduce.9
  1022.2 131.6 %all-reduce.14.cloned.1.call-done = (bf16[576,288]{0,1:T(8,128)(2,1)}, bf16[576,288]{0,1:T(8,128)(2,1)}, bf16[576,288]{0,1:T(8,128)(2,1)}, bf16[288,576]{1,0:T(8...) async-done(((bf16[576,288]{0,1:T(8,128)(2,1)}, bf16[576,288]{0,1:T(8,128)(2,1)}, bf16[576,288]{0,1:T(8,128)(2,1)}, bf16[288,576]{1,0:T(8,128)(2,1)}, ...) | async-done | bytes 3806224 | tf_op jit(solution)/shard_map/psum | solution.py:314
  1163.0 39.9 %reduce-scatter.21.cloned.1.call-done = f32[512,576]{0,1:T(8,128)} async-done(((f32[2048,576]{0,1:T(8,128)}), f32[512,576]{0,1:T(8,128)}) %reduce-scatter.21.cloned.1.call-update) | async-done | bytes 1179664 | tf_op jit(solution)/shard_map/reduce_scatter | solution.py:66
  1204.7 4.9 all-reduce.5
  1209.7 59.1 %all-reduce.4 = (f32[576]{0:T(1024)}, f32[576]{0:T(1024)}, f32[576]{0:T(1024)}, f32[576]{0:T(1024)}, f32[576]{0:T(1024)}, /*index=5*/f32[576]{0:T(1024)}) all-reduce(f32[576]{0:T(1024)S(1)} %get-tuple-element.330, f32[576]{0:T(1024)S(1)} %get-tuple-element.335, ...), channel_id=1, replica_groups=mesh['dp'=4,'tr'=4,'tc'=2] {'dp','tr'}, use_global_device_ids=true, to_apply=%region_32.33 | all-reduce | flops 3456 | bytes 27648 | tf_op jit(solution)/shard_map/psum | solution.py:324
  1268.7 2.8 fusion.66
  (269 shorter events, 94.4 us)
Async XLA Ops:
  7.2 306.2 %copy-start = (bf16[576,1076]{1,0:T(8,128)(2,1)S(1)}, bf16[576,1076]{1,0:T(8,128)(2,1)}, u32[]{:S(2)}) copy-start(bf16[576,1076]{1,0:T(8,128)(2,1)} %param.37) | copy-start | bytes 3718660
  7.2 35.6 %copy-start.40 = (bf16[576,288]{0,1:T(8,128)(2,1)S(1)}, bf16[576,288]{0,1:T(8,128)(2,1)}, u32[]{:S(2)}) copy-start(bf16[576,288]{0,1:T(8,128)(2,1)} %param.31) | copy-start | bytes 995332
  7.2 35.5 %copy-start.42 = (bf16[576,288]{0,1:T(8,128)(2,1)S(1)}, bf16[576,288]{0,1:T(8,128)(2,1)}, u32[]{:S(2)}) copy-start(bf16[576,288]{0,1:T(8,128)(2,1)} %param.30) | copy-start | bytes 995332
  7.2 35.5 %copy-start.44 = (bf16[576,288]{0,1:T(8,128)(2,1)S(1)}, bf16[576,288]{0,1:T(8,128)(2,1)}, u32[]{:S(2)}) copy-start(bf16[576,288]{0,1:T(8,128)(2,1)} %param.28) | copy-start | bytes 995332
  7.2 35.5 %all-gather.11.cloned.1.call-start = ((), (), s32[]{:S(2)}) async-start(), calls=%async_computation.6 | async-start | bytes 2949120 | tf_op jit(solution)/shard_map/all_gather | solution.py:41
  14.6 34.7 %copy-start.26 = (f32[512]{0:T(512)}, f32[512]{0:T(512)S(1)}, u32[]{:S(2)}) copy-start(f32[512]{0:T(512)S(1)} %get-tuple-element.429) | copy-start | bytes 6148
  14.6 34.7 %copy-start.28 = (f32[512]{0:T(512)}, f32[512]{0:T(512)S(1)}, u32[]{:S(2)}) copy-start(f32[512]{0:T(512)S(1)} %get-tuple-element.430) | copy-start | bytes 6148
  16.8 118.4 %reduce-scatter.11.cloned.1.call-start = ((), (), s32[]{:S(2)}) async-start(), calls=%async_computation.7 | async-start | bytes 10616832 | tf_op jit(solution)/shard_map/reduce_scatter | solution.py:215
  49.4 159.5 %all-gather.13.cloned.1.call-start = ((), (), s32[]{:S(2)}) async-start(), calls=%async_computation.8 | async-start | bytes 1769472 | tf_op jit(solution)/shard_map/all_gather | solution.py:45
  136.9 2.5 copy-start.20
  136.9 2.4 copy-start.21
  144.2 2.6 copy-start.14
  155.2 2.6 copy-start.14
  166.1 2.6 copy-start.14
  177.1 2.6 copy-start.14
  183.2 30.5 %copy-start.6 = (bf16[2048,2,72]{0,2,1:T(8,128)(2,1)}, bf16[2048,2,72]{0,2,1:T(8,128)(2,1)S(1)}, u32[]{:S(2)}) copy-start(bf16[2048,2,72]{0,2,1:T(8,128)(2,1)S(1)} %get-tuple-element.713) | copy-start | bytes 1769476
  183.2 25.6 %copy-start.17 = (bf16[288,576]{1,0:T(8,128)(2,1)S(1)}, bf16[288,576]{1,0:T(8,128)(2,1)}, u32[]{:S(2)}) copy-start(bf16[288,576]{1,0:T(8,128)(2,1)} %param.33) | copy-start | bytes 995332
  186.0 75.8 %reduce-scatter.13.cloned.1.call-start = ((), (), s32[]{:S(2)}) async-start(), calls=%async_computation.9 | async-start | bytes 5898240 | tf_op jit(solution)/shard_map/reduce_scatter | solution.py:49
  213.7 48.0 %copy-start.3 = (bf16[512,576]{0,1:T(8,128)(2,1)S(1)}, bf16[512,576]{0,1:T(8,128)(2,1)}, u32[]{:S(2)}) copy-start(bf16[512,576]{0,1:T(8,128)(2,1)} %param.23) | copy-start | bytes 1769476
  213.7 48.0 %copy-start.32 = (f32[576]{0:T(1024)S(1)}, f32[576]{0:T(1024)}, u32[]{:S(2)}) copy-start(f32[576]{0:T(1024)} %param.34) | copy-start | bytes 6916
  213.7 55.5 %copy-start.24 = (f32[576]{0:T(1024)S(1)}, f32[576]{0:T(1024)}, u32[]{:S(2)}) copy-start(f32[576]{0:T(1024)} %param.35) | copy-start | bytes 6916
  213.8 55.5 %copy-start.33 = (f32[576]{0:T(1024)S(1)}, f32[576]{0:T(1024)}, u32[]{:S(2)}) copy-start(f32[576]{0:T(1024)} %param.36) | copy-start | bytes 6916
  213.8 73.5 %all-gather.17.cloned.1.call-start = ((), (), s32[]{:S(2)}) async-start(), calls=%async_computation.12 | async-start | bytes 2949120 | tf_op jit(solution)/shard_map/all_gather | solution.py:58
  214.4 99.0 %all-gather.15.cloned.1.call-start = ((), (), s32[]{:S(2)}) async-start(), calls=%async_computation.10 | async-start | bytes 2949120 | tf_op jit(solution)/shard_map/all_gather | solution.py:41
  271.7 357.3 %all-gather.25.cloned.1.call-start = ((), (), s32[]{:S(2)}) async-start(), calls=%async_computation.19 | async-start | bytes 6684672 | tf_op jit(solution)/shard_map/all_gather | solution.py:261
  322.1 211.7 %copy-start.37 = (u32[32]{0:T(128)S(1)}, u32[32]{0:T(128)}, u32[]{:S(2)}) copy-start(u32[32]{0:T(128)} %constant.181) | copy-start | bytes 388
  528.2 6.8 collective-permute-start.1
  532.5 15.8 %collective-permute-start = (f32[2048,6]{0,1:T(8,128)S(1)}, f32[2048,6]{0,1:T(8,128)S(1)}, u32[]{:S(2)}, u32[]{:S(2)}) collective-permute-start(f32[2048,6]{0,1:T(8,128)S(1)} %slice.36), channel_id=1, source_target_pairs={{0,1},{2,3},{4,5},{6,7},{8,9},{10,11},{12,13},{14,15},{16,17},{18,... | collective-permute-start | bytes 147464
  548.3 13.2 %copy-start.30 = (f32[538]{0:T(1024)S(1)}, f32[538]{0:T(1024)}, u32[]{:S(2)}) copy-start(f32[538]{0:T(1024)} %param.38) | copy-start | bytes 6460
  569.6 121.3 %all-gather.23.cloned.1.call-start = ((), (), s32[]{:S(2)}) async-start(), calls=%async_computation.18 | async-start | bytes 6684672 | tf_op jit(solution)/shard_map/all_gather | solution.py:45
  575.2 166.0 %reduce-scatter.17.cloned.1.call-start = ((), (), s32[]{:S(2)}) async-start(), calls=%async_computation.13 | async-start | bytes 5898240 | tf_op jit(solution)/shard_map/reduce_scatter | solution.py:66
  641.2 54.8 %copy-start.39 = (bf16[1076,576]{0,1:T(8,128)(2,1)S(1)}, bf16[1076,576]{0,1:T(8,128)(2,1)}, u32[]{:S(2)}) copy-start(bf16[1076,576]{0,1:T(8,128)(2,1)} %param.39) | copy-start | bytes 3718660
  641.2 150.4 %reduce-scatter.15.cloned.1.call-start = ((), (), s32[]{:S(2)}) async-start(), calls=%async_computation.11 | async-start | bytes 5898240 | tf_op jit(solution)/shard_map/reduce_scatter | solution.py:49
  703.2 38.1 %copy-start.2 = (f32[512,576]{0,1:T(8,128)S(1)}, f32[512,576]{0,1:T(8,128)}, u32[]{:S(2)}) copy-start(f32[512,576]{0,1:T(8,128)} %get-tuple-element.415) | copy-start | bytes 3538948
  703.2 88.4 %copy-start.13 = (bf16[512,576]{0,1:T(8,128)(2,1)S(1)}, bf16[512,576]{0,1:T(8,128)(2,1)}, u32[]{:S(2)}) copy-start(bf16[512,576]{0,1:T(8,128)(2,1)} %param.41) | copy-start | bytes 1769476
  703.2 88.4 %copy-start.34 = (f32[576]{0:T(1024)S(1)}, f32[576]{0:T(1024)}, u32[]{:S(2)}) copy-start(f32[576]{0:T(1024)} %param.40) | copy-start | bytes 6916
  703.2 117.6 %all-gather.19.cloned.1.call-start = ((), (), s32[]{:S(2)}) async-start(), calls=%async_computation.14 | async-start | bytes 2949120 | tf_op jit(solution)/shard_map/all_gather | solution.py:58
  796.6 63.3 %reduce-scatter.19.cloned.1.call-start = ((), (), s32[]{:S(2)}) async-start(), calls=%async_computation.15 | async-start | bytes 3538944 | tf_op jit(solution)/shard_map/reduce_scatter | solution.py:62
  825.0 37.9 %copy-start.7 = (bf16[2048,2,72]{0,2,1:T(8,128)(2,1)S(1)}, bf16[2048,2,72]{0,2,1:T(8,128)(2,1)}, u32[]{:S(2)}) copy-start(bf16[2048,2,72]{0,2,1:T(8,128)(2,1)} %copy-done.6) | copy-start | bytes 1769476
  825.0 167.1 %all-gather.21.cloned.1.call-start = ((), (), s32[]{:S(2)}) async-start(), calls=%async_computation.16 | async-start | bytes 5308416 | tf_op jit(solution)/shard_map/all_gather | solution.py:295
  867.6 1.3 copy-start.11
  875.5 2.6 copy-start.8
  885.2 1.3 copy-start.11
  894.5 2.6 copy-start.8
  904.2 1.3 copy-start.11
  913.5 2.6 copy-start.8
  923.1 1.3 copy-start.11
  932.4 2.6 copy-start.8
  942.6 211.3 %all-reduce.14.cloned.1.call-start = ((), (), s32[]{:S(2)}) async-start(), calls=%async_computation.20 | async-start | bytes 8257536 | tf_op jit(solution)/shard_map/psum | solution.py:314
  942.6 7.4 copy-start.38
  950.1 7.3 copy-start.12
  950.1 7.3 copy-start.16
  998.8 1.2 copy-start.45
  998.8 204.1 %reduce-scatter.21.cloned.1.call-start = ((), (), s32[]{:S(2)}) async-start(), calls=%async_computation.17 | async-start | bytes 5898240 | tf_op jit(solution)/shard_map/reduce_scatter | solution.py:66
  1006.8 1.4 copy-start.31
  1153.8 4.0 copy-start.23
  1153.8 4.9 copy-start.22
  1153.8 5.8 copy-start.19
  1158.7 2.6 copy-start.18
  1161.3 41.6 %copy-start.4 = (bf16[512,576]{0,1:T(8,128)(2,1)S(1)}, bf16[512,576]{0,1:T(8,128)(2,1)}, u32[]{:S(2)}) copy-start(bf16[512,576]{0,1:T(8,128)(2,1)} %param.23) | copy-start | bytes 1769476
  1161.3 41.6 %copy-start.25 = (f32[576]{0:T(1024)S(1)}, f32[576]{0:T(1024)}, u32[]{:S(2)}) copy-start(f32[576]{0:T(1024)} %param.26) | copy-start | bytes 6916
  1161.3 41.6 %copy-start.27 = (f32[512]{0:T(512)S(1)}, f32[512]{0:T(512)}, u32[]{:S(2)}) copy-start(f32[512]{0:T(512)} %copy-done.26) | copy-start | bytes 6148
  1161.3 41.6 %copy-start.29 = (f32[512]{0:T(512)S(1)}, f32[512]{0:T(512)}, u32[]{:S(2)}) copy-start(f32[512]{0:T(512)} %copy-done.28) | copy-start | bytes 6148
  1161.3 110.3 %copy-start.1 = (bf16[576,1076]{1,0:T(8,128)(2,1)S(1)}, bf16[576,1076]{1,0:T(8,128)(2,1)}, u32[]{:S(2)}) copy-start(bf16[576,1076]{1,0:T(8,128)(2,1)} %param.37) | copy-start | bytes 3718660
  (14 other events, 12.8 us)
Sparse Core Ops, SparseCore 0:
  16.9 25.8 all-gather.10
  49.5 85.5 reduce-scatter.10
  186.1 22.7 all-gather.12
  213.9 47.8 reduce-scatter.12
  263.1 24.0 all-gather.16
  289.3 24.0 all-gather.14
  569.7 59.2 all-gather.24
  631.1 59.6 all-gather.22
  693.4 47.8 reduce-scatter.16
  743.8 47.8 reduce-scatter.14
  796.7 24.0 all-gather.18
  825.1 34.7 reduce-scatter.18
  942.7 49.3 all-gather.20
  998.9 154.8 all-reduce.13
  1156.2 46.6 reduce-scatter.20
where the time goes:
time: 1290 us; the launch traced here: 1280 us
  waiting for transfers between devices  662 us (51%)
  blocking collectives  297 us (23%)
  matrix products  141 us (11%)
  other arithmetic  80.2 us (6%)
  local copies, waits for them, and re-layouts  62.5 us (5%)
  between operations  15.4 us (1%)
  loops' own time  14 us (1%)
    unnamed x1, blocking collectives  205 us
    psum x1, waiting for transfers between devices, local(): lax.psum(grad_w_stack[:, 0].astype(jnp.bfloat16), 'dp').astype(jnp.float32)  132 us
    reduce_scatter x2, waiting for transfers between devices, rows_out(): lax.psum_scatter(term_fn(jnp.int32(0), row_count * lax.axis_size('tr')),...  91 us
    reduce_scatter x1, waiting for transfers between devices, local(): lax.psum_scatter(jnp.einsum('td,dcf->tcf', hidden1, stacked, preferred_el...  85 us
    reduce_scatter x2, waiting for transfers between devices, grad_rows_out(): lax.psum_scatter(term_fn(jnp.int32(0), row_count * lax.axis_size('tr')),...  77.8 us
    all_gather x2, waiting for transfers between devices, cols_in(): return lax.all_gather(values, 'tc', axis=1, tiled=True)  72.4 us
    psum x1, blocking collectives, local(): lax.psum((grad_ln1_gain, grad_ln1_bias, grad_b_out, grad_ln2_gain, grad_l...  59.1 us
    all_gather x1, waiting for transfers between devices, local(): grad_upper_all = lax.all_gather(grad_upper, 'tc', axis=1, tiled=True)  53.3 us
  transfers between devices with their start and end apart: 17, of which 15 were waited for; matrix products, arithmetic and copies ran while one was open for 7% of the time, Pallas kernels for 0%

commit v1 on v0

v1 whole, which is shorter than its diff:
```python
import functools

import jax
import jax.numpy as jnp
from jax import lax
from jax.experimental import pallas as pl
from jax.experimental.pallas import tpu as pltpu
from jax.sharding import PartitionSpec as P

DH = 72
SUB = 256
EPSILON = 1e-06
GELU_C = 0.7978845608028654
GELU_A = 0.044715
MASKED = -1e30
SCALE = DH**-0.5
SCALE2 = SCALE * 1.4426950408889634
BF = jnp.bfloat16
F32 = jnp.float32
VMEM_BYTES = 56 * 1024 * 1024


def swap_perm(axis, bit):
    return [(i, i ^ bit) for i in range(lax.axis_size(axis))]


def px(v):
    return lax.ppermute(v, "tr", swap_perm("tr", 2))


def pc(v):
    return lax.ppermute(v, "tr", swap_perm("tr", 1))


def py(v):
    return lax.ppermute(v, "tc", swap_perm("tc", 1))


def dot(a, b):
    return jnp.dot(a, b, preferred_element_type=F32)


def dot_tn(a, b):
    return lax.dot_general(a, b, (((0,), (0,)), ((), ())), preferred_element_type=F32)


def dot_nt(a, b):
    return lax.dot_general(a, b, (((1,), (1,)), ((), ())), preferred_element_type=F32)


def rows_at(v, first, count):
    return lax.dynamic_slice_in_dim(v, first, count, 0)


def cols_at(v, first, count):
    return lax.dynamic_slice_in_dim(v, first, count, 1)


def rel_rows(v, ypos):
    half = v.shape[0] // 2
    return jnp.concatenate((rows_at(v, ypos * half, half), rows_at(v, (1 - ypos) * half, half)), 0)


def whole_vmem(n):
    return [pl.BlockSpec(memory_space=pltpu.VMEM)] * n


SMEM_SPEC = pl.BlockSpec(memory_space=pltpu.SMEM)


def params(**kw):
    return pltpu.CompilerParams(vmem_limit_bytes=VMEM_BYTES, **kw)


def norm_qkv_kernel(scal, a00, b00, a01, b01, a10, b10, a11, b11, wa, wb, bias, gain, shift, h_ref, qkv_ref, res_ref):
    ypos = scal[0]
    width = a00.shape[1]
    weights = jnp.concatenate((wa[...], wb[...]), 0)
    sources = {(0, 0): (a00, b00), (1, 0): (a01, b01), (0, 1): (a10, b10), (1, 1): (a11, b11)}
    for rc in range(2):
        for ry in range(2):
            for rx in range(2):
                place = (rc * 4 + ry * 2 + rx) * SUB
                first = pl.multiple_of((ypos ^ ry) * SUB, SUB)
                sa, sb = sources[(rc, rx)]
                raw_a, raw_b = sa[pl.ds(first, SUB), :], sb[pl.ds(first, SUB), :]
                raw = jnp.concatenate((raw_a, raw_b), 1)
                if rc == 0 and ry == 0:
                    res_ref[rx * SUB : (rx + 1) * SUB, :] = raw
                v = raw.astype(F32)
                mean = jnp.sum(v, axis=1, keepdims=True) / (2 * width)
                square = jnp.sum(v * v, axis=1, keepdims=True) / (2 * width)
                root = lax.rsqrt(square - mean * mean + EPSILON)
                hidden = ((v - mean) * root * gain[...] + shift[...]).astype(BF)
                h_ref[place : place + SUB, :] = hidden
                qkv_ref[place : place + SUB, :] = (dot(hidden, weights) + bias[...]).astype(BF)


def spots():
    return [(rc, ry, rx) for rc in range(2) for ry in range(2) for rx in range(2)]


def block_of(me, rc, ry, rx):
    return me ^ (rx * 4 + rc * 2 + ry)


def span(block):
    return pl.ds(pl.multiple_of(block * SUB, SUB), SUB)


def attend_kernel(scal, klo, khi, qkv, lo, hi, o00, o01, o10, o11, lse, ks, qt, vt):
    me = scal[1]
    outs = {(0, 0): o00, (0, 1): o01, (1, 0): o10, (1, 1): o11}
    tail = lax.broadcasted_iota(jnp.int32, (8, vt.shape[2]), 0)
    for h in range(2):
        vt[h, DH:, :] = jnp.where(tail == 0, 1.0, 0.0).astype(BF)
    for p, (rc, ry, rx) in enumerate(spots()):
        rows = span(block_of(me, rc, ry, rx))
        here = slice(p * SUB, (p + 1) * SUB)
        for h in range(2):
            ks[h, rows, :] = qkv[here, 144 + DH * h : 144 + DH * (h + 1)]
        qtile = qkv[here, 0:144].T
        vtile = qkv[here, 288:432].T
        for h in range(2):
            qt[h, :, rows] = qtile[DH * h : DH * (h + 1)]
            vt[h, :DH, rows] = vtile[DH * h : DH * (h + 1)]
    places = lax.broadcasted_iota(jnp.int32, (SUB, SUB), 0)
    lanes = lax.broadcasted_iota(jnp.int32, (1, SUB), 1)
    for rc, ry, rx in spots():
        block = block_of(me, rc, ry, rx)
        cols = span(block)
        low, high = lo[:, cols], hi[:, cols]
        own = lanes + block * SUB

        def body(kb, carry):
            base = kb * SUB
            allowed = ((places >= low - base) & (places < high - base)) | (places == own - base)
            new = []
            for h in range(2):
                top, acc = carry[h]
                s = dot(ks[h, span(kb), :], qt[h, :, cols])
                s = jnp.where(allowed, s, MASKED)
                newtop = jnp.maximum(top, jnp.max(s, axis=0, keepdims=True))
                alpha = jnp.exp2((top - newtop) * SCALE2)
                weights = jnp.exp2((s - newtop) * SCALE2).astype(BF)
                acc = acc * alpha + dot(vt[h, :, span(kb)], weights)
                new.append((newtop, acc))
            return tuple(new)

        start = (jnp.full((1, SUB), MASKED, F32), jnp.zeros((DH + 8, SUB), F32))
        done = lax.fori_loop(klo[block], khi[block], body, (start, start))
        heads = []
        for h in range(2):
            top, acc = done[h]
            total = acc[DH : DH + 1, :]
            heads.append(acc[:DH, :] / total)
            lse[h : h + 1, cols] = top * SCALE2 + jnp.log2(total)
        outs[(rc, ry)][:, rx * SUB : (rx + 1) * SUB] = jnp.concatenate(heads, 0).astype(BF)


def attend_back_kernel(
    scal, qlo, qhi, qkv, lo, hi, lse, o00, o01, o10, o11, g00, g01, g10, g11, gs, out,
    ks, kt, vs, qt, gt, delta, dqt, dk, dv,
):
    me = scal[1]
    outs = {(0, 0): o00, (0, 1): o01, (1, 0): o10, (1, 1): o11}
    grads = {(0, 0): g00, (0, 1): g01, (1, 0): g10, (1, 1): g11}
    for p, (rc, ry, rx) in enumerate(spots()):
        rows = span(block_of(me, rc, ry, rx))
        here = slice(p * SUB, (p + 1) * SUB)
        for h in range(2):
            ks[h, rows, :] = qkv[here, 144 + DH * h : 144 + DH * (h + 1)]
            vs[h, rows, :] = qkv[here, 288 + DH * h : 288 + DH * (h + 1)]
        qtile = qkv[here, 0:144].T
        ktile = qkv[here, 144:288].T
        if rc == 0:
            gtile = grads[(rx, ry)][0:144, :]
        else:
            gtile = gs[:, (ry * 2 + rx) * SUB : (ry * 2 + rx + 1) * SUB]
        otile = outs[(rc, ry)][:, rx * SUB : (rx + 1) * SUB]
        both = gtile.astype(F32) * otile.astype(F32)
        for h in range(2):
            part = slice(DH * h, DH * (h + 1))
            qt[h, :, rows] = qtile[part]
            kt[h, :, rows] = ktile[part]
            gt[h, :, rows] = gtile[part]
            delta[h : h + 1, rows] = jnp.sum(both[part], axis=0, keepdims=True)
    dqt[...] = jnp.zeros_like(dqt)
    dk[...] = jnp.zeros_like(dk)
    dv[...] = jnp.zeros_like(dv)
    places = lax.broadcasted_iota(jnp.int32, (SUB, SUB), 0)
    lanes = lax.broadcasted_iota(jnp.int32, (1, SUB), 1)

    @pl.loop(0, 8)
    def _(kb):
        keys = span(kb)
        base = kb * SUB

        def body(qb, carry):
            cols = span(qb)
            low, high = lo[:, cols] - base, hi[:, cols] - base
            own = lanes + (qb * SUB - base)
            allowed = ((places >= low) & (places < high)) | (places == own)
            for h in range(2):
                s = dot(ks[h, keys, :], qt[h, :, cols])
                probs = jnp.where(allowed, jnp.exp2(s * SCALE2 - lse[h : h + 1, cols]), 0.0)
                gprobs = dot(vs[h, keys, :], gt[h, :, cols])
                gscores = (probs * (gprobs - delta[h : h + 1, cols])).astype(BF)
                dv[h, keys, :] += dot_nt(probs.astype(BF), gt[h, :, cols])
                dk[h, keys, :] += dot_nt(gscores, qt[h, :, cols])
                dqt[h, :, cols] += dot(kt[h, :, keys], gscores)
            return carry

        lax.fori_loop(qlo[kb], qhi[kb], body, 0)

    for p, (rc, ry, rx) in enumerate(spots()):
        rows = span(block_of(me, rc, ry, rx))
        parts = [dqt[h, :, rows].T * SCALE for h in range(2)]
        parts += [dk[h, rows, :] * SCALE for h in range(2)]
        parts += [dv[h, rows, :] for h in range(2)]
        out[p * SUB : (p + 1) * SUB, :] = jnp.concatenate(parts, 1).astype(BF)


def gelu_tangent(u):
    return jnp.tanh(GELU_C * (u + GELU_A * u * u * u))


def dp_sum(v):
    return lax.psum(v, "dp")


def local(
    layer_input, picture, token_kept, ln1_gain, ln1_bias, w_query, b_query, w_key, w_value, b_value,
    w_out, b_out, ln2_gain, ln2_bias, w_up, b_up, w_down, b_down, grad_out,
):
    ypos = lax.axis_index("tc").astype(jnp.int32)
    trpos = lax.axis_index("tr").astype(jnp.int32)
    me = trpos * 2 + ypos
    half = layer_input.shape[1]
    width = 2 * half
    seq = picture.shape[0]
    heads2 = b_query.shape[0]
    units = w_up.shape[1]

    numbers = jnp.arange(8, dtype=jnp.int32)[:, None]
    hot = (picture[None, :] == numbers).astype(jnp.int32)
    counts = jnp.sum(hot, axis=1)
    kept = jnp.sum(hot * token_kept[None, :], axis=1)
    starts = jnp.cumsum(counts) - counts
    lo = jnp.sum(hot * starts[:, None], axis=0)
    hi = jnp.sum(hot * (starts + kept)[:, None], axis=0)
    end = jnp.sum(hot * (starts + counts)[:, None], axis=0)
    blocks = seq // SUB
    firsts = lo.reshape(blocks, SUB)[:, 0]
    klo = qlo = firsts // SUB
    lasts = jnp.arange(1, blocks + 1, dtype=jnp.int32) * SUB
    khi = (jnp.maximum(lasts, hi.reshape(blocks, SUB)[:, -1]) + SUB - 1) // SUB
    qhi = (jnp.maximum(lasts, end.reshape(blocks, SUB)[:, -1]) + SUB - 1) // SUB
    lo, hi = lo[None, :], hi[None, :]
    scal = jnp.stack((ypos, me))

    small = jnp.stack((ln1_gain, ln1_bias, ln2_gain, ln2_bias, b_out, b_down))
    both = jnp.concatenate((small, py(small)), 1)
    gain1, shift1, gain2, shift2, bias_out, bias_down = [both[i : i + 1] for i in range(6)]
    up_y = py(b_up)
    up_own = jnp.where(ypos == 0, jnp.concatenate((b_up, up_y)), jnp.concatenate((up_y, b_up)))
    bias_up = jnp.concatenate((up_own, pc(up_own)))[None, :]

    a00 = layer_input
    a10 = px(a00)
    b00 = py(a00)
    b10 = px(b00)
    a01, b01, a11, b11 = pc(a00), pc(b00), pc(a10), pc(b10)

    def heads_of(w, pos):
        return cols_at(w, pos * heads2, heads2)

    wa = jnp.concatenate([heads_of(w, ypos) for w in (w_query, w_key, w_value)], 1)
    wb = py(jnp.concatenate([heads_of(w, 1 - ypos) for w in (w_query, w_key, w_value)], 1))
    qkv_bias = jnp.concatenate((b_query, jnp.zeros_like(b_query), b_value))[None, :]

    h1, qkv, resid = pl.pallas_call(
        norm_qkv_kernel,
        out_shape=(
            jax.ShapeDtypeStruct((seq, width), BF),
            jax.ShapeDtypeStruct((seq, 3 * heads2), BF),
            jax.ShapeDtypeStruct((2 * SUB, width), BF),
        ),
        in_specs=[SMEM_SPEC] + whole_vmem(13),
        out_specs=tuple(whole_vmem(3)),
        compiler_params=params(),
        name="norm_qkv",
    )(scal, a00, b00, a01, b01, a10, b10, a11, b11, wa, wb, qkv_bias, gain1, shift1)

    wo_a = rel_rows(w_out, ypos)
    wo_b = rel_rows(py(wo_a), 1)
    wo_x0 = jnp.concatenate((wo_a, wo_b), 1)
    wo_c = pc(wo_x0)
    n2 = heads2
    wo_half = jnp.concatenate((wo_x0[:n2], wo_c[:n2], wo_x0[n2:], wo_c[n2:]), 0)
    wo = jnp.concatenate((wo_half, px(wo_half)), 0)
    up_a, up_b = w_up, py(w_up)
    up_a2, up_b2 = pc(up_a), pc(up_b)
    wup = jnp.concatenate((jnp.concatenate((up_a, up_a2), 1), jnp.concatenate((up_b, up_b2), 1)), 0)
    down_a, down_b = w_down, py(w_down)
    down_a2, down_b2 = pc(down_a), pc(down_b)
    wdown = jnp.concatenate((jnp.concatenate((down_a, down_b), 1), jnp.concatenate((down_a2, down_b2), 1)), 0)
    go_own = rows_at(grad_out, ypos * SUB, SUB)
    go = jnp.concatenate((go_own, py(rows_at(grad_out, (1 - ypos) * SUB, SUB))), 1)
    go_all = jnp.concatenate((go, px(go)), 0)

    scratch_t = pltpu.VMEM((2, DH, seq), BF)
    scratch_k = pltpu.VMEM((2, seq, DH), BF)
    o_shape = jax.ShapeDtypeStruct((heads2, 2 * SUB), BF)
    o00, o01, o10, o11, lse = pl.pallas_call(
        attend_kernel,
        out_shape=(o_shape,) * 4 + (jax.ShapeDtypeStruct((2, seq), F32),),
        in_specs=[SMEM_SPEC] * 3 + whole_vmem(3),
        out_specs=tuple(whole_vmem(5)),
        scratch_shapes=[scratch_k, scratch_t, pltpu.VMEM((2, DH + 8, seq), BF)],
        compiler_params=params(),
        name="attend",
    )(scal, klo, khi, qkv, lo, hi)

    c0, c1 = pc(o10), pc(o11)
    y0, y1 = py(o01), py(c1)
    x0, x1, xy0, xy1 = px(o00), px(c0), px(y0), px(y1)

    def turned(v):
        return jnp.concatenate((v[:, SUB:], v[:, :SUB]), 1)

    att = jnp.concatenate((o00, c0, y0, y1) + tuple(turned(v) for v in (x0, x1, xy0, xy1)), 0)
    mixed = resid.astype(F32) + dot_tn(att, wo) + bias_out
    mean2 = jnp.mean(mixed, axis=1, keepdims=True)
    root2 = lax.rsqrt(jnp.mean(mixed * mixed, axis=1, keepdims=True) - mean2 * mean2 + EPSILON)
    normed2 = (mixed - mean2) * root2
    h2 = (normed2 * gain2 + shift2).astype(BF)

    upper = dot(h2, wup) + bias_up
    tangent = gelu_tangent(upper)
    activated = (0.5 * upper * (1.0 + tangent)).astype(BF)
    slope = 0.5 * (1.0 + tangent) + 0.5 * upper * (1.0 - tangent * tangent) * GELU_C * (
        1.0 + 3.0 * GELU_A * upper * upper
    )
    grad_upper = (dot_nt(go_all, wdown) * slope).astype(BF)
    part_h2 = dot_nt(grad_upper, wup)
    grad_h2 = part_h2[:SUB] + px(part_h2[SUB:].astype(BF)).astype(F32)
    part_res = dot(activated, wdown)
    result = mixed[:SUB] + part_res[:SUB] + px(part_res[SUB:].astype(BF)).astype(F32) + bias_down
    result = result.astype(BF)
    result_y = py(result[:, half:])
    result = jnp.where(
        ypos == 0,
        jnp.concatenate((result[:, :half], result_y), 0),
        jnp.concatenate((result_y, result[:, :half]), 0),
    )

    weighted = grad_h2 * gain2
    n_own = normed2[:SUB]
    grad_mixed = go.astype(F32) + root2[:SUB] * (
        weighted
        - jnp.mean(weighted, axis=1, keepdims=True)
        - n_own * jnp.mean(weighted * n_own, axis=1, keepdims=True)
    )
    sums2 = jnp.stack((jnp.sum(grad_h2 * n_own, 0), jnp.sum(grad_h2, 0), jnp.sum(grad_mixed, 0)))
    gm_low = grad_mixed.astype(BF)
    gm_x = px(gm_low)
    gm_y = py(gm_low[:, half:])

    gatt = dot_nt(wo, gm_low).astype(BF)
    gx = px(gatt[4 * n2 :])
    gy = py(gatt[2 * n2 : 4 * n2])
    gxy = py(gx[2 * n2 :])
    gs = pc(jnp.concatenate((gatt[n2 : 2 * n2], gx[n2 : 2 * n2], gy[n2:], gxy[n2:]), 1))

    dqkv = pl.pallas_call(
        attend_back_kernel,
        out_shape=jax.ShapeDtypeStruct((seq, 3 * heads2), BF),
        in_specs=[SMEM_SPEC] * 3 + whole_vmem(13),
        out_specs=pl.BlockSpec(memory_space=pltpu.VMEM),
        scratch_shapes=[
            scratch_k, scratch_t, scratch_k, scratch_t, scratch_t,
            pltpu.VMEM((2, seq), F32),
            pltpu.VMEM((2, DH, seq), F32),
            pltpu.VMEM((2, seq, DH), F32),
            pltpu.VMEM((2, seq, DH), F32),
        ],
        compiler_params=params(),
        name="attend_back",
    )(scal, qlo, qhi, qkv, lo, hi, lse, o00, o01, o10, o11, gatt, gy, gx, gxy, gs)

    dwd = dot_tn(activated, go_all)
    dwd = dwd[:units] + pc(dwd[units:].astype(BF)).astype(F32)
    dwd = dwd[:, :half] + py(dwd[:, half:].astype(BF)).astype(F32)
    dwu = dot_tn(h2, grad_upper)
    dwu = dwu[:, :units] + pc(dwu[:, units:].astype(BF)).astype(F32)
    dwu = dwu[:half] + py(dwu[half:].astype(BF)).astype(F32)
    gm_all = jnp.concatenate((gm_low, gm_x), 0)
    dwo = dot(att[: 4 * n2], gm_all)
    dwo_own = jnp.concatenate((dwo[:n2], dwo[2 * n2 : 3 * n2]), 0)
    dwo_sib = jnp.concatenate((dwo[n2 : 2 * n2], dwo[3 * n2 :]), 0)
    dwo = dwo_own + pc(dwo_sib.astype(BF)).astype(F32)
    dwo = dwo[:, :half] + rel_rows(py(dwo[:, half:].astype(BF)), 1).astype(F32)

    wqkv = jnp.concatenate((wa, wb), 0)
    dwqkv = dot_tn(h1, dqkv)
    dwq_y = py(dwqkv[half:].astype(BF))
    dwq_a = dwqkv[:half].astype(BF)

    dwd_t = dp_sum(dwd.astype(BF))
    dwu_t = dp_sum(dwu.astype(BF))
    dwo_t = dp_sum(dwo.astype(BF))
    dwq_t = dp_sum(jnp.concatenate((dwq_a, dwq_y), 1)).astype(F32)
    own_q, other_q = dwq_t[:, : 3 * n2], dwq_t[:, 3 * n2 :]
    first_q = jnp.where(ypos == 0, own_q, other_q)
    second_q = jnp.where(ypos == 0, other_q, own_q)
    gw = [
        jnp.concatenate((first_q[:, i * n2 : (i + 1) * n2], second_q[:, i * n2 : (i + 1) * n2]), 1)
        for i in range(3)
    ]

    q4 = 4 * SUB
    low_part = dot_nt(dqkv[q4:], wqkv).astype(BF)
    part = dot_nt(dqkv[:q4], wqkv) + pc(low_part).astype(F32)
    top, bottom = part[: 2 * SUB], part[2 * SUB :]
    top = top[:SUB] + px(top[SUB:].astype(BF)).astype(F32)
    top_send = top[:, half:].astype(BF)
    return_top = top[:, :half]
    bottom_y = py(bottom[:, half:].astype(BF)).astype(F32)
    bottom_a = bottom[:, :half]
    top_recv = py(top_send).astype(F32)
    extra = px(bottom_a[SUB:].astype(BF)).astype(F32)
    extra_y = px(bottom_y[SUB:].astype(BF)).astype(F32)
    grad_h1_0 = return_top + bottom_y[:SUB] + extra_y
    grad_h1_1 = bottom_a[:SUB] + extra + top_recv
    grad_h1 = jnp.concatenate((grad_h1_0, grad_h1_1), 0)

    own_rel = rel_rows(a00, ypos).astype(F32)
    oth_rel = rel_rows(b00, ypos).astype(F32)
    mean1 = (jnp.sum(own_rel, 1, keepdims=True) + jnp.sum(oth_rel, 1, keepdims=True)) / width
    sq1 = (jnp.sum(own_rel * own_rel, 1, keepdims=True) + jnp.sum(oth_rel * oth_rel, 1, keepdims=True)) / width
    root1 = lax.rsqrt(sq1 - mean1 * mean1 + EPSILON)
    n1 = (own_rel - mean1) * root1
    weighted1 = grad_h1 * ln1_gain[None, :]
    stats = jnp.stack((jnp.sum(weighted1, 1), jnp.sum(weighted1 * n1, 1)))
    stats = stats + rel_rows(py(stats).T, 1).T
    gm_blk = jnp.concatenate((grad_mixed[:, :half], gm_y.astype(F32)), 0)
    gin = gm_blk + root1 * (weighted1 - stats[0][:, None] / width - n1 * (stats[1][:, None] / width))
    gin = rel_rows(gin, ypos).astype(BF)

    sums2 = sums2[:, :half] + py(sums2[:, half:])
    sums1 = jnp.stack((jnp.sum(grad_h1 * n1, 0), jnp.sum(grad_h1, 0)))
    sum_down = jnp.sum(grad_out.astype(F32), 0)
    totals = lax.psum((sums1, sums2, sum_down), ("dp", "tr"))
    gbu = jnp.sum(grad_upper, 0, dtype=F32)
    gbu = gbu[:units] + pc(gbu[units:])
    sums_q = jnp.sum(dqkv, 0, dtype=F32)
    gbu = lax.psum(gbu, ("dp", "tc"))
    n_up = b_up.shape[0]
    gbu = lax.dynamic_slice_in_dim(gbu, ypos * n_up, n_up, 0)
    gbq, gbv = lax.psum((sums_q[:n2], sums_q[2 * n2 :]), "dp")
    return (
        result, gin, totals[0][0], totals[0][1], gw[0], gbq, gw[1], gw[2], gbv,
        rel_rows(dwo_t.astype(F32), ypos), totals[1][2], totals[1][0], totals[1][1],
        dwu_t.astype(F32), gbu, dwd_t.astype(F32), totals[2],
    )


def solution(mesh):
    rows = P(("dp", "tr"), "tc")
    placed = (
        rows, P("dp"), P("dp"), P("tc"), P("tc"), P("tc", "tr"), P(("tr", "tc")), P("tc", "tr"),
        P("tc", "tr"), P(("tr", "tc")), P("tr", "tc"), P("tc"), P("tc"), P("tc"), P("tc", "tr"),
        P(("tr", "tc")), P("tr", "tc"), P("tc"), rows,
    )
    outs = (
        rows, rows, P("tc"), P("tc"), P("tc", "tr"), P(("tr", "tc")), P("tc", "tr"), P("tc", "tr"),
        P(("tr", "tc")), P("tr", "tc"), P("tc"), P("tc"), P("tc"), P("tc", "tr"), P(("tr", "tc")),
        P("tr", "tc"), P("tc"),
    )
    return jax.shard_map(local, mesh=mesh, in_specs=placed, out_specs=outs, check_vma=False)
```

time: 1290 us -> 598 us (0.46)
  waiting for transfers between devices: 662 us -> 194 us
  blocking collectives: 297 us -> 92.8 us
  matrix products: 141 us -> 55.2 us
  Pallas kernels: 0 us -> 57.6 us
  starting transfers between devices: 6.05 us -> 39.1 us
  other arithmetic: 80.2 us -> 49 us
  local copies, waits for them, and re-layouts: 62.5 us -> 84.2 us
  loops' own time: 14 us -> 0 us
    reduce_scatter x6 -> x0, waiting for transfers between devices: 288 us -> none  [the longest x2 91 us: rows_out(): lax.psum_scatter(term_fn(jnp.int32(0), row_count * lax.axis_size('tr')),...]
    all_gather x8 -> x0, waiting for transfers between devices: 241 us -> none  [the longest x2 72.4 us: cols_in(): return lax.all_gather(values, 'tc', axis=1, tiled=True)]
    unnamed x1 -> x0, blocking collectives: 205 us -> none
    ppermute x0 -> x55, waiting for transfers between devices: none -> 143 us  [the longest x22 107 us: py(): return lax.ppermute(v, 'tc', swap_perm('tc', 1))]
    dot_general x40 -> x12, matrix products: 141 us -> 55.2 us  [the longest x5 26.6 us: dot_nt(): lax.dot_general(a, b, (((1,), (1,)), ((), ())), preferred_element_type=F32)]
    psum x1, waiting for transfers between devices: 132 us -> 50.1 us  [dp_sum(): return lax.psum(v, 'dp')]
    pallas_call x0 -> x3, Pallas kernels: none -> 57.6 us  [the longest x1 25.4 us: local(): pl.pallas_call(attend_back_kernel, out_shape=jax.ShapeDtypeStruct((seq, 3...]
    ppermute x0 -> x55, starting transfers between devices: none -> 39.1 us  [the longest x22 24.5 us: py(): return lax.ppermute(v, 'tc', swap_perm('tc', 1))]
  transfers between devices with their start and end apart: 17 -> 56, of which waited for: 15 -> 20; matrix products, arithmetic and copies ran while one was open for 7% -> 27% of each run, Pallas kernels for 0% -> 10%
where the time goes in v1:
time: 598 us; the launch traced here: 587 us
  waiting for transfers between devices  194 us (32%)
  blocking collectives  92.8 us (16%)
  local copies, waits for them, and re-layouts  84.2 us (14%)
  Pallas kernels  57.6 us (10%)
  matrix products  55.2 us (9%)
  other arithmetic  49 us (8%)
  starting transfers between devices  39.1 us (7%)
  between operations  15.9 us (3%)
    ppermute x22, waiting for transfers between devices, py(): return lax.ppermute(v, 'tc', swap_perm('tc', 1))  107 us
    psum x1, blocking collectives, local(): totals = lax.psum((sums1, sums2, sum_down), ('dp', 'tr'))  61.1 us
    psum x1, waiting for transfers between devices, dp_sum(): return lax.psum(v, 'dp')  50.1 us
    ppermute x15, waiting for transfers between devices, px(): return lax.ppermute(v, 'tr', swap_perm('tr', 2))  33.2 us
    unnamed x188, local copies, waits for them, and re-layouts  28.9 us
    dot_general x5, matrix products, dot_nt(): lax.dot_general(a, b, (((1,), (1,)), ((), ())), preferred_element_type=F32)  26.6 us
    pallas_call x1, Pallas kernels, local(): pl.pallas_call(attend_back_kernel, out_shape=jax.ShapeDtypeStruct((seq, 3...  25.4 us
    ppermute x22, starting transfers between devices, py(): return lax.ppermute(v, 'tc', swap_perm('tc', 1))  24.5 us
  transfers between devices with their start and end apart: 56, of which 20 were waited for; matrix products, arithmetic and copies ran while one was open for 27% of the time, Pallas kernels for 10%

profile of v1, /device:TPU:0, one launch (start us, length us, event | category | flops | bytes accessed | tf_op | source)
XLA Modules:
  0.0 587.3 jit_solution(10299695930361025075)
XLA Ops:
  7.3 3.0 collective-permute-start
  33.5 3.2 collective-permute-done.8
  40.4 7.8 %collective-permute-done.17 = bf16[288,576]{1,0:T(8,128)(2,1)S(1)} collective-permute-done((bf16[288,576]{1,0:T(8,128)(2,1)S(1)}, bf16[288,576]{1,0:T(8,128)(2,1)S(1)}, u32[]{:S(2)}, u32[]{:S(2)}) %collective-permute-start.17) | collective-permute-done | bytes 331808 | tf_op jit(solution)/shard_map/ppermute | solution.py:36
  49.5 8.7 %collective-permute-done.7 = bf16[576,432]{0,1:T(8,128)(2,1)} collective-permute-done((bf16[576,432]{0,1:T(8,128)(2,1)}, bf16[576,432]{0,1:T(8,128)(2,1)}, u32[]{:S(2)}, u32[]{:S(2)}) %collective-permute-start.7) | collective-permute-done | bytes 497696 | tf_op jit(solution)/shard_map/ppermute | solution.py:36
  58.7 2.1 copy.129.wb
  62.4 2.1 copy.122.b00
  64.6 2.1 copy.123.a01
  67.2 2.1 copy.125.a10
  69.4 2.0 fusion.69
  71.4 2.8 collective-permute-done.4
  75.2 2.1 copy.126.b10
  77.3 2.1 copy.124.b01
  79.5 2.2 copy.127.a11
  81.6 2.2 copy.128.b11
  83.8 10.1 %norm_qkv.1 = (bf16[2048,1152]{1,0:T(8,128)(2,1)}, bf16[2048,432]{1,0:T(8,128)(2,1)}, bf16[512,1152]{1,0:T(8,128)(2,1)}) custom-call(s32[2]{0:T(128)} %pad_add_fusion.scal, bf16[512,576]{1,0:T(8,128)(2,1)} %copy-done.6, bf16[512,576]{1,0:T(8,128)(2,1)} %copy.122.b00, bf16[512,576]{1,0:T(8,128)(2,1)} %copy.123.a01, bf16[512,576]{1,0:T(8,128)(2,1)} %copy.124.b01, ...), custom_call_target="tpu_custom_call" | custom-call | tf_op jit(solution)/shard_map/norm_qkv/pallas_call | solution.py:282
  93.9 22.1 %attend.1 = (bf16[144,512]{1,0:T(8,128)(2,1)}, bf16[144,512]{1,0:T(8,128)(2,1)}, bf16[144,512]{1,0:T(8,128)(2,1)}, bf16[144,512]{1,0:T(8,128)(2,1)}, f32[2,2048]{1,0:T(2,128)}) custom-call(s32[2]{0:T(128)} %pad_add_fusion.scal, s32[8]{0:T(128)} %and_select_fusion.2.klo.qlo, s32[8]{0:T(128)} %and_select_fusion.1.khi, ...), custom_call_target="tpu_custom_call" | custom-call | tf_op jit(solution)/shard_map/attend/pallas_call | solution.py:315
  118.9 3.6 collective-permute-done.13
  126.4 2.9 collective-permute-done.14
  130.8 28.2 %collective-permute-done.12 = bf16[144,512]{1,0:T(8,128)(2,1)S(1)} collective-permute-done((bf16[144,512]{1,0:T(8,128)(2,1)S(1)}, bf16[144,512]{1,0:T(8,128)(2,1)S(1)}, u32[]{:S(2)}, u32[]{:S(2)}) %collective-permute-start.12) | collective-permute-done | bytes 147488 | tf_op jit(solution)/shard_map/ppermute | solution.py:36
  159.5 4.7 collective-permute-done.15
  164.7 4.6 collective-permute-done.16
  170.7 1.9 fusion.82
  173.7 2.5 collective-permute-done.22
  176.2 4.2 convolution_add_fusion
  180.4 8.7 %fusion.31 = f32[512,1152]{1,0:T(8,128)S(1)} fusion(bf16[1076,576]{0,1:T(8,128)(2,1)S(1)} %collective-permute-done.27, bf16[1076,576]{0,1:T(8,128)(2,1)} %collective-permute-done.26, bf16[1076,576]{0,1:T(8,128)(2,1)} %collective-permute-done.25, bf16[1076,576]{0,1:T(8,128)(2,1)} %param.35, f32[512,2152]{0,1:T(8,128)S(1)} %convolution_add_fusion), kind=kOutput, calls=%fused_computation.87 | convolution fusion | flops 2568351744 | bytes 11724800 | tf_op jit(solution)/shard_map/dot_general | solution.py:40
  191.9 8.7 %convert_reduce_fusion = (f32[2152]{0:T(1024)S(1)}, bf16[512,2152]{0,1:T(8,128)(2,1)S(1)}) fusion(f32[512,2152]{0,1:T(8,128)S(1)} %convolution_add_fusion, bf16[1076,576]{0,1:T(8,128)(2,1)S(1)} %collective-permute-done.27, bf16[1076,576]{0,1:T(8,128)(2,1)} %collective-permute-done.26, bf16[1076,576]{0,1:T(8,128)(2,1)} %collective-permute-done.25, ...), kind=kOutput, calls=%fused_computation.19 | convolution fusion | flops 2583930880 | bytes 12757408 | tf_op jit(solution)/shard_map/dot_general | solution.py:48
  202.0 3.2 fusion.44
  205.2 7.9 %fusion.32 = f32[512,1152]{1,0:T(8,128)S(1)} fusion(bf16[512,2152]{0,1:T(8,128)(2,1)} %copy-done.79, bf16[576,1076]{1,0:T(8,128)(2,1)S(1)} %copy-done.78, bf16[576,1076]{1,0:T(8,128)(2,1)S(1)} %copy-done.74, bf16[576,1076]{1,0:T(8,128)(2,1)S(1)} %copy-done.76, bf16[576,1076]{1,0:T(8,128)(2,1)S(1)} %copy-done.72), kind=kOutput, calls=%fused_computation.88 | convolution fusion | flops 2558435328 | bytes 9521152 | tf_op jit(solution)/shard_map/dot_general | solution.py:48
  215.6 1.9 slice.533
  218.2 3.9 fusion.29
  222.1 3.9 copy-done.8
  226.0 1.9 slice.532
  227.9 22.1 %psum.77 = f32[1076]{0:T(1024)S(1)} all-reduce(f32[1076]{0:T(1024)S(1)} %slice_add_fusion.11), channel_id=1, replica_groups=mesh['dp'=4,'tr'=4,'tc'=2] {'dp','tc'}, use_global_device_ids=true, to_apply=%region_31.32 | all-reduce | flops 1076 | bytes 8608 | tf_op jit(solution)/shard_map/psum | solution.py:458
  250.6 2.2 multiply_reduce_fusion.1
  252.9 1.9 fusion.57
  261.4 14.6 %collective-permute-done.35.g10 = bf16[576,256]{1,0:T(8,128)(2,1)S(1)} collective-permute-done((bf16[576,256]{1,0:T(8,128)(2,1)S(1)}, bf16[576,256]{1,0:T(8,128)(2,1)S(1)}, u32[]{:S(2)}, u32[]{:S(2)}) %collective-permute-start.35) | collective-permute-done | bytes 294944 | tf_op jit(solution)/shard_map/ppermute | solution.py:28
  277.1 2.0 collective-permute-start.29
  279.1 2.2 collective-permute-done.36.g11
  283.9 25.4 %attend_back.1 = bf16[2048,432]{1,0:T(8,128)(2,1)} custom-call(s32[2]{0:T(128)} %pad_add_fusion.scal, s32[8]{0:T(128)} %and_select_fusion.2.klo.qlo, s32[8]{0:T(128)} %and_select_fusion.qhi, bf16[2048,432]{1,0:T(8,128)(2,1)} %get-tuple-element.26.qkv, s32[1,2048]{1,0:T(1,128)} %bitcast.31, s32[1,2048]{1,0:T(1,128)} %bitcast.29, ...), custom_call_target="tpu_custom_call" | custom-call | tf_op jit(solution)/shard_map/attend_back/pallas_call | solution.py:376
  309.3 5.7 convolution_convert_fusion.1
  318.9 3.1 convolution_convert_fusion
  321.9 8.8 %collective-permute-done.45 = bf16[576,432]{0,1:T(8,128)(2,1)S(1)} collective-permute-done((bf16[576,432]{0,1:T(8,128)(2,1)S(1)}, bf16[576,432]{0,1:T(8,128)(2,1)S(1)}, u32[]{:S(2)}, u32[]{:S(2)}) %collective-permute-start.45) | collective-permute-done | bytes 497696 | tf_op jit(solution)/shard_map/ppermute | solution.py:36
  333.0 5.6 collective-permute-done.48
  339.4 2.3 slice_add_fusion.1
  341.7 2.2 copy-done
  344.4 2.1 copy.138
  347.7 3.6 slice_add_fusion
  351.3 2.3 copy-done.1
  354.0 2.2 copy.140
  357.1 2.0 fusion.30
  360.3 6.0 %fusion.80 = (bf16[1024,1152]{1,0:T(8,128)(2,1)S(1)}, f32[1024,1152]{1,0:T(8,128)}) fusion(bf16[1024,1152]{1,0:T(8,128)(2,1)} %collective-permute-done.38, bf16[576,432]{1,0:T(8,128)(2,1)} %copy.129.wb, bf16[576,144]{1,0:T(8,128)(2,1)} %copy-done.20, bf16[576,144]{1,0:T(8,128)(2,1)} %copy-done.22, bf16[576,144]{1,0:T(8,128)(2,1)} %copy-done.24, ...), kind=kOutput, calls=%fused_computation.229 | convolution fusion | flops 1026736128 | bytes 11481088 | tf_op jit(solution)/shard_map/dot_general | solution.py:48
  368.5 10.3 %collective-permute-done.51 = bf16[576,1076]{1,0:T(8,128)(2,1)} collective-permute-done((bf16[576,1076]{1,0:T(8,128)(2,1)}, bf16[576,1076]{1,0:T(8,128)(2,1)}, u32[]{:S(2)}, u32[]{:S(2)}) %collective-permute-start.51) | collective-permute-done | bytes 1239584 | tf_op jit(solution)/shard_map/ppermute | solution.py:36
  379.4 2.6 copy.139
  382.0 3.1 fusion.8
  385.2 21.8 %collective-permute-done.54 = bf16[1076,576]{0,1:T(8,128)(2,1)} collective-permute-done((bf16[1076,576]{0,1:T(8,128)(2,1)}, bf16[1076,576]{0,1:T(8,128)(2,1)}, u32[]{:S(2)}, u32[]{:S(2)}) %collective-permute-start.54) | collective-permute-done | bytes 1239584 | tf_op jit(solution)/shard_map/ppermute | solution.py:36
  407.0 2.4 copy.141
  409.4 3.1 fusion.7
  415.8 1.9 convert_element_type.135
  426.1 10.5 %collective-permute-done.40 = bf16[512,576]{0,1:T(8,128)(2,1)S(1)} collective-permute-done((bf16[512,576]{0,1:T(8,128)(2,1)}, bf16[512,576]{0,1:T(8,128)(2,1)S(1)}, u32[]{:S(2)}, u32[]{:S(2)}) %collective-permute-start.40) | collective-permute-done | bytes 589856 | tf_op jit(solution)/shard_map/ppermute | solution.py:36
  438.3 9.6 %all-reduce.1 = (f32[144]{0:T(256)}, f32[144]{0:T(256)}) all-reduce(f32[144]{0:T(256)S(1)} %get-tuple-element.230, f32[144]{0:T(256)S(1)} %get-tuple-element.229), channel_id=1, replica_groups=mesh['dp'=4,'tr'=4,'tc'=2] {'dp'}, use_global_device_ids=true, to_apply=%region_22.23 | all-reduce | flops 288 | bytes 2304 | tf_op jit(solution)/shard_map/psum | solution.py:461
  452.7 61.1 %all-reduce = (f32[2,576]{1,0:T(2,128)S(1)}, f32[3,576]{1,0:T(4,128)S(1)}, f32[576]{0:T(1024)}) all-reduce(f32[2,576]{1,0:T(2,128)S(1)} %pad_maximum_fusion.26, f32[3,576]{1,0:T(4,128)S(1)} %slice_add_fusion.10, f32[576]{0:T(1024)S(1)} %copy-done.62), channel_id=1, replica_groups=mesh['dp'=4,'tr'=4,'tc'=2] {'dp','tr'}, use_global_device_ids=true, to_apply=%region_19.20 | all-reduce | flops 3456 | bytes 27648 | tf_op jit(solution)/shard_map/psum | solution.py:454
  518.0 50.1 %all-reduce.5.cloned.1.call-done = (bf16[576,1076]{0,1:T(8,128)(2,1)}, bf16[1076,576]{1,0:T(8,128)(2,1)}, bf16[576,864]{0,1:T(8,128)(2,1)}, bf16[288,576]{1,0:T(8,128)(2,1)}) async-done(((bf16[576,1076]{0,1:T(8,128)(2,1)}, bf16[1076,576]{1,0:T(8,128)(2,1)}, bf16[576,864]{0,1:T(8,128)(2,1)}, bf16[288,576]{1,0:T(8,128)(2,1)}), (bf16[576,1076]{0,1:T(8,128)(2,1)}, bf16[1076,576]{1,0:T(8,128)(2,1)}, ...) | async-done | bytes 3806224 | tf_op jit(solution)/shard_map/psum | solution.py:229
  570.7 2.9 copy.144
  573.7 2.9 copy.145
  (409 shorter events, 103.3 us)
Async XLA Ops:
  7.2 560.8 %all-reduce.5.cloned.1.call-start = ((), (), s32[]{:S(2)}) async-start(), calls=%async_computation | async-start | bytes 8478720 | tf_op jit(solution)/shard_map/psum | solution.py:229
  7.3 53.5 %collective-permute-start = (bf16[512,576]{0,1:T(8,128)(2,1)}, bf16[512,576]{0,1:T(8,128)(2,1)}, u32[]{:S(2)}, u32[]{:S(2)}) collective-permute-start(bf16[512,576]{0,1:T(8,128)(2,1)} %param.19), channel_id=1, source_target_pairs={{0,1},{1,0},{2,3},{3,2},{4,5},{5,4},{6,7},{7,6},{8,9},{9,8},{10,11... | collective-permute-start | bytes 1769480 | tf_op jit(solution)/shard_map/ppermute | solution.py:36
  10.3 54.2 %collective-permute-start.1 = (bf16[512,576]{0,1:T(8,128)(2,1)}, bf16[512,576]{0,1:T(8,128)(2,1)}, u32[]{:S(2)}, u32[]{:S(2)}) collective-permute-start(bf16[512,576]{0,1:T(8,128)(2,1)} %param.19), channel_id=1, source_target_pairs={{0,2},{2,0},{4,6},{6,4},{1,3},{3,1},{5,7},{7,5},{8,10},{10,8},{12,... | collective-permute-start | bytes 1769480 | tf_op jit(solution)/shard_map/ppermute | solution.py:32
  10.3 56.4 %collective-permute-start.3 = (bf16[512,576]{0,1:T(8,128)(2,1)}, bf16[512,576]{0,1:T(8,128)(2,1)}, u32[]{:S(2)}, u32[]{:S(2)}) collective-permute-start(bf16[512,576]{0,1:T(8,128)(2,1)} %param.19), channel_id=1, source_target_pairs={{0,4},{2,6},{4,0},{6,2},{1,5},{3,7},{5,1},{7,3},{8,12},{10,14},{12... | collective-permute-start | bytes 1769480 | tf_op jit(solution)/shard_map/ppermute | solution.py:28
  11.8 19.1 %collective-permute-start.23 = (f32[538]{0:T(1024)}, f32[538]{0:T(1024)}, u32[]{:S(2)}, u32[]{:S(2)}) collective-permute-start(f32[538]{0:T(1024)} %param.34), channel_id=1, source_target_pairs={{0,1},{1,0},{2,3},{3,2},{4,5},{5,4},{6,7},{7,6},{8,9},{9,8},{10,11... | collective-permute-start | bytes 6464 | tf_op jit(solution)/shard_map/ppermute | solution.py:36
  14.3 23.6 %collective-permute-start.30 = (bf16[256,576]{1,0:T(8,128)(2,1)}, bf16[256,576]{1,0:T(8,128)(2,1)S(1)}, u32[]{:S(2)}, u32[]{:S(2)}) collective-permute-start(bf16[256,576]{1,0:T(8,128)(2,1)} %copy.150), channel_id=1, source_target_pairs={{0,1},{1,0},{2,3},{3,2},{4,5},{5,4},{6,7},{7,6},{8,9},{9,8},{10,11... | collective-permute-start | bytes 884744 | tf_op jit(solution)/shard_map/ppermute | solution.py:36
  31.8 1.2 collective-permute-start.24
  32.9 3.8 collective-permute-start.8
  36.7 11.5 %collective-permute-start.17 = (bf16[288,576]{1,0:T(8,128)(2,1)S(1)}, bf16[288,576]{1,0:T(8,128)(2,1)S(1)}, u32[]{:S(2)}, u32[]{:S(2)}) collective-permute-start(bf16[288,576]{1,0:T(8,128)(2,1)S(1)} %copy-done.44), channel_id=1, source_target_pairs={{0,1},{1,0},{2,3},{3,2},{4,5},{5,4},{6,7},{7,6},{8,9},{9,8},{10,11... | collective-permute-start | bytes 995336 | tf_op jit(solution)/shard_map/ppermute | solution.py:36
  37.9 20.3 %collective-permute-start.7 = (bf16[576,432]{0,1:T(8,128)(2,1)}, bf16[576,432]{0,1:T(8,128)(2,1)}, u32[]{:S(2)}, u32[]{:S(2)}) collective-permute-start(bf16[576,432]{0,1:T(8,128)(2,1)} %pad_maximum_fusion.19), channel_id=1, source_target_pairs={{0,1},{1,0},{2,3},{3,2},{4,5},{5,4},{6,7},{7,6},{8,9},{9,8},{10,11... | collective-permute-start | bytes 1493000 | tf_op jit(solution)/shard_map/ppermute | solution.py:36
  48.5 20.9 %collective-permute-start.18 = (bf16[288,1152]{1,0:T(8,128)(2,1)S(1)}, bf16[288,1152]{1,0:T(8,128)(2,1)}, u32[]{:S(2)}, u32[]{:S(2)}) collective-permute-start(bf16[288,1152]{1,0:T(8,128)(2,1)S(1)} %maximum_maximum_fusion.3), channel_id=1, source_target_pairs={{0,2},{2,0},{4,6},{6,4},{1,3},{3,1},{5,7},{7,5},{8,10},{10,8},{12,... | collective-permute-start | bytes 1990664 | tf_op jit(solution)/shard_map/ppermute | solution.py:32
  58.2 111.2 %collective-permute-start.25 = (bf16[1076,576]{0,1:T(8,128)(2,1)}, bf16[1076,576]{0,1:T(8,128)(2,1)}, u32[]{:S(2)}, u32[]{:S(2)}) collective-permute-start(bf16[1076,576]{0,1:T(8,128)(2,1)} %param.35), channel_id=1, source_target_pairs={{0,1},{1,0},{2,3},{3,2},{4,5},{5,4},{6,7},{7,6},{8,9},{9,8},{10,11... | collective-permute-start | bytes 3718664 | tf_op jit(solution)/shard_map/ppermute | solution.py:36
  60.8 13.4 %collective-permute-start.4 = (bf16[512,576]{0,1:T(8,128)(2,1)}, bf16[512,576]{0,1:T(8,128)(2,1)}, u32[]{:S(2)}, u32[]{:S(2)}) collective-permute-start(bf16[512,576]{0,1:T(8,128)(2,1)} %collective-permute-done), channel_id=1, source_target_pairs={{0,4},{2,6},{4,0},{6,2},{1,5},{3,7},{5,1},{7,3},{8,12},{10,14},{12... | collective-permute-start | bytes 1769480 | tf_op jit(solution)/shard_map/ppermute | solution.py:28
  64.6 115.8 %collective-permute-start.26 = (bf16[1076,576]{0,1:T(8,128)(2,1)}, bf16[1076,576]{0,1:T(8,128)(2,1)}, u32[]{:S(2)}, u32[]{:S(2)}) collective-permute-start(bf16[1076,576]{0,1:T(8,128)(2,1)} %param.35), channel_id=1, source_target_pairs={{0,2},{2,0},{4,6},{6,4},{1,3},{3,1},{5,7},{7,5},{8,10},{10,8},{12,... | collective-permute-start | bytes 3718664 | tf_op jit(solution)/shard_map/ppermute | solution.py:32
  66.7 10.6 %collective-permute-start.2 = (bf16[512,576]{0,1:T(8,128)(2,1)}, bf16[512,576]{0,1:T(8,128)(2,1)}, u32[]{:S(2)}, u32[]{:S(2)}) collective-permute-start(bf16[512,576]{0,1:T(8,128)(2,1)} %collective-permute-done), channel_id=1, source_target_pairs={{0,2},{2,0},{4,6},{6,4},{1,3},{3,1},{5,7},{7,5},{8,10},{10,8},{12,... | collective-permute-start | bytes 1769480 | tf_op jit(solution)/shard_map/ppermute | solution.py:32
  69.4 10.1 %collective-permute-start.5 = (bf16[512,576]{0,1:T(8,128)(2,1)}, bf16[512,576]{0,1:T(8,128)(2,1)}, u32[]{:S(2)}, u32[]{:S(2)}) collective-permute-start(bf16[512,576]{0,1:T(8,128)(2,1)} %collective-permute-done.3), channel_id=1, source_target_pairs={{0,2},{2,0},{4,6},{6,4},{1,3},{3,1},{5,7},{7,5},{8,10},{10,8},{12,... | collective-permute-start | bytes 1769480 | tf_op jit(solution)/shard_map/ppermute | solution.py:32
  74.1 7.5 %collective-permute-start.6 = (bf16[512,576]{0,1:T(8,128)(2,1)}, bf16[512,576]{0,1:T(8,128)(2,1)}, u32[]{:S(2)}, u32[]{:S(2)}) collective-permute-start(bf16[512,576]{0,1:T(8,128)(2,1)} %collective-permute-done.4), channel_id=1, source_target_pairs={{0,2},{2,0},{4,6},{6,4},{1,3},{3,1},{5,7},{7,5},{8,10},{10,8},{12,... | collective-permute-start | bytes 1769480 | tf_op jit(solution)/shard_map/ppermute | solution.py:32
  93.9 22.6 %copy-start.31 = (bf16[144,1152]{1,0:T(8,128)(2,1)S(1)}, bf16[144,1152]{1,0:T(8,128)(2,1)}, u32[]{:S(2)}) copy-start(bf16[144,1152]{1,0:T(8,128)(2,1)} %get-tuple-element.183) | copy-start | bytes 995332
  116.0 6.5 %collective-permute-start.13 = (bf16[144,512]{1,0:T(8,128)(2,1)}, bf16[144,512]{1,0:T(8,128)(2,1)S(1)}, u32[]{:S(2)}, u32[]{:S(2)}) collective-permute-start(bf16[144,512]{1,0:T(8,128)(2,1)} %get-tuple-element.27.o00), channel_id=1, source_target_pairs={{0,4},{2,6},{4,0},{6,2},{1,5},{3,7},{5,1},{7,3},{8,12},{10,14},{12... | collective-permute-start | bytes 442376 | tf_op jit(solution)/shard_map/ppermute | solution.py:28
  116.6 52.7 %copy-start.41 = (bf16[256,1152]{1,0:T(8,128)(2,1)S(1)}, bf16[256,1152]{1,0:T(8,128)(2,1)}, u32[]{:S(2)}) copy-start(bf16[256,1152]{1,0:T(8,128)(2,1)} %pad_maximum_fusion.17) | copy-start | bytes 1769476
  116.9 5.7 collective-permute-start.9
  117.4 5.8 collective-permute-start.10
  122.5 2.2 collective-permute-start.11
  122.6 48.0 %copy-start.51 = (bf16[144,512]{1,0:T(8,128)(2,1)}, bf16[144,512]{1,0:T(8,128)(2,1)S(1)}, u32[]{:S(2)}) copy-start(bf16[144,512]{1,0:T(8,128)(2,1)S(1)} %collective-permute-done.9) | copy-start | bytes 442372
  122.6 6.7 %collective-permute-start.14 = (bf16[144,512]{1,0:T(8,128)(2,1)S(1)}, bf16[144,512]{1,0:T(8,128)(2,1)S(1)}, u32[]{:S(2)}, u32[]{:S(2)}) collective-permute-start(bf16[144,512]{1,0:T(8,128)(2,1)S(1)} %collective-permute-done.9), channel_id=1, source_target_pairs={{0,4},{2,6},{4,0},{6,2},{1,5},{3,7},{5,1},{7,3},{8,12},{10,14},{12... | collective-permute-start | bytes 442376 | tf_op jit(solution)/shard_map/ppermute | solution.py:28
  123.2 47.4 %copy-start.53 = (bf16[144,512]{1,0:T(8,128)(2,1)}, bf16[144,512]{1,0:T(8,128)(2,1)S(1)}, u32[]{:S(2)}) copy-start(bf16[144,512]{1,0:T(8,128)(2,1)S(1)} %collective-permute-done.10) | copy-start | bytes 442372
  123.2 46.9 %collective-permute-start.19 = (bf16[576,1152]{1,0:T(8,128)(2,1)S(1)}, bf16[576,1152]{1,0:T(8,128)(2,1)S(1)}, u32[]{:S(2)}, u32[]{:S(2)}) collective-permute-start(bf16[576,1152]{1,0:T(8,128)(2,1)S(1)} %pad_maximum_fusion.2), channel_id=1, source_target_pairs={{0,4},{2,6},{4,0},{6,2},{1,5},{3,7},{5,1},{7,3},{8,12},{10,14},{12... | collective-permute-start | bytes 3981320 | tf_op jit(solution)/shard_map/ppermute | solution.py:28
  124.8 45.1 %collective-permute-start.21 = (bf16[576,1076]{1,0:T(8,128)(2,1)S(1)}, bf16[576,1076]{1,0:T(8,128)(2,1)S(1)}, u32[]{:S(2)}, u32[]{:S(2)}) collective-permute-start(bf16[576,1076]{1,0:T(8,128)(2,1)S(1)} %copy-done.72), channel_id=1, source_target_pairs={{0,1},{1,0},{2,3},{3,2},{4,5},{5,4},{6,7},{7,6},{8,9},{9,8},{10,11... | collective-permute-start | bytes 3718664 | tf_op jit(solution)/shard_map/ppermute | solution.py:36
  129.3 29.7 %collective-permute-start.12 = (bf16[144,512]{1,0:T(8,128)(2,1)S(1)}, bf16[144,512]{1,0:T(8,128)(2,1)S(1)}, u32[]{:S(2)}, u32[]{:S(2)}) collective-permute-start(bf16[144,512]{1,0:T(8,128)(2,1)S(1)} %collective-permute-done.11), channel_id=1, source_target_pairs={{0,1},{1,0},{2,3},{3,2},{4,5},{5,4},{6,7},{7,6},{8,9},{9,8},{10,11... | collective-permute-start | bytes 442376 | tf_op jit(solution)/shard_map/ppermute | solution.py:36
  159.0 5.1 collective-permute-start.15
  164.2 5.1 collective-permute-start.16
  169.3 4.3 collective-permute-start.20
  169.4 22.5 %collective-permute-start.31 = (bf16[256,1152]{1,0:T(8,128)(2,1)S(1)}, bf16[256,1152]{1,0:T(8,128)(2,1)S(1)}, u32[]{:S(2)}, u32[]{:S(2)}) collective-permute-start(bf16[256,1152]{1,0:T(8,128)(2,1)S(1)} %copy-done.41), channel_id=1, source_target_pairs={{0,4},{2,6},{4,0},{6,2},{1,5},{3,7},{5,1},{7,3},{8,12},{10,14},{12... | collective-permute-start | bytes 1769480 | tf_op jit(solution)/shard_map/ppermute | solution.py:28
  169.9 10.5 %collective-permute-start.27 = (bf16[1076,576]{0,1:T(8,128)(2,1)}, bf16[1076,576]{0,1:T(8,128)(2,1)S(1)}, u32[]{:S(2)}, u32[]{:S(2)}) collective-permute-start(bf16[1076,576]{0,1:T(8,128)(2,1)} %collective-permute-done.25), channel_id=1, source_target_pairs={{0,2},{2,0},{4,6},{6,4},{1,3},{3,1},{5,7},{7,5},{8,10},{10,8},{12,... | collective-permute-start | bytes 3718664 | tf_op jit(solution)/shard_map/ppermute | solution.py:32
  170.1 6.0 %collective-permute-start.22 = (bf16[576,1076]{1,0:T(8,128)(2,1)S(1)}, bf16[576,1076]{1,0:T(8,128)(2,1)S(1)}, u32[]{:S(2)}, u32[]{:S(2)}) collective-permute-start(bf16[576,1076]{1,0:T(8,128)(2,1)S(1)} %collective-permute-done.21), channel_id=1, source_target_pairs={{0,2},{2,0},{4,6},{6,4},{1,3},{3,1},{5,7},{7,5},{8,10},{10,8},{12,... | collective-permute-start | bytes 3718664 | tf_op jit(solution)/shard_map/ppermute | solution.py:32
  173.6 27.0 %copy-start.4 = (f32[512,1152]{1,0:T(8,128)}, f32[512,1152]{1,0:T(8,128)S(1)}, u32[]{:S(2)}) copy-start(f32[512,1152]{1,0:T(8,128)S(1)} %subtract_multiply_fusion) | copy-start | bytes 7077892
  191.4 67.1 %collective-permute-start.28 = (bf16[256,1152]{1,0:T(8,128)(2,1)}, bf16[256,1152]{1,0:T(8,128)(2,1)}, u32[]{:S(2)}, u32[]{:S(2)}) collective-permute-start(bf16[256,1152]{1,0:T(8,128)(2,1)} %slice.537), channel_id=1, source_target_pairs={{0,4},{2,6},{4,0},{6,2},{1,5},{3,7},{5,1},{7,3},{8,12},{10,14},{12... | collective-permute-start | bytes 1769480 | tf_op jit(solution)/shard_map/ppermute | solution.py:28
  214.1 36.6 %collective-permute-start.32 = (bf16[256,1152]{1,0:T(8,128)(2,1)}, bf16[256,1152]{1,0:T(8,128)(2,1)S(1)}, u32[]{:S(2)}, u32[]{:S(2)}) collective-permute-start(bf16[256,1152]{1,0:T(8,128)(2,1)} %slice.536), channel_id=1, source_target_pairs={{0,4},{2,6},{4,0},{6,2},{1,5},{3,7},{5,1},{7,3},{8,12},{10,14},{12... | collective-permute-start | bytes 1769480 | tf_op jit(solution)/shard_map/ppermute | solution.py:28
  217.6 121.8 %collective-permute-start.50 = (bf16[1152,1076]{0,1:T(8,128)(2,1)}, bf16[1152,1076]{0,1:T(8,128)(2,1)}, u32[]{:S(2)}, u32[]{:S(2)}) collective-permute-start(bf16[1152,1076]{0,1:T(8,128)(2,1)} %slice.533), channel_id=1, source_target_pairs={{0,2},{2,0},{4,6},{6,4},{1,3},{3,1},{5,7},{7,5},{8,10},{10,8},{12,... | collective-permute-start | bytes 7437320 | tf_op jit(solution)/shard_map/ppermute | solution.py:32
  217.6 10.2 %collective-permute-start.52 = (f32[1076]{0:T(1024)S(1)}, f32[1076]{0:T(1024)S(1)}, u32[]{:S(2)}, u32[]{:S(2)}) collective-permute-start(f32[1076]{0:T(1024)S(1)} %slice.454), channel_id=1, source_target_pairs={{0,2},{2,0},{4,6},{6,4},{1,3},{3,1},{5,7},{7,5},{8,10},{10,8},{12,... | collective-permute-start | bytes 12920 | tf_op jit(solution)/shard_map/ppermute | solution.py:32
  227.8 25.0 %copy-start.19 = (bf16[256,576]{1,0:T(8,128)(2,1)S(1)}, bf16[256,576]{1,0:T(8,128)(2,1)}, u32[]{:S(2)}) copy-start(bf16[256,576]{1,0:T(8,128)(2,1)} %copy-done.18) | copy-start | bytes 884740
  227.9 119.8 %collective-permute-start.53 = (bf16[1076,1152]{1,0:T(8,128)(2,1)}, bf16[1076,1152]{1,0:T(8,128)(2,1)}, u32[]{:S(2)}, u32[]{:S(2)}) collective-permute-start(bf16[1076,1152]{1,0:T(8,128)(2,1)} %slice.532), channel_id=1, source_target_pairs={{0,2},{2,0},{4,6},{6,4},{1,3},{3,1},{5,7},{7,5},{8,10},{10,8},{12,... | collective-permute-start | bytes 7437320 | tf_op jit(solution)/shard_map/ppermute | solution.py:32
  257.8 23.6 %collective-permute-start.46 = (bf16[256,1152]{1,0:T(8,128)(2,1)S(1)}, bf16[256,1152]{1,0:T(8,128)(2,1)S(1)}, u32[]{:S(2)}, u32[]{:S(2)}) collective-permute-start(bf16[256,1152]{1,0:T(8,128)(2,1)S(1)} %convert_element_type.134), channel_id=1, source_target_pairs={{0,4},{2,6},{4,0},{6,2},{1,5},{3,7},{5,1},{7,3},{8,12},{10,14},{12... | collective-permute-start | bytes 1769480 | tf_op jit(solution)/shard_map/ppermute | solution.py:28
  258.5 18.6 %collective-permute-start.34 = (bf16[288,256]{1,0:T(8,128)(2,1)S(1)}, bf16[288,256]{1,0:T(8,128)(2,1)S(1)}, u32[]{:S(2)}, u32[]{:S(2)}) collective-permute-start(bf16[288,256]{1,0:T(8,128)(2,1)S(1)} %slice.406), channel_id=1, source_target_pairs={{0,1},{1,0},{2,3},{3,2},{4,5},{5,4},{6,7},{7,6},{8,9},{9,8},{10,11... | collective-permute-start | bytes 442376 | tf_op jit(solution)/shard_map/ppermute | solution.py:36
  258.5 17.6 %collective-permute-start.35 = (bf16[576,256]{1,0:T(8,128)(2,1)S(1)}, bf16[576,256]{1,0:T(8,128)(2,1)S(1)}, u32[]{:S(2)}, u32[]{:S(2)}) collective-permute-start(bf16[576,256]{1,0:T(8,128)(2,1)S(1)} %slice.407), channel_id=1, source_target_pairs={{0,4},{2,6},{4,0},{6,2},{1,5},{3,7},{5,1},{7,3},{8,12},{10,14},{12... | collective-permute-start | bytes 884744 | tf_op jit(solution)/shard_map/ppermute | solution.py:28
  276.1 5.2 collective-permute-start.36
  277.1 135.5 %collective-permute-start.29 = (bf16[256,576]{1,0:T(8,128)(2,1)}, bf16[256,576]{1,0:T(8,128)(2,1)}, u32[]{:S(2)}, u32[]{:S(2)}) collective-permute-start(bf16[256,576]{1,0:T(8,128)(2,1)} %get-tuple-element.198), channel_id=1, source_target_pairs={{0,1},{1,0},{2,3},{3,2},{4,5},{5,4},{6,7},{7,6},{8,9},{9,8},{10,11... | collective-permute-start | bytes 884744 | tf_op jit(solution)/shard_map/ppermute | solution.py:36
  281.3 1.8 collective-permute-start.37
  282.5 33.9 %collective-permute-start.47 = (bf16[288,1152]{1,0:T(8,128)(2,1)S(1)}, bf16[288,1152]{1,0:T(8,128)(2,1)S(1)}, u32[]{:S(2)}, u32[]{:S(2)}) collective-permute-start(bf16[288,1152]{1,0:T(8,128)(2,1)S(1)} %pad_maximum_fusion.13), channel_id=1, source_target_pairs={{0,2},{2,0},{4,6},{6,4},{1,3},{3,1},{5,7},{7,5},{8,10},{10,8},{12,... | collective-permute-start | bytes 1990664 | tf_op jit(solution)/shard_map/ppermute | solution.py:32
  309.3 30.1 %slice-start = ((s8[9916416]{0:T(1024)(128)(4,1)}), s8[4194304]{0:T(1024)(128)(4,1)S(1)}, s32[]{:S(2)}) async-start(s8[9916416]{0:T(1024)(128)(4,1)} %bitcast.26), calls=%async_computation.1 | async-start | bytes 8388608
  309.3 30.1 %slice-start.1 = ((s8[9916416]{0:T(1024)(128)(4,1)}), s8[4194304]{0:T(1024)(128)(4,1)S(1)}, s32[]{:S(2)}) async-start(s8[9916416]{0:T(1024)(128)(4,1)} %bitcast.26), calls=%async_computation.2 | async-start | bytes 8388608
  315.3 15.5 %collective-permute-start.45 = (bf16[576,432]{0,1:T(8,128)(2,1)S(1)}, bf16[576,432]{0,1:T(8,128)(2,1)S(1)}, u32[]{:S(2)}, u32[]{:S(2)}) collective-permute-start(bf16[576,432]{0,1:T(8,128)(2,1)S(1)} %get-tuple-element.178), channel_id=1, source_target_pairs={{0,1},{1,0},{2,3},{3,2},{4,5},{5,4},{6,7},{7,6},{8,9},{9,8},{10,11... | collective-permute-start | bytes 1493000 | tf_op jit(solution)/shard_map/ppermute | solution.py:36
  317.9 20.8 %collective-permute-start.48 = (bf16[288,576]{1,0:T(8,128)(2,1)S(1)}, bf16[288,576]{1,0:T(8,128)(2,1)S(1)}, u32[]{:S(2)}, u32[]{:S(2)}) collective-permute-start(bf16[288,576]{1,0:T(8,128)(2,1)S(1)} %slice.538), channel_id=1, source_target_pairs={{0,1},{1,0},{2,3},{3,2},{4,5},{5,4},{6,7},{7,6},{8,9},{9,8},{10,11... | collective-permute-start | bytes 995336 | tf_op jit(solution)/shard_map/ppermute | solution.py:36
  330.7 85.1 %collective-permute-start.33 = (bf16[256,576]{1,0:T(8,128)(2,1)}, bf16[256,576]{1,0:T(8,128)(2,1)}, u32[]{:S(2)}, u32[]{:S(2)}) collective-permute-start(bf16[256,576]{1,0:T(8,128)(2,1)} %slice.404), channel_id=1, source_target_pairs={{0,1},{1,0},{2,3},{3,2},{4,5},{5,4},{6,7},{7,6},{8,9},{9,8},{10,11... | collective-permute-start | bytes 884744 | tf_op jit(solution)/shard_map/ppermute | solution.py:36
  338.6 20.5 %collective-permute-start.38 = (bf16[1024,1152]{1,0:T(8,128)(2,1)}, bf16[1024,1152]{1,0:T(8,128)(2,1)}, u32[]{:S(2)}, u32[]{:S(2)}) collective-permute-start(bf16[1024,1152]{1,0:T(8,128)(2,1)} %convolution_convert_fusion), channel_id=1, source_target_pairs={{0,2},{2,0},{4,6},{6,4},{1,3},{3,1},{5,7},{7,5},{8,10},{10,8},{12,... | collective-permute-start | bytes 7077896 | tf_op jit(solution)/shard_map/ppermute | solution.py:32
  346.6 32.2 %collective-permute-start.51 = (bf16[576,1076]{1,0:T(8,128)(2,1)}, bf16[576,1076]{1,0:T(8,128)(2,1)}, u32[]{:S(2)}, u32[]{:S(2)}) collective-permute-start(bf16[576,1076]{1,0:T(8,128)(2,1)} %copy.138), channel_id=1, source_target_pairs={{0,1},{1,0},{2,3},{3,2},{4,5},{5,4},{6,7},{7,6},{8,9},{9,8},{10,11... | collective-permute-start | bytes 3718664 | tf_op jit(solution)/shard_map/ppermute | solution.py:36
  356.2 50.7 %collective-permute-start.54 = (bf16[1076,576]{0,1:T(8,128)(2,1)}, bf16[1076,576]{0,1:T(8,128)(2,1)}, u32[]{:S(2)}, u32[]{:S(2)}) collective-permute-start(bf16[1076,576]{0,1:T(8,128)(2,1)} %copy.140), channel_id=1, source_target_pairs={{0,1},{1,0},{2,3},{3,2},{4,5},{5,4},{6,7},{7,6},{8,9},{9,8},{10,11... | collective-permute-start | bytes 3718664 | tf_op jit(solution)/shard_map/ppermute | solution.py:36
  359.1 53.4 %collective-permute-start.49 = (f32[3,576]{1,0:T(4,128)S(1)}, f32[3,576]{1,0:T(4,128)S(1)}, u32[]{:S(2)}, u32[]{:S(2)}) collective-permute-start(f32[3,576]{1,0:T(4,128)S(1)} %slice.445), channel_id=1, source_target_pairs={{0,1},{1,0},{2,3},{3,2},{4,5},{5,4},{6,7},{7,6},{8,9},{9,8},{10,11... | collective-permute-start | bytes 20744 | tf_op jit(solution)/shard_map/ppermute | solution.py:36
  378.8 44.6 %collective-permute-start.39 = (bf16[256,1152]{1,0:T(8,128)(2,1)}, bf16[256,1152]{1,0:T(8,128)(2,1)}, u32[]{:S(2)}, u32[]{:S(2)}) collective-permute-start(bf16[256,1152]{1,0:T(8,128)(2,1)} %slice.416), channel_id=1, source_target_pairs={{0,4},{2,6},{4,0},{6,2},{1,5},{3,7},{5,1},{7,3},{8,12},{10,14},{12... | collective-permute-start | bytes 1769480 | tf_op jit(solution)/shard_map/ppermute | solution.py:28
  420.2 16.4 %collective-permute-start.40 = (bf16[512,576]{0,1:T(8,128)(2,1)}, bf16[512,576]{0,1:T(8,128)(2,1)S(1)}, u32[]{:S(2)}, u32[]{:S(2)}) collective-permute-start(bf16[512,576]{0,1:T(8,128)(2,1)} %copy.135), channel_id=1, source_target_pairs={{0,1},{1,0},{2,3},{3,2},{4,5},{5,4},{6,7},{7,6},{8,9},{9,8},{10,11... | collective-permute-start | bytes 1769480 | tf_op jit(solution)/shard_map/ppermute | solution.py:36
  422.8 25.4 %collective-permute-start.42 = (bf16[256,576]{1,0:T(8,128)(2,1)S(1)}, bf16[256,576]{1,0:T(8,128)(2,1)}, u32[]{:S(2)}, u32[]{:S(2)}) collective-permute-start(bf16[256,576]{1,0:T(8,128)(2,1)S(1)} %slice.422), channel_id=1, source_target_pairs={{0,4},{2,6},{4,0},{6,2},{1,5},{3,7},{5,1},{7,3},{8,12},{10,14},{12... | collective-permute-start | bytes 884744 | tf_op jit(solution)/shard_map/ppermute | solution.py:28
  425.1 23.1 %collective-permute-start.43 = (bf16[256,576]{1,0:T(8,128)(2,1)S(1)}, bf16[256,576]{1,0:T(8,128)(2,1)}, u32[]{:S(2)}, u32[]{:S(2)}) collective-permute-start(bf16[256,576]{1,0:T(8,128)(2,1)S(1)} %slice.539), channel_id=1, source_target_pairs={{0,1},{1,0},{2,3},{3,2},{4,5},{5,4},{6,7},{7,6},{8,9},{9,8},{10,11... | collective-permute-start | bytes 884744 | tf_op jit(solution)/shard_map/ppermute | solution.py:36
  437.6 12.1 %collective-permute-start.41 = (bf16[256,576]{1,0:T(8,128)(2,1)}, bf16[256,576]{1,0:T(8,128)(2,1)}, u32[]{:S(2)}, u32[]{:S(2)}) collective-permute-start(bf16[256,576]{1,0:T(8,128)(2,1)} %copy.152), channel_id=1, source_target_pairs={{0,4},{2,6},{4,0},{6,2},{1,5},{3,7},{5,1},{7,3},{8,12},{10,14},{12... | collective-permute-start | bytes 884744 | tf_op jit(solution)/shard_map/ppermute | solution.py:28
  451.6 63.4 %collective-permute-start.44 = (f32[2,512]{1,0:T(2,128)S(1)}, f32[2,512]{1,0:T(2,128)S(1)}, u32[]{:S(2)}, u32[]{:S(2)}) collective-permute-start(f32[2,512]{1,0:T(2,128)S(1)} %pad_maximum_fusion.30), channel_id=1, source_target_pairs={{0,1},{1,0},{2,3},{3,2},{4,5},{5,4},{6,7},{7,6},{8,9},{9,8},{10,11... | collective-permute-start | bytes 12296 | tf_op jit(solution)/shard_map/ppermute | solution.py:36
  (78 other events, 534.2 us)
Sparse Core Ops, SparseCore 0:
  412.7 155.3 all-reduce.4

commit v2 on v1

v2 whole, which is shorter than its diff:
```python
import jax
import jax.numpy as jnp
from jax import lax
from jax.experimental import pallas as pl
from jax.experimental.pallas import tpu as pltpu
from jax.sharding import PartitionSpec as P

DH = 72
PITCH = 80
SUB = 256
EPSILON = 1e-06
GELU_C = 0.7978845608028654
GELU_A = 0.044715
MASKED = -1e30
SCALE = DH**-0.5
SCALE2 = SCALE * 1.4426950408889634
BF = jnp.bfloat16
F32 = jnp.float32
MIB = 1024 * 1024


def swap_perm(axis, bit):
    return [(i, i ^ bit) for i in range(lax.axis_size(axis))]


def px(v):
    return lax.ppermute(v, "tr", swap_perm("tr", 2))


def pc(v):
    return lax.ppermute(v, "tr", swap_perm("tr", 1))


def py(v):
    return lax.ppermute(v, "tc", swap_perm("tc", 1))


def after(v, *earlier):
    return lax.optimization_barrier((v,) + earlier)[0]


def dot(a, b):
    return jnp.dot(a, b, preferred_element_type=F32)


def dot_tn(a, b):
    return lax.dot_general(a, b, (((0,), (0,)), ((), ())), preferred_element_type=F32)


def dot_nt(a, b):
    return lax.dot_general(a, b, (((1,), (1,)), ((), ())), preferred_element_type=F32)


def rows_at(v, first, count):
    return lax.dynamic_slice_in_dim(v, first, count, 0)


def cols_at(v, first, count):
    return lax.dynamic_slice_in_dim(v, first, count, 1)


def rel_rows(v, ypos):
    half = v.shape[0] // 2
    return jnp.concatenate((rows_at(v, ypos * half, half), rows_at(v, (1 - ypos) * half, half)), 0)


VM = pl.BlockSpec(memory_space=pltpu.VMEM)
SM = pl.BlockSpec(memory_space=pltpu.SMEM)


def shape(*dims, dtype=BF):
    return jax.ShapeDtypeStruct(dims, dtype)


def call(body, name, scalars, arrays, outs, us, scratch=(), vmem=24):
    return pl.pallas_call(
        body,
        out_shape=tuple(outs),
        in_specs=[SM] * len(scalars) + [VM] * len(arrays),
        out_specs=tuple([VM] * len(outs)),
        scratch_shapes=list(scratch),
        compiler_params=pltpu.CompilerParams(vmem_limit_bytes=vmem * MIB),
        cost_estimate=pl.CostEstimate(
            flops=int(us * 600e6), bytes_accessed=int(us * 3e6), transcendentals=0
        ),
        name=name,
    )(*scalars, *arrays)


def spots():
    return [(rc, ry, rx) for rc in range(2) for ry in range(2) for rx in range(2)]


def block_of(me, rc, ry, rx):
    return me ^ (rx * 4 + rc * 2 + ry)


def span(block):
    return pl.ds(pl.multiple_of(block * SUB, SUB), SUB)


def norm_qkv_kernel(
    scal, a00, b00, a01, b01, a10, b10, a11, b11, wa, wb, bias, gain, shift,
    h_ref, qkv_ref, kv_ref, res_ref, w_ref, gain_s, shift_s, bias_s,
):
    ypos, me = scal[0], scal[1]
    half = a00.shape[0]
    weights = jnp.concatenate((wa[...], wb[...]), 1)
    w_ref[...] = weights.T
    gain_s[...] = jnp.broadcast_to(gain[...], gain_s.shape)
    shift_s[...] = jnp.broadcast_to(shift[...], shift_s.shape)
    bias_s[...] = jnp.broadcast_to(bias[...], bias_s.shape)
    sources = {(0, 0): (a00, b00), (1, 0): (a01, b01), (0, 1): (a10, b10), (1, 1): (a11, b11)}
    for p, (rc, ry, rx) in enumerate(spots()):
        here = slice(p * SUB, (p + 1) * SUB)
        there = span(block_of(me, rc, ry, rx))
        cols = span(ypos ^ ry)
        sa, sb = sources[(rc, rx)]
        raw = jnp.concatenate((sa[:, cols], sb[:, cols]), 0)
        if rc == 0 and ry == 0:
            res_ref[:, rx * SUB : (rx + 1) * SUB] = raw
        v = raw.astype(F32)
        mean = jnp.sum(v, axis=0, keepdims=True) / (2 * half)
        square = jnp.sum(v * v, axis=0, keepdims=True) / (2 * half)
        root = lax.rsqrt(square - mean * mean + EPSILON)
        hidden = ((v - mean) * root * gain_s[...] + shift_s[...]).astype(BF)
        h_ref[:, here] = hidden
        qkv = (dot(weights, hidden) + bias_s[...]).astype(BF)
        qkv_ref[:, there] = qkv
        for i in range(4):
            kv_ref[there, 128 * i : 128 * i + PITCH] = qkv[PITCH * (2 + i) : PITCH * (3 + i), :].T


def attend_kernel(scal, klo, khi, qkv, kv, lo, hi, o00, o01, o10, o11, lse):
    me = scal[1]
    outs = {(0, 0): o00, (0, 1): o01, (1, 0): o10, (1, 1): o11}
    places = lax.broadcasted_iota(jnp.int32, (SUB, SUB), 0)
    lanes = lax.broadcasted_iota(jnp.int32, (1, SUB), 1)
    for rc, ry, rx in sorted(spots(), reverse=True):
        block = block_of(me, rc, ry, rx)
        cols = span(block)
        low, high = lo[:, cols], hi[:, cols]
        own = lanes + block * SUB

        def body(kb, carry):
            base = kb * SUB
            allowed = ((places >= low - base) & (places < high - base)) | (places == own - base)
            new = []
            for h in range(2):
                top, acc = carry[h]
                s = dot(kv[span(kb), 128 * h : 128 * h + PITCH], qkv[PITCH * h : PITCH * (h + 1), cols])
                s = jnp.where(allowed, s, MASKED)
                newtop = jnp.maximum(top, jnp.max(s, axis=0, keepdims=True))
                alpha = jnp.exp2((top - newtop) * SCALE2)
                weights = jnp.exp2((s - newtop) * SCALE2).astype(BF)
                acc = acc * alpha + dot(qkv[PITCH * (4 + h) : PITCH * (5 + h), span(kb)], weights)
                new.append((newtop, acc))
            return tuple(new)

        start = (jnp.full((1, SUB), MASKED, F32), jnp.zeros((PITCH, SUB), F32))
        done = lax.fori_loop(klo[block], khi[block], body, (start, start))
        heads = []
        for h in range(2):
            top, acc = done[h]
            total = acc[DH : DH + 1, :]
            heads.append(acc[:DH, :] / total)
            lse[h : h + 1, cols] = top * SCALE2 + jnp.log2(total)
        outs[(rc, ry)][:, rx * SUB : (rx + 1) * SUB] = jnp.concatenate(heads, 0).astype(BF)


def attend_back_kernel(
    scal, qlo, qhi, qkv, kv, lo, hi, lse, o00, o01, o10, o11, g00, g10, g01, g11, gs, out,
    gt, delta, dqt, dk, dv,
):
    me = scal[1]
    outs = {(0, 0): o00, (0, 1): o01, (1, 0): o10, (1, 1): o11}
    grads = {(0, 0): g00, (0, 1): g01, (1, 0): g10, (1, 1): g11}
    for rc, ry, rx in spots():
        cols = span(block_of(me, rc, ry, rx))
        if rc == 0:
            gtile = grads[(rx, ry)][0 : 2 * DH, :].astype(F32)
        else:
            gtile = gs[:, (ry * 2 + rx) * SUB : (ry * 2 + rx + 1) * SUB].astype(F32)
        both = gtile * outs[(rc, ry)][:, rx * SUB : (rx + 1) * SUB].astype(F32)
        for h in range(2):
            part = slice(DH * h, DH * (h + 1))
            padded = jnp.concatenate((gtile[part], jnp.zeros((PITCH - DH, SUB), F32)), 0)
            gt[PITCH * h : PITCH * (h + 1), cols] = padded.astype(BF)
            delta[h : h + 1, cols] = jnp.sum(both[part], axis=0, keepdims=True)
    dqt[...] = jnp.zeros_like(dqt)
    dk[...] = jnp.zeros_like(dk)
    dv[...] = jnp.zeros_like(dv)
    places = lax.broadcasted_iota(jnp.int32, (SUB, SUB), 0)
    lanes = lax.broadcasted_iota(jnp.int32, (1, SUB), 1)

    @pl.loop(0, 8)
    def _(kb):
        keys = span(kb)
        base = kb * SUB

        def body(qb, carry):
            cols = span(qb)
            low, high = lo[:, cols] - base, hi[:, cols] - base
            own = lanes + (qb * SUB - base)
            allowed = ((places >= low) & (places < high)) | (places == own)
            for h in range(2):
                head = slice(PITCH * h, PITCH * (h + 1))
                s = dot(kv[keys, 128 * h : 128 * h + PITCH], qkv[head, cols])
                probs = jnp.where(allowed, jnp.exp2(s * SCALE2 - lse[h : h + 1, cols]), 0.0)
                gprobs = dot(kv[keys, 256 + 128 * h : 256 + 128 * h + PITCH], gt[head, cols])
                gscores = (probs * (gprobs - delta[h : h + 1, cols])).astype(BF)
                dv[h, keys, :] += dot_nt(probs.astype(BF), gt[head, cols])
                dk[h, keys, :] += dot_nt(gscores, qkv[head, cols])
                dqt[head, cols] += dot(qkv[PITCH * (2 + h) : PITCH * (3 + h), keys], gscores)
            return carry

        lax.fori_loop(qlo[kb], qhi[kb], body, 0)

    for p, (rc, ry, rx) in enumerate(spots()):
        here = slice(p * SUB, (p + 1) * SUB)
        rows = span(block_of(me, rc, ry, rx))
        out[: 2 * PITCH, here] = (dqt[:, rows] * SCALE).astype(BF)
        for h in range(2):
            out[PITCH * (2 + h) : PITCH * (3 + h), here] = (dk[h, rows, :].T * SCALE).astype(BF)
            out[PITCH * (4 + h) : PITCH * (5 + h), here] = dv[h, rows, :].T.astype(BF)


def mix_kernel(o0, o1, o2, o3, x0, x1, x2, x3, woa, wob, res, bias, gain, shift, mixed, h2t, h2):
    weights = jnp.concatenate((woa[...], wob[...]), 1)
    for rx in range(2):
        here = slice(rx * SUB, (rx + 1) * SUB)
        turned = slice((1 - rx) * SUB, (2 - rx) * SUB)
        att = jnp.concatenate([o[:, here] for o in (o0, o1, o2, o3)] + [x[:, turned] for x in (x0, x1, x2, x3)], 0)
        v = res[:, here].astype(F32) + dot_tn(weights, att) + bias[...]
        mixed[:, here] = v
        mean = jnp.mean(v, axis=0, keepdims=True)
        root = lax.rsqrt(jnp.mean(v * v, axis=0, keepdims=True) - mean * mean + EPSILON)
        hidden = ((v - mean) * root * gain[...] + shift[...]).astype(BF)
        h2t[:, here] = hidden
        h2[here, :] = hidden.T


def gelu_both(u):
    square = u * u
    tangent = jnp.tanh(GELU_C * (u + GELU_A * square * u))
    plus = 0.5 * (1.0 + tangent)
    slope = plus + 0.5 * u * (1.0 - tangent * tangent) * GELU_C * (1.0 + 3.0 * GELU_A * square)
    return u * plus, slope


def feed_kernel(h2, go, uaa, uba, uas, ubs, daa, dba, das, dbs, bias, act0, act1, gu0, gu1, send):
    for k, (ua, ub, da, db, act, gu) in enumerate(
        ((uaa, uba, daa, dba, act0, gu0), (uas, ubs, das, dbs, act1, gu1))
    ):
        upper = dot(h2[...], jnp.concatenate((ua[...], ub[...]), 0)) + bias[k : k + 1, :]
        value, slope = gelu_both(upper)
        act[...] = value.astype(BF)
        gact = dot(go[...], jnp.concatenate((da[...], db[...]), 0))
        gu[...] = (gact * slope).astype(BF)
    half = uaa.shape[0]
    other = slice(SUB, 2 * SUB)
    for first, u0, u1 in ((0, uaa, uas), (half, uba, ubs)):
        part = dot_nt(u0[...], gu0[other, :]) + dot_nt(u1[...], gu1[other, :])
        send[first : first + half, :] = part.astype(BF)


def feed_back_kernel(uaa, uba, uas, ubs, gu0, gu1, own):
    half = uaa.shape[0]
    here = slice(0, SUB)
    for first, u0, u1 in ((0, uaa, uas), (half, uba, ubs)):
        own[first : first + half, :] = dot_nt(u0[...], gu0[here, :]) + dot_nt(u1[...], gu1[here, :])


def norm2_back_kernel(own, recv, mixed, go, gain, woa, wob, gm, low, g_own, g_y, g_x, sums):
    e = own[...] + recv[...].astype(F32)
    v = mixed[:, :SUB]
    mean = jnp.mean(v, axis=0, keepdims=True)
    root = lax.rsqrt(jnp.mean(v * v, axis=0, keepdims=True) - mean * mean + EPSILON)
    n = (v - mean) * root
    w = e * gain[...]
    grad = go[...].astype(F32) + root * (
        w - jnp.mean(w, axis=0, keepdims=True) - n * jnp.mean(w * n, axis=0, keepdims=True)
    )
    gm[...] = grad
    rounded = grad.astype(BF)
    low[...] = rounded
    half = woa.shape[1]
    gatt = (dot(woa[...], rounded[:half]) + dot(wob[...], rounded[half:])).astype(BF)
    n2 = 2 * DH
    g_own[...] = gatt[: 2 * n2]
    g_y[...] = gatt[2 * n2 : 4 * n2]
    g_x[...] = gatt[4 * n2 :]
    sums[:, 0:1] = jnp.sum(e * n, axis=1, keepdims=True)
    sums[:, 1:2] = jnp.sum(e, axis=1, keepdims=True)
    sums[:, 2:3] = jnp.sum(grad, axis=1, keepdims=True)


def part_kernel(w, dqkv, send):
    send[...] = dot(w[...], dqkv[:, 4 * SUB :]).astype(BF)


HALF = SUB // 2


def spread_kernel(w, dqkv, recv, to_x, to_y, keep_p, keep_q):
    half = w.shape[0] // 2
    total = dot(w[...], dqkv[:, : 4 * SUB]) + recv[...].astype(F32)
    for ry in range(2):
        at = slice(ry * HALF, (ry + 1) * HALF)
        for rx in range(2):
            first = (ry * 2 + rx) * SUB
            p = total[:, first : first + HALF]
            q = total[:, first + HALF : first + SUB]
            if rx == 0:
                keep_p[:, at] = p
            else:
                to_x[:, at] = p.astype(BF)
            where = slice((ry * 2 + rx) * HALF, (ry * 2 + rx + 1) * HALF)
            keep_q[:, where] = q[:half]
            to_y[:, where] = q[half:].astype(BF)


def spread2_kernel(keep_p, keep_q, from_x, from_y, to_x, to_y, own_p, own_q):
    half = own_p.shape[0]
    p = keep_p[...] + from_x[...].astype(F32)
    own_p[...] = p[:half]
    to_y[...] = p[half:].astype(BF)
    for ry in range(2):
        at = slice(ry * HALF, (ry + 1) * HALF)
        for rx in range(2):
            mine = slice((ry * 2 + rx) * HALF, (ry * 2 + rx + 1) * HALF)
            theirs = slice(((1 - ry) * 2 + rx) * HALF, ((1 - ry) * 2 + rx + 1) * HALF)
            q = keep_q[:, mine] + from_y[:, theirs].astype(F32)
            if rx == 0:
                own_q[:, at] = q
            else:
                to_x[:, at] = q.astype(BF)


def norm1_stats_kernel(scal, own_p, own_q, from_x, from_y, a, b, gain, grad, normed, stats, sums):
    ypos = scal[0]
    half = a.shape[0]
    for ry in range(2):
        at = slice(ry * HALF, (ry + 1) * HALF)
        other = slice((1 - ry) * HALF, (2 - ry) * HALF)
        e = jnp.concatenate(
            (own_p[:, at] + from_y[:, other].astype(F32), own_q[:, at] + from_x[:, at].astype(F32)), 1
        )
        here = slice(ry * SUB, (ry + 1) * SUB)
        cols = span(ypos ^ ry)
        va, vb = a[:, cols].astype(F32), b[:, cols].astype(F32)
        mean = (jnp.sum(va, 0, keepdims=True) + jnp.sum(vb, 0, keepdims=True)) / (2 * half)
        square = (jnp.sum(va * va, 0, keepdims=True) + jnp.sum(vb * vb, 0, keepdims=True)) / (2 * half)
        root = lax.rsqrt(square - mean * mean + EPSILON)
        n = (va - mean) * root
        w = e * gain[...]
        grad[:, here] = w
        normed[:, here] = n
        stats[0:1, here] = jnp.sum(w, 0, keepdims=True)
        stats[1:2, here] = jnp.sum(w * n, 0, keepdims=True)
        stats[2:3, here] = root
        more = (jnp.sum(e * n, 1, keepdims=True), jnp.sum(e, 1, keepdims=True))
        for i in range(2):
            if ry == 0:
                sums[:, i : i + 1] = more[i]
            else:
                sums[:, i : i + 1] += more[i]


def norm1_back_kernel(scal, grad, normed, stats, recv, gm_own, gm_y, out):
    ypos = scal[0]
    width = 2 * grad.shape[0]
    for ry in range(2):
        here = slice(ry * SUB, (ry + 1) * SUB)
        other = slice((1 - ry) * SUB, (2 - ry) * SUB)
        total = (stats[0:1, here] + recv[0:1, other]) / width
        along = (stats[1:2, here] + recv[1:2, other]) / width
        gm = gm_own[: grad.shape[0], :] if ry == 0 else gm_y[...].astype(F32)
        whole = gm + stats[2:3, here] * (grad[:, here] - total - normed[:, here] * along)
        out[:, span(ypos ^ ry)] = whole.astype(BF)


def local(
    layer_input, picture, token_kept, ln1_gain, ln1_bias, w_query, b_query, w_key, w_value, b_value,
    w_out, b_out, ln2_gain, ln2_bias, w_up, b_up, w_down, b_down, grad_out,
):
    ypos = lax.axis_index("tc").astype(jnp.int32)
    trpos = lax.axis_index("tr").astype(jnp.int32)
    me = trpos * 2 + ypos
    half = layer_input.shape[1]
    width = 2 * half
    seq = picture.shape[0]
    n2 = b_query.shape[0]
    units = w_up.shape[1]
    scal = jnp.stack((ypos, me))

    a00 = layer_input.T
    a10, b00 = px(a00), py(a00)
    weights = (w_query.T, w_key.T, w_value.T)
    wa = jnp.concatenate([rows_at(w, ypos * n2, n2) for w in weights], 0)
    wb = py(after(jnp.concatenate([rows_at(w, (1 - ypos) * n2, n2) for w in weights], 0), b00))
    b10 = px(b00)
    a01, b01, a11, b11 = pc(a00), pc(b00), pc(a10), pc(b10)

    small = jnp.stack((ln1_gain, ln1_bias, ln2_gain, ln2_bias, b_out, b_down))
    both = jnp.concatenate((small, py(small)), 1)[:, :, None]
    gain1, shift1, gain2, shift2, bias_out, bias_down = [both[i] for i in range(6)]
    up_y = py(b_up)
    up_own = jnp.where(ypos == 0, jnp.concatenate((b_up, up_y)), jnp.concatenate((up_y, b_up)))
    bias_up = jnp.stack((up_own, pc(up_own)))

    def padded(w):
        w = w.reshape(6, DH, w.shape[1])
        return jnp.pad(w, ((0, 0), (0, PITCH - DH), (0, 0))).reshape(6 * PITCH, -1)

    qkv_bias = jnp.concatenate((b_query, jnp.zeros_like(b_query), b_value)).reshape(6, DH)
    ones = (jnp.arange(6) >= 4).astype(F32)[:, None]
    qkv_bias = jnp.concatenate((qkv_bias, ones, jnp.zeros((6, PITCH - DH - 1), F32)), 1).reshape(-1, 1)

    numbers = jnp.arange(8, dtype=jnp.int32)[:, None]
    hot = (picture[None, :] == numbers).astype(jnp.int32)
    counts = jnp.sum(hot, axis=1)
    kept = jnp.sum(hot * token_kept[None, :], axis=1)
    starts = jnp.cumsum(counts) - counts
    lo = jnp.sum(hot * starts[:, None], axis=0)
    hi = jnp.sum(hot * (starts + kept)[:, None], axis=0)
    end = jnp.sum(hot * (starts + counts)[:, None], axis=0)
    blocks = seq // SUB
    klo = qlo = lo.reshape(blocks, SUB)[:, 0] // SUB
    lasts = jnp.arange(1, blocks + 1, dtype=jnp.int32) * SUB
    khi = (jnp.maximum(lasts, hi.reshape(blocks, SUB)[:, -1]) + SUB - 1) // SUB
    qhi = (jnp.maximum(lasts, end.reshape(blocks, SUB)[:, -1]) + SUB - 1) // SUB
    lo, hi = lo[None, :], hi[None, :]

    h1, qkv, kv, resid, w_all = call(
        norm_qkv_kernel, "norm_qkv", (scal,),
        (a00, b00, a01, b01, a10, b10, a11, b11, padded(wa), padded(wb), qkv_bias, gain1, shift1),
        (shape(width, seq), shape(6 * PITCH, seq), shape(seq, 512), shape(width, 2 * SUB), shape(width, 6 * PITCH)),
        8,
        scratch=[pltpu.VMEM((width, SUB), F32)] * 2 + [pltpu.VMEM((6 * PITCH, SUB), F32)],
        vmem=32,
    )

    wo_own = rel_rows(w_out, ypos)
    wo_y = rel_rows(py(after(wo_own, wb)), 1)
    wo_sib, wo_ysib = pc(wo_own), pc(wo_y)

    def by_heads(own, sib):
        return jnp.concatenate((own[:n2], sib[:n2], own[n2:], sib[n2:]), 0)

    wo_a, wo_b = by_heads(wo_own, wo_sib), by_heads(wo_y, wo_ysib)
    wo_a = jnp.concatenate((wo_a, px(after(wo_a, b10))), 0)
    wo_b = jnp.concatenate((wo_b, px(wo_b)), 0)
    u_aa = w_up
    u_ba = py(after(w_up, wo_y))
    u_as, u_bs = pc(u_aa), pc(u_ba)
    go_t = grad_out.T
    go_own = cols_at(go_t, ypos * SUB, SUB)
    go_send = cols_at(go_t, (1 - ypos) * SUB, SUB)
    go_b = py(after(go_send, wo_y))
    go_mine = jnp.concatenate((go_own, go_b), 0)
    go_both = jnp.concatenate((go_mine, px(after(go_mine, b10))), 1)
    go = go_both.T
    d_aa = w_down.T
    d_ba = py(after(d_aa, u_ba))
    d_as, d_bs = pc(d_aa), pc(d_ba)

    o00, o01, o10, o11, lse = call(
        attend_kernel, "attend", (scal, klo, khi), (qkv, kv, lo, hi),
        (shape(n2, 2 * SUB),) * 4 + (shape(2, seq, dtype=F32),), 18,
    )
    c0, c1 = pc(o10), pc(o11)
    y0, y1 = py(o01), py(c1)
    x0, x1, xy0, xy1 = px(o00), px(c0), px(y0), px(y1)
    mixed, h2t, h2 = call(
        mix_kernel, "mix", (),
        (o00, c0, y0, y1, x0, x1, xy0, xy1, wo_a, wo_b, resid, bias_out, gain2, shift2),
        (shape(width, 2 * SUB, dtype=F32), shape(width, 2 * SUB), shape(2 * SUB, width)), 6,
    )

    act0, act1, gu0, gu1, gh_send = call(
        feed_kernel, "feed", (),
        (h2, go, u_aa, u_ba, u_as, u_bs, d_aa, d_ba, d_as, d_bs, bias_up),
        (shape(2 * SUB, units),) * 4 + (shape(width, SUB),), 12, vmem=40,
    )
    gh_recv = px(gh_send)
    (gh_own,) = call(
        feed_back_kernel, "feed_back", (), (u_aa, u_ba, u_as, u_bs, gu0, gu1),
        (shape(width, SUB, dtype=F32),), 3,
    )
    gm, gm_low, g_own, g_y, g_x, sums2 = call(
        norm2_back_kernel, "norm2_back", (),
        (gh_own, gh_recv, mixed, go_mine, gain2, wo_a, wo_b),
        (
            shape(width, SUB, dtype=F32), shape(width, SUB), shape(2 * n2, SUB), shape(2 * n2, SUB),
            shape(4 * n2, SUB), shape(width, 3, dtype=F32),
        ),
        4,
    )
    gx = px(g_x)
    gy = py(g_y)
    gxy = py(gx[2 * n2 :])
    gs = pc(jnp.concatenate((g_own[n2:], gx[n2 : 2 * n2], gy[n2:], gxy[n2:]), 1))
    (dqkv,) = call(
        attend_back_kernel, "attend_back", (scal, qlo, qhi),
        (qkv, kv, lo, hi, lse, o00, o01, o10, o11, g_own, gx, gy, gxy, gs),
        (shape(6 * PITCH, seq),), 22,
        scratch=[
            pltpu.VMEM((2 * PITCH, seq), BF), pltpu.VMEM((2, seq), F32), pltpu.VMEM((2 * PITCH, seq), F32),
            pltpu.VMEM((2, seq, PITCH), F32), pltpu.VMEM((2, seq, PITCH), F32),
        ],
    )

    part_d = [dot(go_both, act).astype(BF) for act in (act0, act1)]
    dwd = part_d[0].astype(F32) + pc(part_d[1]).astype(F32)
    dwd = dwd[:half] + py(dwd[half:].astype(BF)).astype(F32)
    part_u = [dot(h2t, gu).astype(BF) for gu in (gu0, gu1)]
    dwu = part_u[0].astype(F32) + pc(part_u[1]).astype(F32)
    dwu = dwu[:half] + py(dwu[half:].astype(BF)).astype(F32)
    gm_x, gm_y = px(gm_low), py(gm_low[half:])
    gm_both = jnp.concatenate((gm_low, gm_x), 1)
    dwo_own = dot_nt(jnp.concatenate((o00, y0), 0), gm_both)
    dwo_sib = dot_nt(jnp.concatenate((c0, y1), 0), gm_both).astype(BF)
    dwo = dwo_own + pc(dwo_sib).astype(F32)
    dwo = dwo[:, :half] + rel_rows(py(dwo[:, half:].astype(BF)), 1).astype(F32)

    part_r = dot_nt(jnp.concatenate((jnp.concatenate((d_aa, d_as), 1), jnp.concatenate((d_ba, d_bs), 1)), 0),
                    jnp.concatenate((act0, act1), 1))
    result = mixed[:, :SUB] + part_r[:, :SUB] + px(part_r[:, SUB:].astype(BF)).astype(F32) + bias_down
    result = result.astype(BF)

    def by_place(own, other):
        return jnp.where(ypos == 0, jnp.concatenate((own, other), 1), jnp.concatenate((other, own), 1))

    result = by_place(result[:half], py(result[half:])).T

    (p_send,) = call(part_kernel, "part", (), (w_all, dqkv), (shape(width, 4 * SUB),), 3)
    p_recv = pc(p_send)
    to_x, to_y, keep_p, keep_q = call(
        spread_kernel, "spread", (), (w_all, dqkv, p_recv),
        (shape(width, SUB), shape(half, 2 * SUB), shape(width, SUB, dtype=F32), shape(half, 2 * SUB, dtype=F32)), 4,
    )
    to_x2, to_y2, own_p, own_q = call(
        spread2_kernel, "spread2", (), (keep_p, keep_q, px(to_x), py(to_y)),
        (shape(half, SUB), shape(half, SUB), shape(half, SUB, dtype=F32), shape(half, SUB, dtype=F32)), 2,
    )
    grad, normed, stats, sums1 = call(
        norm1_stats_kernel, "norm1_stats", (scal,),
        (own_p, own_q, px(to_x2), py(to_y2), a00, b00, ln1_gain[:, None]),
        (
            shape(half, 2 * SUB, dtype=F32), shape(half, 2 * SUB, dtype=F32),
            shape(8, 2 * SUB, dtype=F32), shape(half, 2, dtype=F32),
        ),
        2,
    )
    (gin,) = call(
        norm1_back_kernel, "norm1_back", (scal,), (grad, normed, stats, py(stats), gm, gm_y),
        (shape(half, 2 * SUB),), 1,
    )

    dwq = dot_nt(dqkv, h1).astype(BF).reshape(6, PITCH, width)[:, :DH].reshape(3, n2, width)
    dwq_y = py(dwq[:, :, half:])
    dwq = jnp.stack((dwq[:, :, :half], dwq_y), 1)
    dwq = lax.psum(dwq, "dp").astype(F32)
    dwq = jnp.where(ypos == 0, dwq, dwq[:, ::-1]).reshape(3, 2 * n2, half)

    dwd, dwu, dwo = lax.psum((dwd.astype(BF), dwu.astype(BF), dwo.astype(BF)), "dp")

    sums2 = sums2[:half] + py(sums2[half:])
    sum_down = jnp.sum(go_t.astype(F32), 1, keepdims=True)
    totals = lax.psum(jnp.concatenate((sums1, sums2, sum_down), 1), ("dp", "tr"))
    gbu = jnp.stack((jnp.sum(gu0, 0, dtype=F32), jnp.sum(gu1, 0, dtype=F32)))
    gbu = gbu[0] + pc(gbu[1])
    sums_q = jnp.sum(dqkv, 1, dtype=F32).reshape(3, 2, PITCH)[:, :, :DH].reshape(3, n2)
    gbu = lax.psum(gbu, ("dp", "tc"))
    n_up = b_up.shape[0]
    gbu = lax.dynamic_slice_in_dim(gbu, ypos * n_up, n_up, 0)
    sums_q = lax.psum(sums_q, "dp")
    return (
        result, gin.T, totals[:, 0], totals[:, 1], dwq[0].T, sums_q[0], dwq[1].T, dwq[2].T, sums_q[2],
        rel_rows(dwo.astype(F32), ypos), totals[:, 4], totals[:, 2], totals[:, 3],
        dwu.astype(F32), gbu, dwd.astype(F32).T, totals[:, 5],
    )


def solution(mesh):
    rows = P(("dp", "tr"), "tc")
    placed = (
        rows, P("dp"), P("dp"), P("tc"), P("tc"), P("tc", "tr"), P(("tr", "tc")), P("tc", "tr"),
        P("tc", "tr"), P(("tr", "tc")), P("tr", "tc"), P("tc"), P("tc"), P("tc"), P("tc", "tr"),
        P(("tr", "tc")), P("tr", "tc"), P("tc"), rows,
    )
    outs = (
        rows, rows, P("tc"), P("tc"), P("tc", "tr"), P(("tr", "tc")), P("tc", "tr"), P("tc", "tr"),
        P(("tr", "tc")), P("tr", "tc"), P("tc"), P("tc"), P("tc"), P("tc", "tr"), P(("tr", "tc")),
        P("tr", "tc"), P("tc"),
    )
    return jax.shard_map(local, mesh=mesh, in_specs=placed, out_specs=outs, check_vma=False)
```

time: 598 us -> 536 us (0.90); the launches traced: 587 us -> 532 us
  waiting for transfers between devices: 194 us -> 135 us
  Pallas kernels: 57.6 us -> 91.8 us
  matrix products: 55.2 us -> 24.1 us
  other arithmetic: 49 us -> 27.9 us
  blocking collectives: 92.8 us -> 102 us
  local copies, waits for them, and re-layouts: 84.2 us -> 92.1 us
    psum x1, waiting for transfers between devices: 50.1 us -> 0.01 us  [local(): lax.psum((dwd.astype(BF), dwu.astype(BF), dwo.astype(BF)), 'dp')]
    ppermute x22, waiting for transfers between devices: 107 us -> 69.2 us  [py(): return lax.ppermute(v, 'tc', swap_perm('tc', 1))]
    pallas_call x3 -> x12, Pallas kernels: 57.6 us -> 91.8 us  [call(): pl.pallas_call(body, out_shape=tuple(outs), in_specs=[SM] * len(scalars)...]
    ppermute x15, waiting for transfers between devices: 33.2 us -> 65.8 us  [px(): return lax.ppermute(v, 'tr', swap_perm('tr', 2))]
    dot_general x4 -> x0, matrix products: 14.7 us -> none  [dot_tn(): lax.dot_general(a, b, (((0,), (0,)), ((), ())), preferred_element_type=F32)]
    unnamed x188 -> x273, local copies, waits for them, and re-layouts: 28.9 us -> 43.2 us
    ppermute x6 -> x0, local copies, waits for them, and re-layouts: 12.9 us -> none  [the longest x4 8.61 us: pc(): return lax.ppermute(v, 'tr', swap_perm('tr', 1))]
    dot_general x5 -> x4, matrix products: 26.6 us -> 14 us  [dot_nt(): lax.dot_general(a, b, (((1,), (1,)), ((), ())), preferred_element_type=F32)]
  transfers between devices with their start and end apart: 56 -> 57, of which waited for: 20 -> 15; matrix products, arithmetic and copies ran while one was open for 27% -> 20% of each run, Pallas kernels for 10% -> 15%
where the time goes in v2:
time: 536 us; the launch traced here: 532 us
  waiting for transfers between devices  135 us (25%)
  blocking collectives  102 us (19%)
  local copies, waits for them, and re-layouts  92.1 us (17%)
  Pallas kernels  91.8 us (17%)
  starting transfers between devices  43.7 us (8%)
  other arithmetic  27.9 us (5%)
  matrix products  24.1 us (4%)
  between operations  15.9 us (3%)
    pallas_call x12, Pallas kernels, call(): pl.pallas_call(body, out_shape=tuple(outs), in_specs=[SM] * len(scalars)...  91.8 us
    ppermute x22, waiting for transfers between devices, py(): return lax.ppermute(v, 'tc', swap_perm('tc', 1))  69.2 us
    ppermute x15, waiting for transfers between devices, px(): return lax.ppermute(v, 'tr', swap_perm('tr', 2))  65.8 us
    psum x1, blocking collectives, local(): lax.psum(jnp.concatenate((sums1, sums2, sum_down), 1), ('dp', 'tr'))  59.8 us
    unnamed x273, local copies, waits for them, and re-layouts  43.2 us
    psum x1, blocking collectives, local(): gbu = lax.psum(gbu, ('dp', 'tc'))  29.9 us
    ppermute x22, starting transfers between devices, py(): return lax.ppermute(v, 'tc', swap_perm('tc', 1))  23.2 us
    ppermute x15, starting transfers between devices, px(): return lax.ppermute(v, 'tr', swap_perm('tr', 2))  18 us
  transfers between devices with their start and end apart: 57, of which 15 were waited for; matrix products, arithmetic and copies ran while one was open for 20% of the time, Pallas kernels for 15%

profile of v2, /device:TPU:0, one launch (start us, length us, event | category | flops | bytes accessed | tf_op | source)
XLA Modules:
  0.0 532.1 jit_solution(6381167996590429150)
XLA Ops:
  7.3 3.0 collective-permute-start
  11.8 1.7 constant_dynamic-update-slice_fusion.4
  17.5 6.6 %collective-permute-done.b00.b = bf16[576,512]{1,0:T(8,128)(2,1)} collective-permute-done((bf16[576,512]{1,0:T(8,128)(2,1)}, bf16[576,512]{1,0:T(8,128)(2,1)}, u32[]{:S(2)}, u32[]{:S(2)}) %collective-permute-start) | collective-permute-done | bytes 589856 | tf_op jit(solution)/shard_map/ppermute | solution.py:35
  24.0 1.7 collective-permute-start.7
  28.0 9.8 %collective-permute-done.7 = bf16[432,576]{1,0:T(8,128)(2,1)} collective-permute-done((bf16[432,576]{1,0:T(8,128)(2,1)S(1)}, bf16[432,576]{1,0:T(8,128)(2,1)}, u32[]{:S(2)}, u32[]{:S(2)}) %collective-permute-start.7) | collective-permute-done | bytes 497696 | tf_op jit(solution)/shard_map/ppermute | solution.py:35
  41.6 5.5 %collective-permute-done.19 = bf16[288,576]{1,0:T(8,128)(2,1)S(1)} collective-permute-done((bf16[288,576]{1,0:T(8,128)(2,1)}, bf16[288,576]{1,0:T(8,128)(2,1)S(1)}, u32[]{:S(2)}, u32[]{:S(2)}) %collective-permute-start.19) | collective-permute-done | bytes 331808 | tf_op jit(solution)/shard_map/ppermute | solution.py:35
  51.7 3.7 collective-permute-done.4.b10
  55.4 2.2 fusion.26
  57.6 1.8 copy.85.gain
  59.4 1.8 copy.86.shift
  61.1 1.8 copy.88.gain
  62.9 1.8 copy.87.bias
  65.7 1.7 fusion.37
  67.5 1.8 constant_dynamic-update-slice_fusion.2
  73.8 7.1 %norm_qkv.1 = (bf16[1152,2048]{1,0:T(8,128)(2,1)S(1)}, bf16[480,2048]{1,0:T(8,128)(2,1)S(1)}, bf16[2048,512]{1,0:T(8,128)(2,1)S(1)}, bf16[1152,512]{1,0:T(8,128)(2,1)S(1)}, bf16[1152,480]{1,0:T(8,128)(2,1)S(1)}) custom-call(s32[2]{0:T(128)S(1)} %pad_add_fusion.scal, bf16[576,512]{1,0:T(8,128)(2,1)S(1)} %bitcast.85, ...), custom_call_target="tpu_custom_call" | custom-call | flops 4800000000 | bytes 24000000 | tf_op jit(solution)/shard_map/norm_qkv/pallas_call | solution.py:76
  82.5 28.4 %attend.1 = (bf16[144,512]{1,0:T(8,128)(2,1)S(1)}, bf16[144,512]{1,0:T(8,128)(2,1)S(1)}, bf16[144,512]{1,0:T(8,128)(2,1)S(1)}, bf16[144,512]{1,0:T(8,128)(2,1)S(1)}, f32[2,2048]{1,0:T(2,128)S(1)}) custom-call(s32[2]{0:T(128)S(1)} %pad_add_fusion.scal, s32[8]{0:T(128)S(1)} %get-tuple-element.245.klo.qlo, s32[8]{0:T(128)S(1)} %get-tuple-element.244.khi, ...), custom_call_target="tpu_custom_call" | custom-call | flops 10800000000 | bytes 54000000 | tf_op jit(solution)/shard_map/attend/pallas_call | solution.py:76
  117.2 2.4 collective-permute-done.10.o2
  121.1 10.6 %collective-permute-done.13.x0 = bf16[144,512]{1,0:T(8,128)(2,1)S(1)} collective-permute-done((bf16[144,512]{1,0:T(8,128)(2,1)S(1)}, bf16[144,512]{1,0:T(8,128)(2,1)S(1)}, u32[]{:S(2)}, u32[]{:S(2)}) %collective-permute-start.13) | collective-permute-done | bytes 147488 | tf_op jit(solution)/shard_map/ppermute | solution.py:27
  134.6 16.0 %collective-permute-done.14.x1 = bf16[144,512]{1,0:T(8,128)(2,1)S(1)} collective-permute-done((bf16[144,512]{1,0:T(8,128)(2,1)S(1)}, bf16[144,512]{1,0:T(8,128)(2,1)S(1)}, u32[]{:S(2)}, u32[]{:S(2)}) %collective-permute-start.14) | collective-permute-done | bytes 147488 | tf_op jit(solution)/shard_map/ppermute | solution.py:27
  150.6 2.3 collective-permute-done.15.x2
  157.9 2.5 copy.90.go
  160.4 2.2 constant_dynamic-update-slice_fusion.5.wob
  168.6 4.5 mix.1
  173.3 13.4 %feed.1 = (bf16[512,1076]{1,0:T(8,128)(2,1)S(1)}, bf16[512,1076]{1,0:T(8,128)(2,1)S(1)}, bf16[512,1076]{1,0:T(8,128)(2,1)S(1)}, bf16[512,1076]{1,0:T(8,128)(2,1)S(1)}, bf16[1152,256]{1,0:T(8,128)(2,1)S(1)}) custom-call(bf16[512,1152]{1,0:T(8,128)(2,1)S(1)} %get-tuple-element.73.h2, bf16[512,1152]{1,0:T(8,128)(2,1)S(1)} %copy-done.9, ...), custom_call_target="tpu_custom_call" | custom-call | flops 7200000000 | bytes 36000000 | tf_op jit(solution)/shard_map/feed/pallas_call | solution.py:76
  188.2 1.9 convolution_convert_fusion
  190.2 3.6 feed_back.1.own
  193.8 8.2 %collective-permute-done.34.recv = bf16[1152,256]{1,0:T(8,128)(2,1)S(1)} collective-permute-done((bf16[1152,256]{1,0:T(8,128)(2,1)S(1)}, bf16[1152,256]{1,0:T(8,128)(2,1)S(1)}, u32[]{:S(2)}, u32[]{:S(2)}) %collective-permute-start.34) | collective-permute-done | bytes 589856 | tf_op jit(solution)/shard_map/ppermute | solution.py:27
  202.1 2.2 norm2_back.1
  206.4 3.1 convolution_convert_fusion.2
  210.2 15.0 %collective-permute-done.35.g10 = bf16[576,256]{1,0:T(8,128)(2,1)S(1)} collective-permute-done((bf16[576,256]{1,0:T(8,128)(2,1)S(1)}, bf16[576,256]{1,0:T(8,128)(2,1)S(1)}, u32[]{:S(2)}, u32[]{:S(2)}) %collective-permute-start.35) | collective-permute-done | bytes 294944 | tf_op jit(solution)/shard_map/ppermute | solution.py:27
  226.1 4.4 collective-permute-done.37.g11
  230.8 3.0 convolution_convert_fusion.5
  234.0 20.0 %attend_back.1.dqkv = bf16[480,2048]{1,0:T(8,128)(2,1)S(1)} custom-call(s32[2]{0:T(128)S(1)} %copy-done.35, s32[8]{0:T(128)S(1)} %copy-done.39, s32[8]{0:T(128)S(1)} %and_select_fusion.qhi, bf16[480,2048]{1,0:T(8,128)(2,1)S(1)} %copy-done.82, bf16[2048,512]{1,0:T(8,128)(2,1)S(1)} %copy-done.80, s32[1,2048]{1,0:T(1,128)S(1)} %bitcast.81, ...), custom_call_target="tpu_custom_call" | custom-call | flops 13200000000 | bytes 66000000 | tf_op jit(solution)/shard_map/attend_back/pallas_call | solution.py:76
  254.1 2.7 convolution_convert_fusion.4
  258.9 2.8 part.1
  261.7 1.6 fusion.1
  263.4 2.2 copy-done.87
  267.2 2.6 copy.98
  271.2 2.0 convolution_add_fusion
  275.9 3.4 fusion.3
  279.4 2.2 copy-done.88
  283.1 2.7 copy.96
  287.2 2.3 pad_maximum_fusion.4
  289.5 20.5 %collective-permute-done.50 = bf16[288,576]{1,0:T(8,128)(2,1)} collective-permute-done((bf16[288,576]{1,0:T(8,128)(2,1)}, bf16[288,576]{1,0:T(8,128)(2,1)}, u32[]{:S(2)}, u32[]{:S(2)}) %collective-permute-start.50) | collective-permute-done | bytes 331808 | tf_op jit(solution)/shard_map/ppermute | solution.py:35
  311.9 2.6 copy.99
  314.4 3.6 fusion.14
  318.0 20.1 %collective-permute-done.52 = bf16[576,1076]{1,0:T(8,128)(2,1)} collective-permute-done((bf16[576,1076]{1,0:T(8,128)(2,1)}, bf16[576,1076]{1,0:T(8,128)(2,1)}, u32[]{:S(2)}, u32[]{:S(2)}) %collective-permute-start.52) | collective-permute-done | bytes 1239584 | tf_op jit(solution)/shard_map/ppermute | solution.py:35
  338.1 2.7 copy.97
  340.8 3.6 fusion.10
  344.4 6.2 %fusion.5 = f32[1152,512]{1,0:T(8,128)S(1)} fusion(bf16[576,1076]{1,0:T(8,128)(2,1)} %collective-permute-done.25.dbs, bf16[576,1076]{1,0:T(8,128)(2,1)} %collective-permute-done.24.dba, bf16[576,1076]{1,0:T(8,128)(2,1)} %collective-permute-done.22.das, bf16[576,1076]{1,0:T(8,128)(2,1)} %bitcast.22.daa, bf16[512,1076]{1,0:T(8,128)(2,1)} %copy-done.76, ...), kind=kOutput, calls=%fused_computation.10 | convolution fusion | flops 2562842624 | bytes 9521152 | tf_op jit(solution)/shard_map/dot_general | solution.py:51
  358.4 9.9 %collective-permute-done.32 = bf16[1152,256]{1,0:T(8,128)(2,1)} collective-permute-done((bf16[1152,256]{1,0:T(8,128)(2,1)}, bf16[1152,256]{1,0:T(8,128)(2,1)}, u32[]{:S(2)}, u32[]{:S(2)}) %collective-permute-start.32) | collective-permute-done | bytes 589856 | tf_op jit(solution)/shard_map/ppermute | solution.py:27
  368.3 2.2 fusion.17
  371.0 4.1 spread.1
  379.7 29.9 %psum.54 = f32[1076]{0:T(1024)S(1)} all-reduce(f32[1076]{0:T(1024)S(1)} %add.125), channel_id=1, replica_groups=mesh['dp'=4,'tr'=4,'tc'=2] {'dp','tc'}, use_global_device_ids=true, to_apply=%region_15.16 | all-reduce | flops 1076 | bytes 8608 | tf_op jit(solution)/shard_map/psum | solution.py:575
  410.3 1.7 slice.177
  414.1 2.0 fusion.19
  422.5 1.7 collective-permute-start.43
  424.7 11.8 %psum.51 = f32[3,144]{1,0:T(4,128)S(1)} all-reduce(f32[3,144]{1,0:T(4,128)S(1)} %reshape.202), channel_id=1, replica_groups=mesh['dp'=4,'tr'=4,'tc'=2] {'dp'}, use_global_device_ids=true, to_apply=%region_10.11 | all-reduce | flops 432 | bytes 3456 | tf_op jit(solution)/shard_map/psum | solution.py:578
  445.2 2.2 norm1_stats.1
  448.1 1.7 copy.93
  451.2 59.8 %psum.49 = f32[576,6]{0,1:T(8,128)} all-reduce(f32[576,6]{0,1:T(8,128)} %pad_maximum_fusion.14), channel_id=1, replica_groups=mesh['dp'=4,'tr'=4,'tc'=2] {'dp','tr'}, use_global_device_ids=true, to_apply=%region_7.8 | all-reduce | flops 3456 | bytes 27648 | tf_op jit(solution)/shard_map/psum | solution.py:571
  513.3 2.0 norm1_back.1
  519.1 2.5 copy.100
  521.6 2.5 copy.101
  (455 shorter events, 102.8 us)
Async XLA Ops:
  7.3 508.1 %all-reduce.5.cloned.1.call-start = ((), (), s32[]{:S(2)}) async-start(), calls=%async_computation | async-start | bytes 8478720 | tf_op jit(solution)/shard_map/psum | solution.py:567
  7.3 16.7 %collective-permute-start = (bf16[576,512]{1,0:T(8,128)(2,1)}, bf16[576,512]{1,0:T(8,128)(2,1)}, u32[]{:S(2)}, u32[]{:S(2)}) collective-permute-start(bf16[576,512]{1,0:T(8,128)(2,1)} %bitcast.82), channel_id=1, source_target_pairs={{0,1},{1,0},{2,3},{3,2},{4,5},{5,4},{6,7},{7,6},{8,9},{9,8},{10,11... | collective-permute-start | bytes 1769480 | tf_op jit(solution)/shard_map/ppermute | solution.py:35
  10.3 41.3 %collective-permute-start.3 = (bf16[576,512]{1,0:T(8,128)(2,1)}, bf16[576,512]{1,0:T(8,128)(2,1)}, u32[]{:S(2)}, u32[]{:S(2)}) collective-permute-start(bf16[576,512]{1,0:T(8,128)(2,1)} %bitcast.83), channel_id=1, source_target_pairs={{0,4},{2,6},{4,0},{6,2},{1,5},{3,7},{5,1},{7,3},{8,12},{10,14},{12... | collective-permute-start | bytes 1769480 | tf_op jit(solution)/shard_map/ppermute | solution.py:27
  15.0 36.1 %collective-permute-start.17 = (bf16[288,576]{1,0:T(8,128)(2,1)}, bf16[288,576]{1,0:T(8,128)(2,1)}, u32[]{:S(2)}, u32[]{:S(2)}) collective-permute-start(bf16[288,576]{1,0:T(8,128)(2,1)} %pad_maximum_fusion.11), channel_id=1, source_target_pairs={{0,2},{2,0},{4,6},{6,4},{1,3},{3,1},{5,7},{7,5},{8,10},{10,8},{12,... | collective-permute-start | bytes 995336 | tf_op jit(solution)/shard_map/ppermute | solution.py:31
  15.0 24.2 %collective-permute-start.30 = (f32[538]{0:T(1024)S(1)}, f32[538]{0:T(1024)S(1)}, u32[]{:S(2)}, u32[]{:S(2)}) collective-permute-start(f32[538]{0:T(1024)S(1)} %copy-done.120), channel_id=1, source_target_pairs={{0,1},{1,0},{2,3},{3,2},{4,5},{5,4},{6,7},{7,6},{8,9},{9,8},{10,11... | collective-permute-start | bytes 6464 | tf_op jit(solution)/shard_map/ppermute | solution.py:35
  17.5 65.0 %copy-start.38 = (s32[8]{0:T(128)}, s32[8]{0:T(128)S(1)}, u32[]{:S(2)}) copy-start(s32[8]{0:T(128)S(1)} %get-tuple-element.245.klo.qlo) | copy-start | bytes 100
  24.0 13.8 %collective-permute-start.7 = (bf16[432,576]{1,0:T(8,128)(2,1)S(1)}, bf16[432,576]{1,0:T(8,128)(2,1)}, u32[]{:S(2)}, u32[]{:S(2)}) collective-permute-start(bf16[432,576]{1,0:T(8,128)(2,1)S(1)} %pad_maximum_fusion.10), channel_id=1, source_target_pairs={{0,1},{1,0},{2,3},{3,2},{4,5},{5,4},{6,7},{7,6},{8,9},{9,8},{10,11... | collective-permute-start | bytes 1493000 | tf_op jit(solution)/shard_map/ppermute | solution.py:35
  27.0 55.5 %copy-start.34 = (s32[2]{0:T(128)}, s32[2]{0:T(128)S(1)}, u32[]{:S(2)}) copy-start(s32[2]{0:T(128)S(1)} %pad_add_fusion.scal) | copy-start | bytes 28
  37.8 9.2 %collective-permute-start.19 = (bf16[288,576]{1,0:T(8,128)(2,1)}, bf16[288,576]{1,0:T(8,128)(2,1)S(1)}, u32[]{:S(2)}, u32[]{:S(2)}) collective-permute-start(bf16[288,576]{1,0:T(8,128)(2,1)} %pad_maximum_fusion.11), channel_id=1, source_target_pairs={{0,1},{1,0},{2,3},{3,2},{4,5},{5,4},{6,7},{7,6},{8,9},{9,8},{10,11... | collective-permute-start | bytes 995336 | tf_op jit(solution)/shard_map/ppermute | solution.py:35
  39.3 1.7 collective-permute-start.31
  39.3 16.1 %collective-permute-start.4 = (bf16[576,512]{1,0:T(8,128)(2,1)}, bf16[576,512]{1,0:T(8,128)(2,1)}, u32[]{:S(2)}, u32[]{:S(2)}) collective-permute-start(bf16[576,512]{1,0:T(8,128)(2,1)} %collective-permute-done.b00.b), channel_id=1, source_target_pairs={{0,4},{2,6},{4,0},{6,2},{1,5},{3,7},{5,1},{7,3},{8,12},{10,14},{12... | collective-permute-start | bytes 1769480 | tf_op jit(solution)/shard_map/ppermute | solution.py:27
  41.0 10.1 %collective-permute-start.8 = (f32[6,576]{1,0:T(8,128)}, f32[6,576]{1,0:T(8,128)S(1)}, u32[]{:S(2)}, u32[]{:S(2)}) collective-permute-start(f32[6,576]{1,0:T(8,128)} %stack.55), channel_id=1, source_target_pairs={{0,1},{1,0},{2,3},{3,2},{4,5},{5,4},{6,7},{7,6},{8,9},{9,8},{10,11... | collective-permute-start | bytes 41480 | tf_op jit(solution)/shard_map/ppermute | solution.py:35
  49.4 31.5 %collective-permute-start.23 = (bf16[576,1076]{1,0:T(8,128)(2,1)S(1)}, bf16[576,1076]{1,0:T(8,128)(2,1)S(1)}, u32[]{:S(2)}, u32[]{:S(2)}) collective-permute-start(bf16[576,1076]{1,0:T(8,128)(2,1)S(1)} %copy-done.3), channel_id=1, source_target_pairs={{0,1},{1,0},{2,3},{3,2},{4,5},{5,4},{6,7},{7,6},{8,9},{9,8},{10,11... | collective-permute-start | bytes 3718664 | tf_op jit(solution)/shard_map/ppermute | solution.py:35
  51.1 20.3 %collective-permute-start.1 = (bf16[576,512]{1,0:T(8,128)(2,1)}, bf16[576,512]{1,0:T(8,128)(2,1)}, u32[]{:S(2)}, u32[]{:S(2)}) collective-permute-start(bf16[576,512]{1,0:T(8,128)(2,1)} %bitcast.84), channel_id=1, source_target_pairs={{0,2},{2,0},{4,6},{6,4},{1,3},{3,1},{5,7},{7,5},{8,10},{10,8},{12,... | collective-permute-start | bytes 1769480 | tf_op jit(solution)/shard_map/ppermute | solution.py:31
  51.1 21.9 %collective-permute-start.2 = (bf16[576,512]{1,0:T(8,128)(2,1)}, bf16[576,512]{1,0:T(8,128)(2,1)}, u32[]{:S(2)}, u32[]{:S(2)}) collective-permute-start(bf16[576,512]{1,0:T(8,128)(2,1)} %collective-permute-done.b00.b), channel_id=1, source_target_pairs={{0,2},{2,0},{4,6},{6,4},{1,3},{3,1},{5,7},{7,5},{8,10},{10,8},{12,... | collective-permute-start | bytes 1769480 | tf_op jit(solution)/shard_map/ppermute | solution.py:31
  51.6 21.6 %collective-permute-start.5 = (bf16[576,512]{1,0:T(8,128)(2,1)}, bf16[576,512]{1,0:T(8,128)(2,1)}, u32[]{:S(2)}, u32[]{:S(2)}) collective-permute-start(bf16[576,512]{1,0:T(8,128)(2,1)} %collective-permute-done.3.a10), channel_id=1, source_target_pairs={{0,2},{2,0},{4,6},{6,4},{1,3},{3,1},{5,7},{7,5},{8,10},{10,8},{12,... | collective-permute-start | bytes 1769480 | tf_op jit(solution)/shard_map/ppermute | solution.py:31
  55.4 18.4 %collective-permute-start.6 = (bf16[576,512]{1,0:T(8,128)(2,1)}, bf16[576,512]{1,0:T(8,128)(2,1)}, u32[]{:S(2)}, u32[]{:S(2)}) collective-permute-start(bf16[576,512]{1,0:T(8,128)(2,1)} %collective-permute-done.4.b10), channel_id=1, source_target_pairs={{0,2},{2,0},{4,6},{6,4},{1,3},{3,1},{5,7},{7,5},{8,10},{10,8},{12,... | collective-permute-start | bytes 1769480 | tf_op jit(solution)/shard_map/ppermute | solution.py:31
  71.4 41.4 %collective-permute-start.18 = (bf16[576,576]{1,0:T(8,128)(2,1)S(1)}, bf16[576,576]{1,0:T(8,128)(2,1)S(1)}, u32[]{:S(2)}, u32[]{:S(2)}) collective-permute-start(bf16[576,576]{1,0:T(8,128)(2,1)S(1)} %pad_maximum_fusion.5), channel_id=1, source_target_pairs={{0,4},{2,6},{4,0},{6,2},{1,5},{3,7},{5,1},{7,3},{8,12},{10,14},{12... | collective-permute-start | bytes 1990664 | tf_op jit(solution)/shard_map/ppermute | solution.py:27
  73.0 39.2 %collective-permute-start.20 = (bf16[288,576]{1,0:T(8,128)(2,1)S(1)}, bf16[288,576]{1,0:T(8,128)(2,1)S(1)}, u32[]{:S(2)}, u32[]{:S(2)}) collective-permute-start(bf16[288,576]{1,0:T(8,128)(2,1)S(1)} %copy-done.114), channel_id=1, source_target_pairs={{0,2},{2,0},{4,6},{6,4},{1,3},{3,1},{5,7},{7,5},{8,10},{10,8},{12,... | collective-permute-start | bytes 995336 | tf_op jit(solution)/shard_map/ppermute | solution.py:31
  73.2 38.4 %collective-permute-start.26 = (bf16[576,256]{1,0:T(8,128)(2,1)S(1)}, bf16[576,256]{1,0:T(8,128)(2,1)S(1)}, u32[]{:S(2)}, u32[]{:S(2)}) collective-permute-start(bf16[576,256]{1,0:T(8,128)(2,1)S(1)} %copy-done.115), channel_id=1, source_target_pairs={{0,1},{1,0},{2,3},{3,2},{4,5},{5,4},{6,7},{7,6},{8,9},{9,8},{10,11... | collective-permute-start | bytes 884744 | tf_op jit(solution)/shard_map/ppermute | solution.py:35
  80.9 72.0 %copy-start.5 = (bf16[576,1076]{1,0:T(8,128)(2,1)}, bf16[576,1076]{1,0:T(8,128)(2,1)S(1)}, u32[]{:S(2)}) copy-start(bf16[576,1076]{1,0:T(8,128)(2,1)S(1)} %collective-permute-done.23.uba) | copy-start | bytes 3718660
  80.9 72.6 %collective-permute-start.24 = (bf16[576,1076]{1,0:T(8,128)(2,1)}, bf16[576,1076]{1,0:T(8,128)(2,1)}, u32[]{:S(2)}, u32[]{:S(2)}) collective-permute-start(bf16[576,1076]{1,0:T(8,128)(2,1)} %bitcast.22.daa), channel_id=1, source_target_pairs={{0,1},{1,0},{2,3},{3,2},{4,5},{5,4},{6,7},{7,6},{8,9},{9,8},{10,11... | collective-permute-start | bytes 3718664 | tf_op jit(solution)/shard_map/ppermute | solution.py:35
  111.6 1.9 collective-permute-start.11
  111.7 45.1 %copy-start.104 = (bf16[576,256]{1,0:T(8,128)(2,1)}, bf16[576,256]{1,0:T(8,128)(2,1)S(1)}, u32[]{:S(2)}) copy-start(bf16[576,256]{1,0:T(8,128)(2,1)S(1)} %collective-permute-done.26) | copy-start | bytes 884740
  111.7 3.2 collective-permute-start.9
  112.3 40.7 %collective-permute-start.27 = (bf16[1152,256]{1,0:T(8,128)(2,1)S(1)}, bf16[1152,256]{1,0:T(8,128)(2,1)S(1)}, u32[]{:S(2)}, u32[]{:S(2)}) collective-permute-start(bf16[1152,256]{1,0:T(8,128)(2,1)S(1)} %pad_maximum_fusion.8.go), channel_id=1, source_target_pairs={{0,4},{2,6},{4,0},{6,2},{1,5},{3,7},{5,1},{7,3},{8,12},{10,14},{12... | collective-permute-start | bytes 1769480 | tf_op jit(solution)/shard_map/ppermute | solution.py:27
  112.9 6.7 %collective-permute-start.10 = (bf16[144,512]{1,0:T(8,128)(2,1)S(1)}, bf16[144,512]{1,0:T(8,128)(2,1)S(1)}, u32[]{:S(2)}, u32[]{:S(2)}) collective-permute-start(bf16[144,512]{1,0:T(8,128)(2,1)S(1)} %get-tuple-element.65.o01), channel_id=1, source_target_pairs={{0,1},{1,0},{2,3},{3,2},{4,5},{5,4},{6,7},{7,6},{8,9},{9,8},{10,11... | collective-permute-start | bytes 442376 | tf_op jit(solution)/shard_map/ppermute | solution.py:35
  113.5 18.2 %collective-permute-start.13 = (bf16[144,512]{1,0:T(8,128)(2,1)S(1)}, bf16[144,512]{1,0:T(8,128)(2,1)S(1)}, u32[]{:S(2)}, u32[]{:S(2)}) collective-permute-start(bf16[144,512]{1,0:T(8,128)(2,1)S(1)} %get-tuple-element.63.o0.o00), channel_id=1, source_target_pairs={{0,4},{2,6},{4,0},{6,2},{1,5},{3,7},{5,1},{7,3},{8,12},{10,14},{12... | collective-permute-start | bytes 442376 | tf_op jit(solution)/shard_map/ppermute | solution.py:27
  114.9 17.3 %collective-permute-start.12 = (bf16[144,512]{1,0:T(8,128)(2,1)S(1)}, bf16[144,512]{1,0:T(8,128)(2,1)}, u32[]{:S(2)}, u32[]{:S(2)}) collective-permute-start(bf16[144,512]{1,0:T(8,128)(2,1)S(1)} %collective-permute-done.11), channel_id=1, source_target_pairs={{0,1},{1,0},{2,3},{3,2},{4,5},{5,4},{6,7},{7,6},{8,9},{9,8},{10,11... | collective-permute-start | bytes 442376 | tf_op jit(solution)/shard_map/ppermute | solution.py:35
  119.6 36.6 %collective-permute-start.21 = (bf16[576,576]{1,0:T(8,128)(2,1)S(1)}, bf16[576,576]{1,0:T(8,128)(2,1)}, u32[]{:S(2)}, u32[]{:S(2)}) collective-permute-start(bf16[576,576]{1,0:T(8,128)(2,1)S(1)} %pad_maximum_fusion.6), channel_id=1, source_target_pairs={{0,4},{2,6},{4,0},{6,2},{1,5},{3,7},{5,1},{7,3},{8,12},{10,14},{12... | collective-permute-start | bytes 1990664 | tf_op jit(solution)/shard_map/ppermute | solution.py:27
  131.7 19.0 %collective-permute-start.14 = (bf16[144,512]{1,0:T(8,128)(2,1)S(1)}, bf16[144,512]{1,0:T(8,128)(2,1)S(1)}, u32[]{:S(2)}, u32[]{:S(2)}) collective-permute-start(bf16[144,512]{1,0:T(8,128)(2,1)S(1)} %collective-permute-done.9.o1), channel_id=1, source_target_pairs={{0,4},{2,6},{4,0},{6,2},{1,5},{3,7},{5,1},{7,3},{8,12},{10,14},{12... | collective-permute-start | bytes 442376 | tf_op jit(solution)/shard_map/ppermute | solution.py:27
  132.2 20.7 %collective-permute-start.15 = (bf16[144,512]{1,0:T(8,128)(2,1)S(1)}, bf16[144,512]{1,0:T(8,128)(2,1)S(1)}, u32[]{:S(2)}, u32[]{:S(2)}) collective-permute-start(bf16[144,512]{1,0:T(8,128)(2,1)S(1)} %collective-permute-done.10.o2), channel_id=1, source_target_pairs={{0,4},{2,6},{4,0},{6,2},{1,5},{3,7},{5,1},{7,3},{8,12},{10,14},{12... | collective-permute-start | bytes 442376 | tf_op jit(solution)/shard_map/ppermute | solution.py:27
  150.6 22.5 %collective-permute-start.22 = (bf16[576,1076]{1,0:T(8,128)(2,1)}, bf16[576,1076]{1,0:T(8,128)(2,1)}, u32[]{:S(2)}, u32[]{:S(2)}) collective-permute-start(bf16[576,1076]{1,0:T(8,128)(2,1)} %bitcast.22.daa), channel_id=1, source_target_pairs={{0,2},{2,0},{4,6},{6,4},{1,3},{3,1},{5,7},{7,5},{8,10},{10,8},{12,... | collective-permute-start | bytes 3718664 | tf_op jit(solution)/shard_map/ppermute | solution.py:31
  152.9 20.2 %collective-permute-start.28 = (bf16[576,1076]{1,0:T(8,128)(2,1)S(1)}, bf16[576,1076]{1,0:T(8,128)(2,1)}, u32[]{:S(2)}, u32[]{:S(2)}) collective-permute-start(bf16[576,1076]{1,0:T(8,128)(2,1)S(1)} %copy-done.3), channel_id=1, source_target_pairs={{0,2},{2,0},{4,6},{6,4},{1,3},{3,1},{5,7},{7,5},{8,10},{10,8},{12,... | collective-permute-start | bytes 3718664 | tf_op jit(solution)/shard_map/ppermute | solution.py:31
  153.0 20.2 %collective-permute-start.29 = (bf16[576,1076]{1,0:T(8,128)(2,1)S(1)}, bf16[576,1076]{1,0:T(8,128)(2,1)}, u32[]{:S(2)}, u32[]{:S(2)}) collective-permute-start(bf16[576,1076]{1,0:T(8,128)(2,1)S(1)} %collective-permute-done.23.uba), channel_id=1, source_target_pairs={{0,2},{2,0},{4,6},{6,4},{1,3},{3,1},{5,7},{7,5},{8,10},{10,8},{12,... | collective-permute-start | bytes 3718664 | tf_op jit(solution)/shard_map/ppermute | solution.py:31
  153.5 19.6 %collective-permute-start.25 = (bf16[576,1076]{1,0:T(8,128)(2,1)}, bf16[576,1076]{1,0:T(8,128)(2,1)}, u32[]{:S(2)}, u32[]{:S(2)}) collective-permute-start(bf16[576,1076]{1,0:T(8,128)(2,1)} %collective-permute-done.24.dba), channel_id=1, source_target_pairs={{0,2},{2,0},{4,6},{6,4},{1,3},{3,1},{5,7},{7,5},{8,10},{10,8},{12,... | collective-permute-start | bytes 3718664 | tf_op jit(solution)/shard_map/ppermute | solution.py:31
  156.2 6.5 %collective-permute-start.16 = (bf16[144,512]{1,0:T(8,128)(2,1)}, bf16[144,512]{1,0:T(8,128)(2,1)}, u32[]{:S(2)}, u32[]{:S(2)}) collective-permute-start(bf16[144,512]{1,0:T(8,128)(2,1)} %collective-permute-done.12.o3), channel_id=1, source_target_pairs={{0,4},{2,6},{4,0},{6,2},{1,5},{3,7},{5,1},{7,3},{8,12},{10,14},{12... | collective-permute-start | bytes 442376 | tf_op jit(solution)/shard_map/ppermute | solution.py:27
  186.7 75.1 %copy-start.63 = (bf16[512,1076]{1,0:T(8,128)(2,1)}, bf16[512,1076]{1,0:T(8,128)(2,1)S(1)}, u32[]{:S(2)}) copy-start(bf16[512,1076]{1,0:T(8,128)(2,1)S(1)} %get-tuple-element.76) | copy-start | bytes 3305476
  186.7 15.4 %collective-permute-start.34 = (bf16[1152,256]{1,0:T(8,128)(2,1)S(1)}, bf16[1152,256]{1,0:T(8,128)(2,1)S(1)}, u32[]{:S(2)}, u32[]{:S(2)}) collective-permute-start(bf16[1152,256]{1,0:T(8,128)(2,1)S(1)} %get-tuple-element.82), channel_id=1, source_target_pairs={{0,4},{2,6},{4,0},{6,2},{1,5},{3,7},{5,1},{7,3},{8,12},{10,14},{12... | collective-permute-start | bytes 1769480 | tf_op jit(solution)/shard_map/ppermute | solution.py:27
  190.1 71.6 %collective-permute-start.54 = (bf16[1152,1076]{0,1:T(8,128)(2,1)S(1)}, bf16[1152,1076]{0,1:T(8,128)(2,1)S(1)}, u32[]{:S(2)}, u32[]{:S(2)}) collective-permute-start(bf16[1152,1076]{0,1:T(8,128)(2,1)S(1)} %convolution_convert_fusion), channel_id=1, source_target_pairs={{0,2},{2,0},{4,6},{6,4},{1,3},{3,1},{5,7},{7,5},{8,10},{10,8},{12,... | collective-permute-start | bytes 7437320 | tf_op jit(solution)/shard_map/ppermute | solution.py:31
  204.3 152.1 %copy-start.11 = (f32[1152,3]{1,0:T(8,128)}, f32[1152,3]{1,0:T(8,128)S(1)}, u32[]{:S(2)}) copy-start(f32[1152,3]{1,0:T(8,128)S(1)} %get-tuple-element.100) | copy-start | bytes 41476
  204.4 26.3 %collective-permute-start.48 = (bf16[1152,256]{1,0:T(8,128)(2,1)S(1)}, bf16[1152,256]{1,0:T(8,128)(2,1)S(1)}, u32[]{:S(2)}, u32[]{:S(2)}) collective-permute-start(bf16[1152,256]{1,0:T(8,128)(2,1)S(1)} %get-tuple-element.98), channel_id=1, source_target_pairs={{0,4},{2,6},{4,0},{6,2},{1,5},{3,7},{5,1},{7,3},{8,12},{10,14},{12... | collective-permute-start | bytes 1769480 | tf_op jit(solution)/shard_map/ppermute | solution.py:27
  205.9 19.3 %collective-permute-start.35 = (bf16[576,256]{1,0:T(8,128)(2,1)S(1)}, bf16[576,256]{1,0:T(8,128)(2,1)S(1)}, u32[]{:S(2)}, u32[]{:S(2)}) collective-permute-start(bf16[576,256]{1,0:T(8,128)(2,1)S(1)} %get-tuple-element.84), channel_id=1, source_target_pairs={{0,4},{2,6},{4,0},{6,2},{1,5},{3,7},{5,1},{7,3},{8,12},{10,14},{12... | collective-permute-start | bytes 884744 | tf_op jit(solution)/shard_map/ppermute | solution.py:27
  209.6 66.3 %collective-permute-start.51 = (bf16[1152,1076]{0,1:T(8,128)(2,1)}, bf16[1152,1076]{0,1:T(8,128)(2,1)}, u32[]{:S(2)}, u32[]{:S(2)}) collective-permute-start(bf16[1152,1076]{0,1:T(8,128)(2,1)} %convolution_convert_fusion.2), channel_id=1, source_target_pairs={{0,2},{2,0},{4,6},{6,4},{1,3},{3,1},{5,7},{7,5},{8,10},{10,8},{12,... | collective-permute-start | bytes 7437320 | tf_op jit(solution)/shard_map/ppermute | solution.py:31
  209.6 16.5 %collective-permute-start.36 = (bf16[288,256]{1,0:T(8,128)(2,1)S(1)}, bf16[288,256]{1,0:T(8,128)(2,1)S(1)}, u32[]{:S(2)}, u32[]{:S(2)}) collective-permute-start(bf16[288,256]{1,0:T(8,128)(2,1)S(1)} %get-tuple-element.85), channel_id=1, source_target_pairs={{0,1},{1,0},{2,3},{3,2},{4,5},{5,4},{6,7},{7,6},{8,9},{9,8},{10,11... | collective-permute-start | bytes 442376 | tf_op jit(solution)/shard_map/ppermute | solution.py:35
  225.3 5.2 collective-permute-start.37
  230.6 3.3 collective-permute-start.38
  233.8 37.4 %collective-permute-start.49 = (bf16[288,1152]{1,0:T(8,128)(2,1)}, bf16[288,1152]{1,0:T(8,128)(2,1)}, u32[]{:S(2)}, u32[]{:S(2)}) collective-permute-start(bf16[288,1152]{1,0:T(8,128)(2,1)} %convolution_convert_fusion.5), channel_id=1, source_target_pairs={{0,2},{2,0},{4,6},{6,4},{1,3},{3,1},{5,7},{7,5},{8,10},{10,8},{12,... | collective-permute-start | bytes 1990664 | tf_op jit(solution)/shard_map/ppermute | solution.py:31
  258.2 29.0 %collective-permute-start.47 = (bf16[3,144,576]{2,1,0:T(8,128)(2,1)}, bf16[3,144,576]{2,1,0:T(8,128)(2,1)}, u32[]{:S(2)}, u32[]{:S(2)}) collective-permute-start(bf16[3,144,576]{2,1,0:T(8,128)(2,1)} %get-tuple-element.211), channel_id=1, source_target_pairs={{0,1},{1,0},{2,3},{3,2},{4,5},{5,4},{6,7},{7,6},{8,9},{9,8},{10,11... | collective-permute-start | bytes 1493000 | tf_op jit(solution)/shard_map/ppermute | solution.py:35
  261.7 108.8 %collective-permute-start.39 = (bf16[1152,1024]{1,0:T(8,128)(2,1)}, bf16[1152,1024]{1,0:T(8,128)(2,1)}, u32[]{:S(2)}, u32[]{:S(2)}) collective-permute-start(bf16[1152,1024]{1,0:T(8,128)(2,1)} %part.1), channel_id=1, source_target_pairs={{0,2},{2,0},{4,6},{6,4},{1,3},{3,1},{5,7},{7,5},{8,10},{10,8},{12,... | collective-permute-start | bytes 7077896 | tf_op jit(solution)/shard_map/ppermute | solution.py:31
  269.8 42.0 %collective-permute-start.55 = (bf16[576,1076]{1,0:T(8,128)(2,1)}, bf16[576,1076]{1,0:T(8,128)(2,1)}, u32[]{:S(2)}, u32[]{:S(2)}) collective-permute-start(bf16[576,1076]{1,0:T(8,128)(2,1)} %copy.98), channel_id=1, source_target_pairs={{0,1},{1,0},{2,3},{3,2},{4,5},{5,4},{6,7},{7,6},{8,9},{9,8},{10,11... | collective-permute-start | bytes 3718664 | tf_op jit(solution)/shard_map/ppermute | solution.py:35
  275.2 34.8 %collective-permute-start.50 = (bf16[288,576]{1,0:T(8,128)(2,1)}, bf16[288,576]{1,0:T(8,128)(2,1)}, u32[]{:S(2)}, u32[]{:S(2)}) collective-permute-start(bf16[288,576]{1,0:T(8,128)(2,1)} %slice.278), channel_id=1, source_target_pairs={{0,1},{1,0},{2,3},{3,2},{4,5},{5,4},{6,7},{7,6},{8,9},{9,8},{10,11... | collective-permute-start | bytes 995336 | tf_op jit(solution)/shard_map/ppermute | solution.py:35
  285.8 52.3 %collective-permute-start.52 = (bf16[576,1076]{1,0:T(8,128)(2,1)}, bf16[576,1076]{1,0:T(8,128)(2,1)}, u32[]{:S(2)}, u32[]{:S(2)}) collective-permute-start(bf16[576,1076]{1,0:T(8,128)(2,1)} %copy.96), channel_id=1, source_target_pairs={{0,1},{1,0},{2,3},{3,2},{4,5},{5,4},{6,7},{7,6},{8,9},{9,8},{10,11... | collective-permute-start | bytes 3718664 | tf_op jit(solution)/shard_map/ppermute | solution.py:35
  352.9 15.3 %collective-permute-start.32 = (bf16[1152,256]{1,0:T(8,128)(2,1)}, bf16[1152,256]{1,0:T(8,128)(2,1)}, u32[]{:S(2)}, u32[]{:S(2)}) collective-permute-start(bf16[1152,256]{1,0:T(8,128)(2,1)} %slice.277), channel_id=1, source_target_pairs={{0,4},{2,6},{4,0},{6,2},{1,5},{3,7},{5,1},{7,3},{8,12},{10,14},{12... | collective-permute-start | bytes 1769480 | tf_op jit(solution)/shard_map/ppermute | solution.py:27
  356.4 23.4 %collective-permute-start.53 = (f32[1076]{0:T(1024)S(1)}, f32[1076]{0:T(1024)S(1)}, u32[]{:S(2)}, u32[]{:S(2)}) collective-permute-start(f32[1076]{0:T(1024)S(1)} %convert_reduce_fusion.1), channel_id=1, source_target_pairs={{0,2},{2,0},{4,6},{6,4},{1,3},{3,1},{5,7},{7,5},{8,10},{10,8},{12,... | collective-permute-start | bytes 12920 | tf_op jit(solution)/shard_map/ppermute | solution.py:31
  357.2 55.1 %collective-permute-start.46 = (f32[576,3]{1,0:T(8,128)}, f32[576,3]{1,0:T(8,128)}, u32[]{:S(2)}, u32[]{:S(2)}) collective-permute-start(f32[576,3]{1,0:T(8,128)} %slice.179), channel_id=1, source_target_pairs={{0,1},{1,0},{2,3},{3,2},{4,5},{5,4},{6,7},{7,6},{8,9},{9,8},{10,11... | collective-permute-start | bytes 20744 | tf_op jit(solution)/shard_map/ppermute | solution.py:35
  375.1 41.0 %collective-permute-start.40 = (bf16[1152,256]{1,0:T(8,128)(2,1)}, bf16[1152,256]{1,0:T(8,128)(2,1)}, u32[]{:S(2)}, u32[]{:S(2)}) collective-permute-start(bf16[1152,256]{1,0:T(8,128)(2,1)} %get-tuple-element.88), channel_id=1, source_target_pairs={{0,4},{2,6},{4,0},{6,2},{1,5},{3,7},{5,1},{7,3},{8,12},{10,14},{12... | collective-permute-start | bytes 1769480 | tf_op jit(solution)/shard_map/ppermute | solution.py:27
  376.7 39.4 %collective-permute-start.41 = (bf16[576,512]{1,0:T(8,128)(2,1)}, bf16[576,512]{1,0:T(8,128)(2,1)}, u32[]{:S(2)}, u32[]{:S(2)}) collective-permute-start(bf16[576,512]{1,0:T(8,128)(2,1)} %get-tuple-element.89), channel_id=1, source_target_pairs={{0,1},{1,0},{2,3},{3,2},{4,5},{5,4},{6,7},{7,6},{8,9},{9,8},{10,11... | collective-permute-start | bytes 1769480 | tf_op jit(solution)/shard_map/ppermute | solution.py:35
  378.5 35.6 %collective-permute-start.33 = (bf16[576,256]{1,0:T(8,128)(2,1)}, bf16[576,256]{1,0:T(8,128)(2,1)}, u32[]{:S(2)}, u32[]{:S(2)}) collective-permute-start(bf16[576,256]{1,0:T(8,128)(2,1)} %get-tuple-element.215), channel_id=1, source_target_pairs={{0,1},{1,0},{2,3},{3,2},{4,5},{5,4},{6,7},{7,6},{8,9},{9,8},{10,11... | collective-permute-start | bytes 884744 | tf_op jit(solution)/shard_map/ppermute | solution.py:35
  412.0 100.6 %collective-permute-start.45 = (bf16[576,256]{1,0:T(8,128)(2,1)}, bf16[576,256]{1,0:T(8,128)(2,1)}, u32[]{:S(2)}, u32[]{:S(2)}) collective-permute-start(bf16[576,256]{1,0:T(8,128)(2,1)} %slice.177), channel_id=1, source_target_pairs={{0,1},{1,0},{2,3},{3,2},{4,5},{5,4},{6,7},{7,6},{8,9},{9,8},{10,11... | collective-permute-start | bytes 884744 | tf_op jit(solution)/shard_map/ppermute | solution.py:35
  421.8 15.2 %collective-permute-start.42 = (bf16[576,256]{1,0:T(8,128)(2,1)S(1)}, bf16[576,256]{1,0:T(8,128)(2,1)S(1)}, u32[]{:S(2)}, u32[]{:S(2)}) collective-permute-start(bf16[576,256]{1,0:T(8,128)(2,1)S(1)} %get-tuple-element.92), channel_id=1, source_target_pairs={{0,4},{2,6},{4,0},{6,2},{1,5},{3,7},{5,1},{7,3},{8,12},{10,14},{12... | collective-permute-start | bytes 884744 | tf_op jit(solution)/shard_map/ppermute | solution.py:27
  422.5 15.3 %collective-permute-start.43 = (bf16[576,256]{1,0:T(8,128)(2,1)S(1)}, bf16[576,256]{1,0:T(8,128)(2,1)S(1)}, u32[]{:S(2)}, u32[]{:S(2)}) collective-permute-start(bf16[576,256]{1,0:T(8,128)(2,1)S(1)} %get-tuple-element.93), channel_id=1, source_target_pairs={{0,1},{1,0},{2,3},{3,2},{4,5},{5,4},{6,7},{7,6},{8,9},{9,8},{10,11... | collective-permute-start | bytes 884744 | tf_op jit(solution)/shard_map/ppermute | solution.py:35
  445.2 67.4 %copy-start.8 = (f32[1152,256]{1,0:T(8,128)S(1)}, f32[1152,256]{1,0:T(8,128)}, u32[]{:S(2)}) copy-start(f32[1152,256]{1,0:T(8,128)} %copy-done.7) | copy-start | bytes 3538948
  449.8 62.8 %collective-permute-start.44 = (f32[8,512]{1,0:T(8,128)S(1)}, f32[8,512]{1,0:T(8,128)}, u32[]{:S(2)}, u32[]{:S(2)}) collective-permute-start(f32[8,512]{1,0:T(8,128)S(1)} %get-tuple-element.96.stats), channel_id=1, source_target_pairs={{0,1},{1,0},{2,3},{3,2},{4,5},{5,4},{6,7},{7,6},{8,9},{9,8},{10,11... | collective-permute-start | bytes 49160 | tf_op jit(solution)/shard_map/ppermute | solution.py:35
  (125 other events, 1086.8 us)
Sparse Core Ops, SparseCore 0:
  344.5 158.5 all-reduce.4

commit v3 on v2

v3 whole, which is shorter than its diff:
```python
import jax
import jax.numpy as jnp
from jax import lax
from jax.experimental import pallas as pl
from jax.experimental.pallas import tpu as pltpu
from jax.sharding import PartitionSpec as P

DH = 72
PITCH = 80
SUB = 256
EPSILON = 1e-06
GELU_C = 0.7978845608028654
GELU_A = 0.044715
MASKED = -1e30
SCALE = DH**-0.5
SCALE2 = SCALE * 1.4426950408889634
BF = jnp.bfloat16
F32 = jnp.float32
MIB = 1024 * 1024


def swap_perm(axis, bit):
    return [(i, i ^ bit) for i in range(lax.axis_size(axis))]


def px(v):
    return lax.ppermute(v, "tr", swap_perm("tr", 2))


def pc(v):
    return lax.ppermute(v, "tr", swap_perm("tr", 1))


def py(v):
    return lax.ppermute(v, "tc", swap_perm("tc", 1))


def phase(*values):
    return lax.optimization_barrier(values)


def after(v, *earlier):
    return phase(v, *earlier)[0]


def dot(a, b):
    return jnp.dot(a, b, preferred_element_type=F32)


def dot_tn(a, b):
    return lax.dot_general(a, b, (((0,), (0,)), ((), ())), preferred_element_type=F32)


def dot_nt(a, b):
    return lax.dot_general(a, b, (((1,), (1,)), ((), ())), preferred_element_type=F32)


def rows_at(v, first, count):
    return lax.dynamic_slice_in_dim(v, first, count, 0)


def cols_at(v, first, count):
    return lax.dynamic_slice_in_dim(v, first, count, 1)


def dp_swap(v, bit):
    return lax.ppermute(v, "dp", swap_perm("dp", bit))


def line(step, v):
    if lax.axis_size("dp") != 4:
        return v
    return lax.ppermute(v, "dp", ([(0, 1), (3, 2)], [(1, 2), (2, 1)], [(1, 0), (2, 3)])[step])


def line_sum(v, received):
    if lax.axis_size("dp") != 4:
        return v
    return (v.astype(F32) + received.astype(F32)).astype(BF)


def line_end(v, received):
    if lax.axis_size("dp") != 4:
        return lax.psum(v, "dp").astype(F32)
    place = lax.axis_index("dp")
    return jnp.where((place == 1) | (place == 2), v, received).astype(F32)


def dp_step(v, bit):
    return dp_swap(v, bit) if lax.axis_size("dp") == 4 else jnp.zeros_like(v)


def dp_last(v):
    return v if lax.axis_size("dp") == 4 else lax.psum(v, "dp")


VM = pl.BlockSpec(memory_space=pltpu.VMEM)
SM = pl.BlockSpec(memory_space=pltpu.SMEM)


def shape(*dims, dtype=BF):
    return jax.ShapeDtypeStruct(dims, dtype)


ANY = pl.BlockSpec(memory_space=pl.ANY)


def call(body, name, scalars, arrays, outs, us, scratch=(), vmem=14, far=()):
    return pl.pallas_call(
        body,
        out_shape=tuple(outs),
        in_specs=[SM] * len(scalars) + [VM] * len(arrays) + [ANY] * len(far),
        out_specs=tuple([VM] * len(outs)),
        scratch_shapes=list(scratch),
        compiler_params=pltpu.CompilerParams(vmem_limit_bytes=vmem * MIB),
        cost_estimate=pl.CostEstimate(
            flops=int(us * 600e6), bytes_accessed=int(us * 3e6), transcendentals=0
        ),
        name=name,
    )(*scalars, *arrays, *far)


def spots():
    return [(rc, ry, rx) for rc in range(2) for ry in range(2) for rx in range(2)]


def block_of(me, rc, ry, rx):
    return me ^ (rx * 4 + rc * 2 + ry)


def span(block):
    return pl.ds(pl.multiple_of(block * SUB, SUB), SUB)


def head_rows(pos):
    return pl.ds(pl.multiple_of(pos * 2 * DH, 16), 2 * DH)


def row_of(col):
    return jnp.broadcast_to(col, (col.shape[0], 128)).T[0:1]


def column(i, *parts):
    return jnp.concatenate([p[...].T[:, i : i + 1] for p in parts], 0)


def pack_kernel(scal, q, k, v, out):
    rows = head_rows(1 - scal[0])
    for i, w in enumerate((q, k, v)):
        out[2 * DH * i : 2 * DH * (i + 1), :] = w[rows, :]


def unpack_kernel(scal, q, k, v, other, wt, w):
    rows = head_rows(scal[0])
    parts = []
    for i, own in enumerate((q, k, v)):
        there = slice(2 * DH * i, 2 * DH * (i + 1))
        both = jnp.concatenate((own[rows, :].astype(F32), other[there, :].astype(F32)), 1)
        gap = jnp.zeros((PITCH - DH, both.shape[1]), F32)
        parts += [both[:DH], gap, both[DH:], gap]
    whole = jnp.concatenate(parts, 0).astype(BF)
    wt[...] = whole
    w[...] = whole.T


def norm_qkv_kernel(
    scal, a00, b00, a01, b01, a10, b10, a11, b11, weights, bias, small, small_y,
    h_ref, qkv_ref, kv_ref, res_ref, gain_s, shift_s, bias_s,
):
    ypos, me = scal[0], scal[1]
    half = a00.shape[0]
    gain_s[...] = jnp.broadcast_to(column(0, small, small_y), gain_s.shape)
    shift_s[...] = jnp.broadcast_to(column(1, small, small_y), shift_s.shape)
    bias_s[...] = jnp.broadcast_to(column(0, bias), bias_s.shape)
    sources = {(0, 0): (a00, b00), (1, 0): (a01, b01), (0, 1): (a10, b10), (1, 1): (a11, b11)}
    for p, (rc, ry, rx) in enumerate(spots()):
        here = slice(p * SUB, (p + 1) * SUB)
        there = span(block_of(me, rc, ry, rx))
        cols = span(ypos ^ ry)
        sa, sb = sources[(rc, rx)]
        raw = jnp.concatenate((sa[:, cols], sb[:, cols]), 0)
        if rc == 0 and ry == 0:
            res_ref[:, rx * SUB : (rx + 1) * SUB] = raw
        v = raw.astype(F32)
        mean = jnp.sum(v, axis=0, keepdims=True) / (2 * half)
        square = jnp.sum(v * v, axis=0, keepdims=True) / (2 * half)
        root = lax.rsqrt(square - mean * mean + EPSILON)
        hidden = ((v - mean) * root * gain_s[...] + shift_s[...]).astype(BF)
        h_ref[:, here] = hidden
        qkv = (dot(weights[...], hidden) + bias_s[...]).astype(BF)
        qkv_ref[:, there] = qkv
        for i in range(4):
            kv_ref[there, 128 * i : 128 * i + PITCH] = qkv[PITCH * (2 + i) : PITCH * (3 + i), :].T


def attend_kernel(scal, klo, khi, qkv, kv, lo, hi, o0, o1, lse, s_ref, acc_ref):
    me = scal[1]
    outs = (o0, o1)
    places = lax.broadcasted_iota(jnp.int32, (SUB, SUB), 0)
    lanes = lax.broadcasted_iota(jnp.int32, (1, SUB), 1)
    for rc, ry, rx in sorted(spots(), reverse=True):
        block = block_of(me, rc, ry, rx)
        cols = span(block)
        low, high = lo[:, cols], hi[:, cols]
        own = lanes + block * SUB

        def score(kb, tops):
            base = kb * SUB
            allowed = ((places >= low - base) & (places < high - base)) | (places == own - base)
            new = []
            for h in range(2):
                s = dot(kv[span(kb), 128 * h : 128 * h + PITCH], qkv[PITCH * h : PITCH * (h + 1), cols])
                s = jnp.where(allowed, s, MASKED)
                s_ref[h, span(kb), :] = s
                new.append(jnp.maximum(tops[h], jnp.max(s.reshape(SUB // 8, 8, SUB), axis=0)))
            return tuple(new)

        start = jnp.full((8, SUB), MASKED, F32)
        tops = lax.fori_loop(klo[block], khi[block], score, (start, start))
        tops = [jnp.max(t, axis=0, keepdims=True) * SCALE2 for t in tops]
        acc_ref[...] = jnp.zeros_like(acc_ref)

        def weigh(kb, carry):
            for h in range(2):
                weights = jnp.exp2(s_ref[h, span(kb), :] * SCALE2 - tops[h]).astype(BF)
                acc_ref[h] += dot(qkv[PITCH * (4 + h) : PITCH * (5 + h), span(kb)], weights)
            return carry

        lax.fori_loop(klo[block], khi[block], weigh, 0)
        heads = []
        for h in range(2):
            total = acc_ref[h, DH : DH + 1, :]
            heads.append(acc_ref[h, :DH, :] / total)
            lse[h : h + 1, cols] = tops[h] + jnp.log2(total)
        rows = slice(rc * 2 * DH, (rc + 1) * 2 * DH)
        outs[ry][rows, rx * SUB : (rx + 1) * SUB] = jnp.concatenate(heads, 0).astype(BF)


def attend_back_kernel(
    scal, qlo, qhi, qkv, kv, lo, hi, lse, o0, o1, g0, gx, gy, gxy, s0, sx, sy, sxy,
    out, gt, delta, dqt, dk, dv,
):
    me = scal[1]
    outs = (o0, o1)
    n2 = 2 * DH
    grads = (g0, gx, gy, gxy, s0, sx, sy, sxy)
    for p, (rc, ry, rx) in enumerate(spots()):
        cols = span(block_of(me, rc, ry, rx))
        rows = slice(rc * n2, (rc + 1) * n2)
        gtile = (grads[p][...] if p in (0, 4) else grads[p][rows, :]).astype(F32)
        both = gtile * outs[ry][rows, rx * SUB : (rx + 1) * SUB].astype(F32)
        for h in range(2):
            part = slice(DH * h, DH * (h + 1))
            padded = jnp.concatenate((gtile[part], jnp.zeros((PITCH - DH, SUB), F32)), 0)
            gt[PITCH * h : PITCH * (h + 1), cols] = padded.astype(BF)
            delta[h : h + 1, cols] = jnp.sum(both[part], axis=0, keepdims=True)
    dqt[...] = jnp.zeros_like(dqt)
    dk[...] = jnp.zeros_like(dk)
    dv[...] = jnp.zeros_like(dv)
    places = lax.broadcasted_iota(jnp.int32, (SUB, SUB), 0)
    lanes = lax.broadcasted_iota(jnp.int32, (1, SUB), 1)

    @pl.loop(0, 8)
    def _(kb):
        keys = span(kb)
        base = kb * SUB

        def body(qb, carry):
            cols = span(qb)
            low, high = lo[:, cols] - base, hi[:, cols] - base
            own = lanes + (qb * SUB - base)
            allowed = ((places >= low) & (places < high)) | (places == own)
            for h in range(2):
                head = slice(PITCH * h, PITCH * (h + 1))
                s = dot(kv[keys, 128 * h : 128 * h + PITCH], qkv[head, cols])
                probs = jnp.where(allowed, jnp.exp2(s * SCALE2 - lse[h : h + 1, cols]), 0.0)
                gprobs = dot(kv[keys, 256 + 128 * h : 256 + 128 * h + PITCH], gt[head, cols])
                gscores = (probs * (gprobs - delta[h : h + 1, cols])).astype(BF)
                dv[h, keys, :] += dot_nt(probs.astype(BF), gt[head, cols])
                dk[h, keys, :] += dot_nt(gscores, qkv[head, cols])
                dqt[head, cols] += dot(qkv[PITCH * (2 + h) : PITCH * (3 + h), keys], gscores)
            return carry

        lax.fori_loop(qlo[kb], qhi[kb], body, 0)

    for p, (rc, ry, rx) in enumerate(spots()):
        here = slice(p * SUB, (p + 1) * SUB)
        rows = span(block_of(me, rc, ry, rx))
        out[: 2 * PITCH, here] = (dqt[:, rows] * SCALE).astype(BF)
        for h in range(2):
            out[PITCH * (2 + h) : PITCH * (3 + h), here] = (dk[h, rows, :].T * SCALE).astype(BF)
            out[PITCH * (4 + h) : PITCH * (5 + h), here] = dv[h, rows, :].T.astype(BF)


def own_and_y(ypos, w):
    return [w[head_rows(ypos), :], w[head_rows(1 - ypos), :]]


def out_weights_kernel(scal, own_a, own_b, x_a, x_b, w):
    parts = []
    for a, b in ((own_a, own_b), (x_a, x_b)):
        for wa, wb in zip(own_and_y(scal[0], a), own_and_y(scal[0], b)):
            parts.append(jnp.concatenate((wa, wb), 1))
    w[...] = jnp.concatenate(parts, 0)


def mix_kernel(own, y, x, xy, sib, ysib, xsib, xysib, w, w_sib, res, small, small_y, mixed, h2t, h2):
    n2 = 2 * DH
    gain, shift, bias = [column(i, small, small_y) for i in (2, 3, 4)]
    parts = []
    for rows, group in ((slice(0, n2), (own, y, x, xy)), (slice(n2, 2 * n2), (sib, ysib, xsib, xysib))):
        for i, o in enumerate(group):
            if i < 2:
                parts.append(o[rows, :])
            else:
                parts.append(jnp.concatenate((o[rows, SUB:], o[rows, :SUB]), 1))
    att = jnp.concatenate(parts, 0)
    weights = jnp.concatenate((w[...], w_sib[...]), 0)
    v = res[...].astype(F32) + dot_tn(weights, att) + bias
    mixed[...] = v
    mean = jnp.mean(v, axis=0, keepdims=True)
    root = lax.rsqrt(jnp.mean(v * v, axis=0, keepdims=True) - mean * mean + EPSILON)
    hidden = ((v - mean) * root * gain + shift).astype(BF)
    h2t[...] = hidden
    h2[...] = hidden.T


def turn_kernel(oa, ob, xa, xb, gof, go):
    half = oa.shape[0]
    for rx, (a, b) in enumerate(((oa, ob), (xa, xb))):
        here = slice(rx * SUB, (rx + 1) * SUB)
        gof[:half, here] = a[...]
        gof[half:, here] = b[...]
        go[here, :] = jnp.concatenate((a[...], b[...]), 0).T


def gelu_both(u):
    square = u * u
    tangent = jnp.tanh(GELU_C * (u + GELU_A * square * u))
    plus = 0.5 * (1.0 + tangent)
    slope = plus + 0.5 * u * (1.0 - tangent * tangent) * GELU_C * (1.0 + 3.0 * GELU_A * square)
    return u * plus, slope


def fetch(sources, buffers, sems):
    half = sources[0].shape[0]
    copies = []
    for i, src in enumerate(sources):
        dst = buffers[i // 2].at[pl.ds((i % 2) * half, half), :]
        copies.append(pltpu.make_async_copy(src, dst, sems.at[i]))
        copies[-1].start()
    return copies


def feed_half(h2, go, bias, u, d, copies, act, gu, sums):
    for c in copies[:2]:
        c.wait()
    upper = dot(h2[...], u[...]) + bias
    value, slope = gelu_both(upper)
    act[...] = value.astype(BF)
    for c in copies[2:]:
        c.wait()
    rounded = (dot(go[...], d[...]) * slope).astype(BF)
    gu[...] = rounded
    sums[...] = jnp.broadcast_to(jnp.sum(rounded.astype(F32), axis=0, keepdims=True), sums.shape)
    return dot_nt(u[...], gu[...])


def feed_own_kernel(h2, go, bias, ua, ub, da, db, act, gu, sums, part, u, d, sems):
    copies = fetch((ua, ub, da, db), (u, d), sems)
    part[...] = feed_half(h2, go, bias[0:1, :], u, d, copies, act, gu, sums)


def feed_sib_kernel(h2, go, bias, part, ua, ub, da, db, act, gu, sums, send, own, u, d, sems):
    copies = fetch((ua, ub, da, db), (u, d), sems)
    total = feed_half(h2, go, bias[1:2, :], u, d, copies, act, gu, sums) + part[...]
    send[...] = total[:, SUB:].astype(BF)
    own[...] = total[:, :SUB]


def padded_units(v, width):
    return jnp.concatenate((v, jnp.zeros((v.shape[0], width - v.shape[1]), v.dtype)), 1)


def outers_kernel(gof, act, h2t, gu, sums, down, up):
    width, rows = down.shape[1], h2t.shape[0]
    down[...] = padded_units(dot(gof[...], act[...]).astype(BF), width)
    up[:rows, :] = padded_units(dot(h2t[...], gu[...]).astype(BF), width)
    up[rows:, :] = padded_units(jnp.concatenate((sums[...], sums[...]), 0).astype(BF), width)


def down_own_kernel(gof, act, recv, keep, send):
    half, width = keep.shape
    total = padded_units(dot(gof[...], act[...]), width) + recv[...].astype(F32)
    keep[...] = total[:half]
    send[...] = total[half:].astype(BF)


def up_own_kernel(h2t, gu, sums, recv, keep, send):
    half = h2t.shape[0] // 2
    width = keep.shape[1]
    total = padded_units(dot(h2t[...], gu[...]), width) + recv[: 2 * half, :].astype(F32)
    more = padded_units(jnp.concatenate((sums[...], sums[...]), 0), width) + recv[2 * half :, :].astype(F32)
    keep[:half, :] = total[:half]
    keep[half:, :] = more
    send[:half, :] = total[half:].astype(BF)
    send[half:, :] = more.astype(BF)


def result_kernel(act0, act1, mixed, small, small_y, daa, dba, das, dbs, send, own, d0, d1, sems):
    copies = fetch((daa, dba, das, dbs), (d0, d1), sems)
    for c in copies:
        c.wait()
    part = dot_nt(d0[...], act0[...]) + dot_nt(d1[...], act1[...])
    send[...] = part[:, SUB:].astype(BF)
    own[...] = part[:, :SUB] + mixed[:, :SUB] + column(5, small, small_y)


def result_sum_kernel(own, recv, out_a, out_b):
    half = out_a.shape[0]
    total = (own[...] + recv[...].astype(F32)).astype(BF)
    out_a[...] = total[:half]
    out_b[...] = total[half:]


def place_kernel(scal, own, other, out):
    out[:, span(scal[0])] = own[...]
    out[:, span(1 - scal[0])] = other[...]


def norm2_back_kernel(
    own, recv, mixed, goa, gob, small, small_y, w, w_sib, gm, low, low_b, g_own, g_sib, g_y, g_x, g_xy, sums
):
    e = own[...] + recv[...].astype(F32)
    v = mixed[:, :SUB]
    mean = jnp.mean(v, axis=0, keepdims=True)
    root = lax.rsqrt(jnp.mean(v * v, axis=0, keepdims=True) - mean * mean + EPSILON)
    n = (v - mean) * root
    weighted = e * column(2, small, small_y)
    go = jnp.concatenate((goa[...], gob[...]), 0).astype(F32)
    grad = go + root * (
        weighted
        - jnp.mean(weighted, axis=0, keepdims=True)
        - n * jnp.mean(weighted * n, axis=0, keepdims=True)
    )
    gm[...] = grad
    rounded = grad.astype(BF)
    low[...] = rounded
    low_b[...] = rounded[low_b.shape[0] :]
    n2 = 2 * DH
    mine = dot(w[...], rounded).astype(BF)
    sibs = dot(w_sib[...], rounded).astype(BF)
    g_own[...] = mine[:n2]
    g_sib[...] = sibs[:n2]
    for i, out in enumerate((g_y, g_x, g_xy)):
        rows = slice(n2 * (i + 1), n2 * (i + 2))
        out[:n2, :] = mine[rows]
        out[n2:, :] = sibs[rows]
    for i, q in enumerate((e * n, e, grad, go)):
        sums[i : i + 1, :] = row_of(jnp.sum(q, axis=1, keepdims=True))
    sums[4:, :] = jnp.zeros_like(sums[4:, :])


def heads_outer_kernel(scal, own, y, sib, ysib, low, low_x, sums, sums_x, keep, send):
    right = jnp.concatenate((low[...], low_x[...]), 1)
    n2 = 2 * DH
    for rows, a, b, out in ((slice(0, n2), own, y, keep), (slice(n2, 2 * n2), sib, ysib, send)):
        out[head_rows(scal[0]), :] = dot_nt(a[rows, :], right).astype(out.dtype)
        out[head_rows(1 - scal[0]), :] = dot_nt(b[rows, :], right).astype(out.dtype)
        total = sums[...] + sums_x[...]
        out[2 * n2 :, :] = jnp.concatenate((total, total), 0).astype(out.dtype)


def qkv_outer_kernel(dqkv, h1, keep_o, recv_o, own, send):
    total = dot_nt(dqkv[...], h1[...])
    half = h1.shape[0] // 2
    lanes = own.shape[1]
    rows = jnp.concatenate([total[PITCH * i : PITCH * i + DH] for i in range(6)], 0)
    n = 6 * DH
    own[:n, :] = padded_units(rows[:, :half].astype(BF), lanes)
    send[:n, :] = padded_units(rows[:, half:].astype(BF), lanes)
    col = jnp.sum(dqkv[...].astype(F32), axis=1, keepdims=True)
    cols = [col[PITCH * i : PITCH * i + DH] for i in (0, 1, 4, 5)]
    cols.append(jnp.zeros((lanes - 4 * DH, 1), F32))
    own[n : n + 16, :] = jnp.broadcast_to(row_of(jnp.concatenate(cols, 0)), (16, lanes)).astype(BF)
    outs = keep_o[...] + recv_o[...].astype(F32)
    own[n + 16 :, :] = padded_units(outs[:, :half].astype(BF), lanes)
    send[n:, :] = padded_units(outs[:, half:].astype(BF), lanes)


def gather_kernel(own, recv, out):
    n = 6 * DH
    out[: n + 16, :] = own[: n + 16, :]
    out[n + 16 : 2 * n + 16, :] = recv[:n, :]
    out[2 * n + 16 :, :] = (own[n + 16 :, :].astype(F32) + recv[n:, :].astype(F32)).astype(BF)


def part_kernel(w, dqkv, send):
    send[...] = dot(w[...], dqkv[:, 4 * SUB :]).astype(BF)


HALF = SUB // 2


def spread_kernel(w, dqkv, recv, to_x, to_y, keep_p, keep_q):
    half = w.shape[0] // 2
    total = dot(w[...], dqkv[:, : 4 * SUB]) + recv[...].astype(F32)
    for ry in range(2):
        at = slice(ry * HALF, (ry + 1) * HALF)
        for rx in range(2):
            first = (ry * 2 + rx) * SUB
            p = total[:, first : first + HALF]
            q = total[:, first + HALF : first + SUB]
            if rx == 0:
                keep_p[:, at] = p
            else:
                to_x[:, at] = p.astype(BF)
            where = slice((ry * 2 + rx) * HALF, (ry * 2 + rx + 1) * HALF)
            keep_q[:, where] = q[:half]
            to_y[:, where] = q[half:].astype(BF)


def spread2_kernel(keep_p, keep_q, from_x, from_y, to_x, to_y, own_p, own_q):
    half = own_p.shape[0]
    p = keep_p[...] + from_x[...].astype(F32)
    own_p[...] = p[:half]
    to_y[...] = p[half:].astype(BF)
    for ry in range(2):
        at = slice(ry * HALF, (ry + 1) * HALF)
        for rx in range(2):
            mine = slice((ry * 2 + rx) * HALF, (ry * 2 + rx + 1) * HALF)
            theirs = slice(((1 - ry) * 2 + rx) * HALF, ((1 - ry) * 2 + rx + 1) * HALF)
            q = keep_q[:, mine] + from_y[:, theirs].astype(F32)
            if rx == 0:
                own_q[:, at] = q
            else:
                to_x[:, at] = q.astype(BF)


def norm1_stats_kernel(scal, own_p, own_q, from_x, from_y, a, b, small, grad, normed, stats, sums):
    ypos = scal[0]
    half = a.shape[0]
    gain = column(0, small)
    cols_sums = [0.0, 0.0]
    for ry in range(2):
        at = slice(ry * HALF, (ry + 1) * HALF)
        other = slice((1 - ry) * HALF, (2 - ry) * HALF)
        e = jnp.concatenate(
            (own_p[:, at] + from_y[:, other].astype(F32), own_q[:, at] + from_x[:, at].astype(F32)), 1
        )
        here = slice(ry * SUB, (ry + 1) * SUB)
        cols = span(ypos ^ ry)
        va, vb = a[:, cols].astype(F32), b[:, cols].astype(F32)
        mean = (jnp.sum(va, 0, keepdims=True) + jnp.sum(vb, 0, keepdims=True)) / (2 * half)
        square = (jnp.sum(va * va, 0, keepdims=True) + jnp.sum(vb * vb, 0, keepdims=True)) / (2 * half)
        root = lax.rsqrt(square - mean * mean + EPSILON)
        n = (va - mean) * root
        w = e * gain
        grad[:, here] = w
        normed[:, here] = n
        stats[0:1, here] = jnp.sum(w, 0, keepdims=True)
        stats[1:2, here] = jnp.sum(w * n, 0, keepdims=True)
        stats[2:3, here] = root
        cols_sums[0] += jnp.sum(e * n, 1, keepdims=True)
        cols_sums[1] += jnp.sum(e, 1, keepdims=True)
    stats[3:, :] = jnp.zeros_like(stats[3:, :])
    for i in range(2):
        sums[i : i + 1, :] = row_of(cols_sums[i])
    sums[2:, :] = jnp.zeros_like(sums[2:, :])


def norm1_back_kernel(scal, grad, normed, stats, recv, gm_own, gm_y, out):
    ypos = scal[0]
    width = 2 * grad.shape[0]
    for ry in range(2):
        here = slice(ry * SUB, (ry + 1) * SUB)
        other = slice((1 - ry) * SUB, (2 - ry) * SUB)
        total = (stats[0:1, here] + recv[0:1, other]) / width
        along = (stats[1:2, here] + recv[1:2, other]) / width
        gm = gm_own[: grad.shape[0], :] if ry == 0 else gm_y[...].astype(F32)
        whole = gm + stats[2:3, here] * (grad[:, here] - total - normed[:, here] * along)
        out[:, span(ypos ^ ry)] = whole.astype(BF)


def local(
    layer_input, picture, token_kept, ln1_gain, ln1_bias, w_query, b_query, w_key, w_value, b_value,
    w_out, b_out, ln2_gain, ln2_bias, w_up, b_up, w_down, b_down, grad_out,
):
    ypos = lax.axis_index("tc").astype(jnp.int32)
    trpos = lax.axis_index("tr").astype(jnp.int32)
    me = trpos * 2 + ypos
    half = layer_input.shape[1]
    width = 2 * half
    seq = picture.shape[0]
    n2 = b_query.shape[0]
    units = w_up.shape[1]
    n_up = b_up.shape[0]
    scal = jnp.stack((ypos, me))
    two = 2 * SUB

    a00 = layer_input.T
    qkv_weights = (w_query.T, w_key.T, w_value.T)
    go_t = grad_out.T
    u_aa, d_aa = w_up, w_down.T
    small = jnp.stack(
        (ln1_gain, ln1_bias, ln2_gain, ln2_bias, b_out, b_down, jnp.pad(b_up, (0, half - n_up)), ln1_gain)
    )
    (w_send,) = call(pack_kernel, "pack", (scal,), qkv_weights, (shape(3 * n2, half),), 1)
    b00, a10, a01, small_y, d_as = py(a00), px(a00), pc(a00), py(small), pc(d_aa)
    go_a = cols_at(go_t, ypos * SUB, SUB)
    go_send = cols_at(go_t, (1 - ypos) * SUB, SUB)
    quarter = half // lax.axis_size("dp")
    first = lax.axis_index("dp") * quarter
    u_part, d_part = rows_at(u_aa, first, quarter), rows_at(d_aa, first, quarter)
    qkv_bias = jnp.concatenate((b_query, jnp.zeros_like(b_query), b_value)).reshape(6, DH)
    ones = (jnp.arange(6) >= 4).astype(F32)[:, None]
    qkv_bias = jnp.concatenate((qkv_bias, ones, jnp.zeros((6, PITCH - DH - 1), F32)), 1).reshape(1, -1)
    qkv_bias = jnp.broadcast_to(qkv_bias, (8, 6 * PITCH))

    numbers = jnp.arange(8, dtype=jnp.int32)[:, None]
    hot = (picture[None, :] == numbers).astype(jnp.int32)
    counts = jnp.sum(hot, axis=1)
    kept = jnp.sum(hot * token_kept[None, :], axis=1)
    starts = jnp.cumsum(counts) - counts
    lo = jnp.sum(hot * starts[:, None], axis=0)
    hi = jnp.sum(hot * (starts + kept)[:, None], axis=0)
    end = jnp.sum(hot * (starts + counts)[:, None], axis=0)
    blocks = seq // SUB
    klo = qlo = lo.reshape(blocks, SUB)[:, 0] // SUB
    lasts = jnp.arange(1, blocks + 1, dtype=jnp.int32) * SUB
    khi = (jnp.maximum(lasts, hi.reshape(blocks, SUB)[:, -1]) + SUB - 1) // SUB
    qhi = (jnp.maximum(lasts, end.reshape(blocks, SUB)[:, -1]) + SUB - 1) // SUB
    lo, hi = lo[None, :], hi[None, :]

    b00, a10, a01, small_y, d_as, w_send, u_part = phase(b00, a10, a01, small_y, d_as, w_send, u_part)
    b10, w_other, b01, a11, u_part = px(b00), py(w_send), pc(b00), pc(a10), py(u_part)
    b10, w_other, b01, a11, u_part, w_out1, go_send, go_a, d_part = phase(
        b10, w_other, b01, a11, u_part, w_out, go_send, go_a, d_part
    )
    u_ba = lax.all_gather(u_part, "dp", axis=0, tiled=True)
    b11, w0b, w2a, go_b, d_part = pc(b10), py(w_out1), px(w_out1), py(go_send), py(d_part)
    go_xa = px(after(go_a, b11))
    wt_all, w_all = call(
        unpack_kernel, "unpack", (scal,), qkv_weights + (w_other,),
        (shape(6 * PITCH, width), shape(width, 6 * PITCH)), 2,
    )
    h1, qkv, kv, resid = call(
        norm_qkv_kernel, "norm_qkv", (scal,),
        (a00, b00, a01, b01, a10, b10, a11, b11, wt_all, qkv_bias, small, small_y),
        (shape(width, seq), shape(6 * PITCH, seq), shape(seq, 512), shape(width, two)),
        8,
        scratch=[pltpu.VMEM((width, SUB), F32)] * 2 + [pltpu.VMEM((6 * PITCH, SUB), F32)],
    )

    o0, o1, lse = call(
        attend_kernel, "attend", (scal, klo, khi), (qkv, kv, lo, hi),
        (shape(2 * n2, two),) * 2 + (shape(2, seq, dtype=F32),), 12,
        scratch=[pltpu.VMEM((2, seq, SUB), F32), pltpu.VMEM((2, PITCH, SUB), F32)],
    )
    o0, o1, w0b, w2a, go_b, go_xa, d_part, u_ba = phase(o0, o1, w0b, w2a, go_b, go_xa, d_part, u_ba)
    d_ba = lax.all_gather(d_part, "dp", axis=0, tiled=True)
    att_y, att_x, att_s, w2b, go_xb = py(o1), px(o0), pc(o0), py(w2a), px(go_b)
    up_y = small_y[6, :n_up]
    up_own = jnp.where(ypos == 0, jnp.concatenate((b_up, up_y)), jnp.concatenate((up_y, b_up)))
    att_y, att_x, att_s, w2b, go_xb, up_own, u_aa1 = phase(att_y, att_x, att_s, w2b, go_xb, up_own, u_aa)
    att_xy, att_sy, att_sx, u_as, up_sib = px(att_y), pc(att_y), pc(att_x), pc(u_aa1), pc(up_own)
    (wo,) = call(out_weights_kernel, "out_weights", (scal,), (w_out, w0b, w2a, w2b), (shape(4 * n2, width),), 1)
    gof, go = call(
        turn_kernel, "turn", (), (go_a, go_b, go_xa, go_xb), (shape(width, two), shape(two, width)), 2
    )
    att_xy, att_sy, att_sx, wo1, u_as, up_sib, u_ba, d_ba = phase(
        att_xy, att_sy, att_sx, wo, u_as, up_sib, u_ba, d_ba
    )
    att_sxy, wo_sib, u_bs, d_bs = pc(att_xy), pc(wo1), pc(u_ba), pc(d_ba)
    bias_up = jnp.stack((up_own, up_sib))
    mixed, h2t, h2 = call(
        mix_kernel, "mix", (),
        (o0, att_y, att_x, att_xy, att_s, att_sy, att_sx, att_sxy, wo, wo_sib, resid, small, small_y),
        (shape(width, two, dtype=F32), shape(width, two), shape(two, width)), 5,
    )
    held = pltpu.VMEM((width, units), BF)
    four = pltpu.SemaphoreType.DMA((4,))
    u_shape = shape(two, units)
    sum_shape = shape(8, units, dtype=F32)
    act0, gu0, gu_sums0, gh_part = call(
        feed_own_kernel, "feed_own", (), (h2, go, bias_up),
        (u_shape, u_shape, sum_shape, shape(width, two, dtype=F32)), 7, vmem=24,
        scratch=[held, held, four], far=(u_aa, u_ba, d_aa, d_ba),
    )
    act1, gu1, gu_sums1, gh_send, gh_own = call(
        feed_sib_kernel, "feed_sib", (), (h2, go, bias_up, gh_part),
        (u_shape, u_shape, sum_shape, shape(width, SUB), shape(width, SUB, dtype=F32)), 7, vmem=24,
        scratch=[held, held, four], far=(u_as, u_bs, d_as, d_bs),
    )
    gh_recv = px(gh_send)
    wide = (units + 127) // 128 * 128
    d_send, u_send = call(
        outers_kernel, "outers", (), (gof, act1, h2t, gu1, gu_sums1), (shape(width, wide), shape(width + 16, wide)), 4
    )
    d_recv, u_recv = pc(d_send), pc(u_send)
    keep_d, d_send = call(
        down_own_kernel, "down_own", (), (gof, act0, d_recv), (shape(half, wide, dtype=F32), shape(half, wide)), 2,
    )
    d_recv = py(d_send)
    keep_u, u_send = call(
        up_own_kernel, "up_own", (), (h2t, after(gu0, d_send), gu_sums0, u_recv),
        (shape(half + 16, wide, dtype=F32), shape(half + 16, wide)), 2,
    )
    r_send, r_own = call(
        result_kernel, "result", (), (act0, act1, after(mixed, u_send), small, small_y),
        (shape(width, SUB), shape(width, SUB, dtype=F32)), 6, vmem=20,
        scratch=[held, held, four], far=(d_aa, d_ba, d_as, d_bs),
    )
    gm, low, low_b, g_own, g_sib, g_y, g_x, g_xy, sums2 = call(
        norm2_back_kernel, "norm2_back", (),
        (gh_own, gh_recv, mixed, go_a, go_b, after(small, r_send), small_y, wo, wo_sib),
        (shape(width, SUB, dtype=F32), shape(width, SUB), shape(half, SUB))
        + (shape(n2, SUB),) * 2
        + (shape(2 * n2, SUB),) * 3
        + (shape(8, width, dtype=F32),),
        4,
    )
    g_x, g_xy, g_y, g_s = px(g_x), px(g_xy), py(g_y), pc(g_sib)
    g_x, g_xy, g_y, g_s, low1, r_send, u_send = phase(g_x, g_xy, g_y, g_s, low, r_send, u_send)
    g_xy, g_sx, g_sy = py(g_xy), pc(g_x), pc(g_y)
    g_xy, g_sx, g_sy, d_recv = phase(g_xy, g_sx, g_sy, d_recv)
    g_sxy = pc(g_xy)
    d_sum = (keep_d + d_recv.astype(F32)).astype(BF)
    low_x, u_recv, d_in, r_recv, sums2_x = px(low1), py(after(u_send, d_recv)), line(0, d_sum), px(r_send), px(sums2)
    heads = phase(qkv, kv, lo, hi, lse, o0, o1, g_own, g_x, g_y, g_xy, g_s, g_sx, g_sy, g_sxy, d_sum)[:-1]
    (dqkv,) = call(
        attend_back_kernel, "attend_back", (scal, qlo, qhi), heads, (shape(6 * PITCH, seq),), 19,
        scratch=[
            pltpu.VMEM((2 * PITCH, seq), BF), pltpu.VMEM((2, seq), F32), pltpu.VMEM((2 * PITCH, seq), F32),
            pltpu.VMEM((2, seq, PITCH), F32), pltpu.VMEM((2, seq, PITCH), F32),
        ],
    )
    dqkv, low_x, u_recv, d_in, r_recv, sums2_x = phase(dqkv, low_x, u_recv, d_in, r_recv, sums2_x)
    d_sum = line_sum(d_sum, d_in)
    u_sum = (keep_u + u_recv.astype(F32)).astype(BF)

    (p_send,) = call(part_kernel, "part", (), (w_all, dqkv), (shape(width, 4 * SUB),), 3)
    d_in, u_in, p_recv = line(1, d_sum), line(0, u_sum), pc(p_send)
    keep_o, o_send = call(
        heads_outer_kernel, "heads_outer", (scal,), (o0, att_y, att_s, att_sy, after(low, p_send), low_x, sums2, sums2_x),
        (shape(2 * n2 + 16, width, dtype=F32), shape(2 * n2 + 16, width)), 2,
    )
    o_recv = pc(o_send)
    r_a, r_b = call(
        result_sum_kernel, "result_sum", (), (r_own, after(r_recv, o_send)), (shape(half, SUB), shape(half, SUB)), 1
    )
    lanes = (half + 127) // 128 * 128
    q_own, q_send = call(
        qkv_outer_kernel, "qkv_outer", (), (after(dqkv, r_b), h1, keep_o, o_recv),
        (shape(5 * n2 + 32, lanes), shape(5 * n2 + 16, lanes)), 4,
    )
    to_x, to_y, keep_p, keep_q = call(
        spread_kernel, "spread", (), (w_all, after(dqkv, q_send), p_recv),
        (shape(width, SUB), shape(half, two), shape(width, SUB, dtype=F32), shape(half, two, dtype=F32)), 4,
    )
    q_y, from_x, from_y = py(q_send), px(to_x), py(to_y)
    from_x, from_y, q_y, d_in, u_in = phase(from_x, from_y, q_y, d_in, u_in)
    d_sum, u_sum = line_sum(d_sum, d_in), line_sum(u_sum, u_in)
    to_x2, to_y2, own_p, own_q = call(
        spread2_kernel, "spread2", (), (keep_p, keep_q, from_x, from_y),
        (shape(half, SUB), shape(half, SUB), shape(half, SUB, dtype=F32), shape(half, SUB, dtype=F32)), 2,
    )
    (qo_sum,) = call(gather_kernel, "gather", (), (q_own, q_y), (shape(8 * n2 + 32, lanes),), 1)
    from_x2, from_y2 = px(to_x2), py(to_y2)
    d_in, u_in, qo_in = line(2, d_sum), line(1, u_sum), line(0, qo_sum)
    from_x2, from_y2, low_b, r_b = phase(from_x2, from_y2, low_b, r_b)
    grad, normed, stats, sums1 = call(
        norm1_stats_kernel, "norm1_stats", (scal,), (own_p, own_q, from_x2, from_y2, a00, b00, small),
        (shape(half, two, dtype=F32), shape(half, two, dtype=F32), shape(8, two, dtype=F32), shape(8, half, dtype=F32)),
        2,
    )
    stats_y, sums1_c = py(stats), pc(sums1)
    stats_y, sums1_c, low_b, r_b = phase(stats_y, sums1_c, low_b, r_b)
    sums1 = sums1 + sums1_c
    sums1_x, low_y = px(sums1), py(low_b)
    d_in, u_in, qo_in, sums1_x, low_y, r_b = phase(d_in, u_in, qo_in, sums1_x, low_y, r_b)
    u_sum, qo_sum = line_sum(u_sum, u_in), line_sum(qo_sum, qo_in)
    sums1 = sums1 + sums1_x
    u_in, qo_in, sums1_z, r_y = line(2, u_sum), line(1, qo_sum), dp_step(sums1, 1), py(r_b)
    dwd = line_end(d_sum, d_in)
    (gin,) = call(
        norm1_back_kernel, "norm1_back", (scal,), (grad, normed, stats, stats_y, gm, low_y), (shape(half, two),), 1,
    )
    u_in, qo_in, sums1_z, gin, r_y, dwd = phase(u_in, qo_in, sums1_z, gin, r_y, dwd)
    sums1 = sums1 + sums1_z
    qo_sum = line_sum(qo_sum, qo_in)
    qo_in, sums1_z = line(2, qo_sum), dp_step(sums1, 2)
    dwu = line_end(u_sum, u_in)
    (result,) = call(place_kernel, "place", (scal,), (r_a, r_y), (shape(half, two),), 1)
    qo_in, sums1_z, dwu, result = phase(qo_in, sums1_z, dwu, result)
    sums1 = dp_last(sums1 + sums1_z)
    qo = line_end(qo_sum, qo_in)[:, :half]
    dwq_own, dwq_y, dwo = qo[: 3 * n2 + 16], qo[3 * n2 + 16 : 6 * n2 + 16], qo[6 * n2 + 16 :]

    bias_q = dwq_own[3 * n2]
    dwq_own = dwq_own[: 3 * n2]
    first = jnp.where(ypos == 0, dwq_own, dwq_y).reshape(3, n2, half)
    second = jnp.where(ypos == 0, dwq_y, dwq_own).reshape(3, n2, half)
    dwq = jnp.concatenate((first, second), 1)
    gbu = lax.dynamic_slice_in_dim(dwu[half], ypos * n_up, n_up, 0)
    sums2 = dwo[2 * n2 :]
    return (
        result.T, gin.T, sums1[0], sums1[1], dwq[0].T, bias_q[:n2], dwq[1].T, dwq[2].T, bias_q[n2 : 2 * n2],
        dwo[: 2 * n2], sums2[2], sums2[0], sums2[1], dwu[:half, :units], gbu, dwd[:, :units].T, sums2[3],
    )


def solution(mesh):
    rows = P(("dp", "tr"), "tc")
    placed = (
        rows, P("dp"), P("dp"), P("tc"), P("tc"), P("tc", "tr"), P(("tr", "tc")), P("tc", "tr"),
        P("tc", "tr"), P(("tr", "tc")), P("tr", "tc"), P("tc"), P("tc"), P("tc"), P("tc", "tr"),
        P(("tr", "tc")), P("tr", "tc"), P("tc"), rows,
    )
    outs = (
        rows, rows, P("tc"), P("tc"), P("tc", "tr"), P(("tr", "tc")), P("tc", "tr"), P("tc", "tr"),
        P(("tr", "tc")), P("tr", "tc"), P("tc"), P("tc"), P("tc"), P("tc", "tr"), P(("tr", "tc")),
        P("tr", "tc"), P("tc"),
    )
    return jax.shard_map(local, mesh=mesh, in_specs=placed, out_specs=outs, check_vma=False)
```

time: 536 us -> 418 us (0.78)
  blocking collectives: 102 us -> 0 us
  local copies, waits for them, and re-layouts: 92.1 us -> 44.3 us
  waiting for transfers between devices: 135 us -> 167 us
  matrix products: 24.1 us -> 0 us
  starting transfers between devices: 43.7 us -> 67.8 us
  other arithmetic: 27.9 us -> 19.5 us
    psum x3 -> x0, blocking collectives: 102 us -> none  [the longest x1 59.8 us: local(): lax.psum(jnp.concatenate((sums1, sums2, sum_down), 1), ('dp', 'tr'))]
    ppermute x0 -> x11, waiting for transfers between devices: none -> 69.9 us  [the longest x9 48.3 us: line(): lax.ppermute(v, 'dp', ([(0, 1), (3, 2)], [(1, 2), (2, 1)], [(1, 0), (2, 3...]
    ppermute x15 -> x16, waiting for transfers between devices: 65.8 us -> 26.9 us  [px(): return lax.ppermute(v, 'tr', swap_perm('tr', 2))]
    ppermute x0 -> x11, starting transfers between devices: none -> 24.8 us  [the longest x9 16.7 us: line(): lax.ppermute(v, 'dp', ([(0, 1), (3, 2)], [(1, 2), (2, 1)], [(1, 0), (2, 3...]
    dot_general x8 -> x0, matrix products: 24.1 us -> none  [the longest x4 14 us: dot_nt(): lax.dot_general(a, b, (((1,), (1,)), ((), ())), preferred_element_type=F32)]
    unnamed x273 -> x154, local copies, waits for them, and re-layouts: 43.2 us -> 26.5 us
    slice x20 -> x8, local copies, waits for them, and re-layouts: 19.5 us -> 4.48 us  [the longest x1 1.67 us: local(): dwu[:half, :units]]
    ppermute x22 -> x19, waiting for transfers between devices: 69.2 us -> 56.7 us  [py(): return lax.ppermute(v, 'tc', swap_perm('tc', 1))]
  transfers between devices with their start and end apart: 57 -> 71, of which waited for: 15 -> 28; matrix products, arithmetic and copies ran while one was open for 20% -> 5% of each run, Pallas kernels for 15% -> 20%
where the time goes in v3:
time: 418 us; the launch traced here: 410 us
  waiting for transfers between devices  167 us (40%)
  Pallas kernels  95.8 us (23%)
  starting transfers between devices  67.8 us (16%)
  local copies, waits for them, and re-layouts  44.3 us (11%)
  other arithmetic  19.5 us (5%)
  between operations  15.6 us (4%)
    pallas_call x25, Pallas kernels, call(): pl.pallas_call(body, out_shape=tuple(outs), in_specs=[SM] * len(scalars)...  95.8 us
    ppermute x19, waiting for transfers between devices, py(): return lax.ppermute(v, 'tc', swap_perm('tc', 1))  56.7 us
    ppermute x9, waiting for transfers between devices, line(): lax.ppermute(v, 'dp', ([(0, 1), (3, 2)], [(1, 2), (2, 1)], [(1, 0), (2, 3...  48.3 us
    ppermute x16, waiting for transfers between devices, px(): return lax.ppermute(v, 'tr', swap_perm('tr', 2))  26.9 us
    unnamed x154, local copies, waits for them, and re-layouts  26.5 us
    ppermute x2, waiting for transfers between devices, dp_swap(): return lax.ppermute(v, 'dp', swap_perm('dp', bit))  21.6 us
    ppermute x16, starting transfers between devices, px(): return lax.ppermute(v, 'tr', swap_perm('tr', 2))  19.4 us
    ppermute x19, starting transfers between devices, py(): return lax.ppermute(v, 'tc', swap_perm('tc', 1))  19.2 us
  transfers between devices with their start and end apart: 71, of which 28 were waited for; matrix products, arithmetic and copies ran while one was open for 5% of the time, Pallas kernels for 20%

profile of v3, /device:TPU:0, one launch (start us, length us, event | category | flops | bytes accessed | tf_op | source)
XLA Modules:
  0.0 410.1 jit_solution(17961578384360869826)
XLA Ops:
  7.8 2.9 collective-permute-start.1
  18.7 1.7 constant_dynamic-slice_fusion
  27.0 1.7 collective-permute-start.6
  29.1 1.8 dynamic-slice_bitcast_fusion.1
  30.9 1.7 dynamic-slice_bitcast_fusion
  32.6 16.4 %collective-permute-done.9 = bf16[144,1076]{1,0:T(8,128)(2,1)} collective-permute-done((bf16[144,1076]{1,0:T(8,128)(2,1)}, bf16[144,1076]{1,0:T(8,128)(2,1)}, u32[]{:S(2)}, u32[]{:S(2)}) %collective-permute-start.9) | collective-permute-done | bytes 309920 | tf_op jit(solution)/shard_map/ppermute | solution.py:35
  49.8 1.7 collective-permute-start.12
  58.1 1.6 unpack.1
  61.3 7.0 %norm_qkv.1 = (bf16[1152,2048]{1,0:T(8,128)(2,1)S(1)}, bf16[480,2048]{1,0:T(8,128)(2,1)S(1)}, bf16[2048,512]{1,0:T(8,128)(2,1)S(1)}, bf16[1152,512]{1,0:T(8,128)(2,1)S(1)}) custom-call(s32[2]{0:T(128)S(1)} %pad_add_fusion.scal, bf16[576,512]{1,0:T(8,128)(2,1)S(1)} %bitcast.49, bf16[576,512]{1,0:T(8,128)(2,1)S(1)} %collective-permute-done.b00.b, ...), custom_call_target="tpu_custom_call" | custom-call | flops 4800000000 | bytes 24000000 | tf_op jit(solution)/shard_map/norm_qkv/pallas_call | solution.py:109
  68.2 2.2 copy-done.52
  71.4 13.6 %attend.1 = (bf16[288,512]{1,0:T(8,128)(2,1)S(1)}, bf16[288,512]{1,0:T(8,128)(2,1)S(1)}, f32[2,2048]{1,0:T(2,128)S(1)}) custom-call(s32[2]{0:T(128)S(1)} %pad_add_fusion.scal, s32[8]{0:T(128)S(1)} %get-tuple-element.374.klo.qlo, s32[8]{0:T(128)S(1)} %get-tuple-element.373.khi, bf16[480,2048]{1,0:T(8,128)(2,1)S(1)} %get-tuple-element.268.qkv, ...), custom_call_target="tpu_custom_call" | custom-call | flops 7200000000 | bytes 36000000 | tf_op jit(solution)/shard_map/attend/pallas_call | solution.py:109
  85.6 1.7 collective-permute-start.16
  88.0 1.5 collective-permute-start.20
  90.1 11.1 %collective-permute-done.16.y = bf16[288,512]{1,0:T(8,128)(2,1)} collective-permute-done((bf16[288,512]{1,0:T(8,128)(2,1)S(1)}, bf16[288,512]{1,0:T(8,128)(2,1)}, u32[]{:S(2)}, u32[]{:S(2)}) %collective-permute-start.16) | collective-permute-done | bytes 294944 | tf_op jit(solution)/shard_map/ppermute | solution.py:35
  107.8 5.1 %collective-permute-done.21.xy = bf16[288,512]{1,0:T(8,128)(2,1)} collective-permute-done((bf16[288,512]{1,0:T(8,128)(2,1)}, bf16[288,512]{1,0:T(8,128)(2,1)}, u32[]{:S(2)}, u32[]{:S(2)}) %collective-permute-start.21) | collective-permute-done | bytes 294944 | tf_op jit(solution)/shard_map/ppermute | solution.py:27
  114.0 3.2 all-gather.5.cloned.1.call-done.db.dba
  119.3 1.6 turn.1
  120.9 3.8 collective-permute-done.26.xysib
  124.8 4.3 %mix.1 = (f32[1152,512]{1,0:T(8,128)S(1)}, bf16[1152,512]{1,0:T(8,128)(2,1)S(1)}, bf16[512,1152]{1,0:T(8,128)(2,1)S(1)}) custom-call(bf16[288,512]{1,0:T(8,128)(2,1)S(1)} %copy-done.33, bf16[288,512]{1,0:T(8,128)(2,1)} %collective-permute-done.16.y, bf16[288,512]{1,0:T(8,128)(2,1)} %collective-permute-done.17.x, ...), custom_call_target="tpu_custom_call" | custom-call | flops 3000000000 | bytes 15000000 | tf_op jit(solution)/shard_map/mix/pallas_call | solution.py:109
  129.1 8.2 %feed_own.1 = (bf16[512,1076]{1,0:T(8,128)(2,1)S(1)}, bf16[512,1076]{1,0:T(8,128)(2,1)S(1)}, f32[8,1076]{1,0:T(8,128)S(1)}, f32[1152,512]{1,0:T(8,128)S(1)}) custom-call(bf16[512,1152]{1,0:T(8,128)(2,1)S(1)} %get-tuple-element.224.h2, bf16[512,1152]{1,0:T(8,128)(2,1)S(1)} %get-tuple-element.227.go, f32[2,1076]{1,0:T(2,128)S(1)} %pad_maximum_fusion.1.bias, ...), custom_call_target="tpu_custom_call" | custom-call | flops 4200000000 | bytes 21000000 | tf_op jit(solution)/shard_map/feed_own/pallas_call | solution.py:109
  137.4 7.4 %feed_sib.1 = (bf16[512,1076]{1,0:T(8,128)(2,1)S(1)}, bf16[512,1076]{1,0:T(8,128)(2,1)S(1)}, f32[8,1076]{1,0:T(8,128)S(1)}, bf16[1152,256]{1,0:T(8,128)(2,1)S(1)}, f32[1152,256]{1,0:T(8,128)S(1)}) custom-call(bf16[512,1152]{1,0:T(8,128)(2,1)S(1)} %get-tuple-element.224.h2, bf16[512,1152]{1,0:T(8,128)(2,1)S(1)} %get-tuple-element.227.go, ...), custom_call_target="tpu_custom_call" | custom-call | flops 4200000000 | bytes 21000000 | tf_op jit(solution)/shard_map/feed_sib/pallas_call | solution.py:109
  144.8 3.3 outers.1
  148.6 4.4 %collective-permute-done.31.recv = bf16[1152,1152]{1,0:T(8,128)(2,1)S(1)} collective-permute-done((bf16[1152,1152]{1,0:T(8,128)(2,1)S(1)}, bf16[1152,1152]{1,0:T(8,128)(2,1)S(1)}, u32[]{:S(2)}, u32[]{:S(2)}) %collective-permute-start.31) | collective-permute-done | bytes 2654240 | tf_op jit(solution)/shard_map/ppermute | solution.py:31
  153.0 2.8 down_own.1
  160.2 1.7 up_own.1
  163.1 4.0 result.1
  167.1 6.7 %collective-permute-done.30.recv = bf16[1152,256]{1,0:T(8,128)(2,1)S(1)} collective-permute-done((bf16[1152,256]{1,0:T(8,128)(2,1)S(1)}, bf16[1152,256]{1,0:T(8,128)(2,1)S(1)}, u32[]{:S(2)}, u32[]{:S(2)}) %collective-permute-start.30) | collective-permute-done | bytes 589856 | tf_op jit(solution)/shard_map/ppermute | solution.py:27
  173.9 3.3 norm2_back.1
  185.6 2.0 collective-permute-done.33.gx
  187.5 1.7 collective-permute-done.34
  189.2 2.6 collective-permute-done.35.gy
  193.8 3.4 collective-permute-done.37.gxy
  197.3 2.5 add_convert_fusion.7
  199.8 2.9 collective-permute-start.44
  208.1 1.5 copy-done.66
  209.6 21.5 %attend_back.1.dqkv = bf16[480,2048]{1,0:T(8,128)(2,1)S(1)} custom-call(s32[2]{0:T(128)S(1)} %pad_add_fusion.scal, s32[8]{0:T(128)S(1)} %get-tuple-element.374.klo.qlo, s32[8]{0:T(128)S(1)} %and_select_fusion.1.qhi, bf16[480,2048]{1,0:T(8,128)(2,1)S(1)} %copy-done.66, bf16[2048,512]{1,0:T(8,128)(2,1)S(1)} %copy-done.64, s32[1,2048]{1,0:T(1,128)S(1)} %bitcast.45, ...), custom_call_target="tpu_custom_call" | custom-call | flops 11399999488 | bytes 57000000 | tf_op jit(solution)/shard_map/attend_back/pallas_call | solution.py:109
  231.2 2.9 collective-permute-done.45.recv
  236.0 1.7 collective-permute-start.53
  237.7 2.6 heads_outer.1
  242.6 3.0 qkv_outer.1
  250.3 17.4 %collective-permute-done.53 = bf16[592,1152]{1,0:T(8,128)(2,1)S(1)} collective-permute-done((bf16[592,1152]{1,0:T(8,128)(2,1)S(1)}, bf16[592,1152]{1,0:T(8,128)(2,1)S(1)}, u32[]{:S(2)}, u32[]{:S(2)}) %collective-permute-start.53) | collective-permute-done | bytes 1364000 | tf_op jit(solution)/shard_map/ppermute | solution.py:73
  267.6 1.8 collective-permute-done.51.recv
  269.4 12.1 %collective-permute-done.50.from_y = bf16[576,512]{1,0:T(8,128)(2,1)S(1)} collective-permute-done((bf16[576,512]{1,0:T(8,128)(2,1)S(1)}, bf16[576,512]{1,0:T(8,128)(2,1)S(1)}, u32[]{:S(2)}, u32[]{:S(2)}) %collective-permute-start.50) | collective-permute-done | bytes 589856 | tf_op jit(solution)/shard_map/ppermute | solution.py:35
  282.8 4.8 %collective-permute-start.56 = (bf16[1184,640]{1,0:T(8,128)(2,1)S(1)}, bf16[1184,640]{1,0:T(8,128)(2,1)S(1)}, u32[]{:S(2)}, u32[]{:S(2)}) collective-permute-start(bf16[1184,640]{1,0:T(8,128)(2,1)S(1)} %gather.1), channel_id=1, source_target_pairs={{0,8},{24,16},{1,9},{25,17},{2,10},{26,18},{3,11},{27,19},{4,12},{... | collective-permute-start | bytes 4546568 | tf_op jit(solution)/shard_map/ppermute | solution.py:73
  291.2 5.6 %collective-permute-done.57.from_x = bf16[576,256]{1,0:T(8,128)(2,1)S(1)} collective-permute-done((bf16[576,256]{1,0:T(8,128)(2,1)S(1)}, bf16[576,256]{1,0:T(8,128)(2,1)S(1)}, u32[]{:S(2)}, u32[]{:S(2)}) %collective-permute-start.57) | collective-permute-done | bytes 294944 | tf_op jit(solution)/shard_map/ppermute | solution.py:27
  297.6 1.9 norm1_stats.1
  300.2 3.2 collective-permute-done.59.recv
  304.9 2.8 collective-permute-done.61
  307.7 4.2 %collective-permute-done.62.gm_y = bf16[576,256]{1,0:T(8,128)(2,1)S(1)} collective-permute-done((bf16[576,256]{1,0:T(8,128)(2,1)S(1)}, bf16[576,256]{1,0:T(8,128)(2,1)S(1)}, u32[]{:S(2)}, u32[]{:S(2)}) %collective-permute-start.62) | collective-permute-done | bytes 294944 | tf_op jit(solution)/shard_map/ppermute | solution.py:35
  311.8 7.3 %collective-permute-done.54 = bf16[576,1152]{1,0:T(8,128)(2,1)S(1)} collective-permute-done((bf16[576,1152]{1,0:T(8,128)(2,1)S(1)}, bf16[576,1152]{1,0:T(8,128)(2,1)S(1)}, u32[]{:S(2)}, u32[]{:S(2)}) %collective-permute-start.54) | collective-permute-done | bytes 1327136 | tf_op jit(solution)/shard_map/ppermute | solution.py:73
  320.3 1.5 add_convert_fusion.1
  321.8 1.8 collective-permute-start.64
  326.4 3.7 collective-permute-start.65
  330.6 3.0 select_convert_fusion.2
  333.6 1.6 norm1_back.1
  335.3 21.6 %collective-permute-done.65 = f32[8,576]{1,0:T(8,128)S(1)} collective-permute-done((f32[8,576]{1,0:T(8,128)S(1)}, f32[8,576]{1,0:T(8,128)S(1)}, u32[]{:S(2)}, u32[]{:S(2)}) %collective-permute-start.65) | collective-permute-done | bytes 18464 | tf_op jit(solution)/shard_map/ppermute | solution.py:67
  356.8 3.4 add_convert_fusion
  361.5 4.4 %collective-permute-start.68 = (f32[8,576]{1,0:T(8,128)S(1)}, f32[8,576]{1,0:T(8,128)S(1)}, u32[]{:S(2)}, u32[]{:S(2)}) collective-permute-start(f32[8,576]{1,0:T(8,128)S(1)} %add.94), channel_id=1, source_target_pairs={{0,16},{8,24},{16,0},{24,8},{1,17},{9,25},{17,1},{25,9},{2,18},{10... | collective-permute-start | bytes 55304 | tf_op jit(solution)/shard_map/ppermute | solution.py:67
  365.9 1.7 slice_bitcast_fusion
  367.6 1.6 select_convert_fusion.1
  369.2 1.7 place.1
  370.9 23.6 %collective-permute-done.67 = bf16[1184,640]{1,0:T(8,128)(2,1)} collective-permute-done((bf16[1184,640]{1,0:T(8,128)(2,1)}, bf16[1184,640]{1,0:T(8,128)(2,1)}, u32[]{:S(2)}, u32[]{:S(2)}) %collective-permute-start.67) | collective-permute-done | bytes 1515552 | tf_op jit(solution)/shard_map/ppermute | solution.py:73
  394.5 1.7 slice.106
  396.2 1.6 select_convert_fusion
  (325 shorter events, 85.9 us)
Async XLA Ops:
  7.2 78.0 %all-gather.3.cloned.1.call-start = ((), (), s32[]{:S(2)}) async-start(), calls=%async_computation | async-start | bytes 1658880 | tf_op jit(solution)/shard_map/all_gather | solution.py:640
  7.2 19.2 %collective-permute-start.4 = (bf16[576,1076]{1,0:T(8,128)(2,1)}, bf16[576,1076]{1,0:T(8,128)(2,1)S(1)}, u32[]{:S(2)}, u32[]{:S(2)}) collective-permute-start(bf16[576,1076]{1,0:T(8,128)(2,1)} %bitcast.39), channel_id=1, source_target_pairs={{0,2},{2,0},{4,6},{6,4},{1,3},{3,1},{5,7},{7,5},{8,10},{10,8},{12,... | collective-permute-start | bytes 3718664 | tf_op jit(solution)/shard_map/ppermute | solution.py:31
  7.8 18.7 %collective-permute-start.2 = (bf16[576,512]{1,0:T(8,128)(2,1)}, bf16[576,512]{1,0:T(8,128)(2,1)S(1)}, u32[]{:S(2)}, u32[]{:S(2)}) collective-permute-start(bf16[576,512]{1,0:T(8,128)(2,1)} %bitcast.46), channel_id=1, source_target_pairs={{0,2},{2,0},{4,6},{6,4},{1,3},{3,1},{5,7},{7,5},{8,10},{10,8},{12,... | collective-permute-start | bytes 1769480 | tf_op jit(solution)/shard_map/ppermute | solution.py:31
  7.8 18.6 %collective-permute-start.1 = (bf16[576,512]{1,0:T(8,128)(2,1)}, bf16[576,512]{1,0:T(8,128)(2,1)}, u32[]{:S(2)}, u32[]{:S(2)}) collective-permute-start(bf16[576,512]{1,0:T(8,128)(2,1)} %bitcast.47), channel_id=1, source_target_pairs={{0,4},{2,6},{4,0},{6,2},{1,5},{3,7},{5,1},{7,3},{8,12},{10,14},{12... | collective-permute-start | bytes 1769480 | tf_op jit(solution)/shard_map/ppermute | solution.py:27
  10.7 15.7 %collective-permute-start = (bf16[576,512]{1,0:T(8,128)(2,1)}, bf16[576,512]{1,0:T(8,128)(2,1)S(1)}, u32[]{:S(2)}, u32[]{:S(2)}) collective-permute-start(bf16[576,512]{1,0:T(8,128)(2,1)} %bitcast.48), channel_id=1, source_target_pairs={{0,1},{1,0},{2,3},{3,2},{4,5},{5,4},{6,7},{7,6},{8,9},{9,8},{10,11... | collective-permute-start | bytes 1769480 | tf_op jit(solution)/shard_map/ppermute | solution.py:35
  17.1 9.3 %collective-permute-start.3 = (f32[8,576]{1,0:T(8,128)S(1)}, f32[8,576]{1,0:T(8,128)S(1)}, u32[]{:S(2)}, u32[]{:S(2)}) collective-permute-start(f32[8,576]{1,0:T(8,128)S(1)} %stack.53.small), channel_id=1, source_target_pairs={{0,1},{1,0},{2,3},{3,2},{4,5},{5,4},{6,7},{7,6},{8,9},{9,8},{10,11... | collective-permute-start | bytes 55304 | tf_op jit(solution)/shard_map/ppermute | solution.py:35
  26.5 22.5 %collective-permute-start.7 = (bf16[576,512]{1,0:T(8,128)(2,1)S(1)}, bf16[576,512]{1,0:T(8,128)(2,1)}, u32[]{:S(2)}, u32[]{:S(2)}) collective-permute-start(bf16[576,512]{1,0:T(8,128)(2,1)S(1)} %collective-permute-done.b00.b), channel_id=1, source_target_pairs={{0,2},{2,0},{4,6},{6,4},{1,3},{3,1},{5,7},{7,5},{8,10},{10,8},{12,... | collective-permute-start | bytes 1769480 | tf_op jit(solution)/shard_map/ppermute | solution.py:31
  26.6 22.5 %collective-permute-start.5 = (bf16[576,512]{1,0:T(8,128)(2,1)S(1)}, bf16[576,512]{1,0:T(8,128)(2,1)}, u32[]{:S(2)}, u32[]{:S(2)}) collective-permute-start(bf16[576,512]{1,0:T(8,128)(2,1)S(1)} %collective-permute-done.b00.b), channel_id=1, source_target_pairs={{0,4},{2,6},{4,0},{6,2},{1,5},{3,7},{5,1},{7,3},{8,12},{10,14},{12... | collective-permute-start | bytes 1769480 | tf_op jit(solution)/shard_map/ppermute | solution.py:27
  27.0 22.0 %collective-permute-start.6 = (bf16[432,576]{1,0:T(8,128)(2,1)}, bf16[432,576]{1,0:T(8,128)(2,1)}, u32[]{:S(2)}, u32[]{:S(2)}) collective-permute-start(bf16[432,576]{1,0:T(8,128)(2,1)} %copy-done.25), channel_id=1, source_target_pairs={{0,1},{1,0},{2,3},{3,2},{4,5},{5,4},{6,7},{7,6},{8,9},{9,8},{10,11... | collective-permute-start | bytes 1493000 | tf_op jit(solution)/shard_map/ppermute | solution.py:35
  28.7 20.3 %collective-permute-start.8 = (bf16[576,512]{1,0:T(8,128)(2,1)}, bf16[576,512]{1,0:T(8,128)(2,1)}, u32[]{:S(2)}, u32[]{:S(2)}) collective-permute-start(bf16[576,512]{1,0:T(8,128)(2,1)} %collective-permute-done.1.a10), channel_id=1, source_target_pairs={{0,2},{2,0},{4,6},{6,4},{1,3},{3,1},{5,7},{7,5},{8,10},{10,8},{12,... | collective-permute-start | bytes 1769480 | tf_op jit(solution)/shard_map/ppermute | solution.py:31
  28.8 20.2 %collective-permute-start.9 = (bf16[144,1076]{1,0:T(8,128)(2,1)}, bf16[144,1076]{1,0:T(8,128)(2,1)}, u32[]{:S(2)}, u32[]{:S(2)}) collective-permute-start(bf16[144,1076]{1,0:T(8,128)(2,1)} %constant_dynamic-slice_fusion), channel_id=1, source_target_pairs={{0,1},{1,0},{2,3},{3,2},{4,5},{5,4},{6,7},{7,6},{8,9},{9,8},{10,11... | collective-permute-start | bytes 929672 | tf_op jit(solution)/shard_map/ppermute | solution.py:35
  49.1 68.1 %all-gather.5.cloned.1.call-start = ((), (), s32[]{:S(2)}) async-start(), calls=%async_computation.1 | async-start | bytes 1658880 | tf_op jit(solution)/shard_map/all_gather | solution.py:661
  49.1 11.6 %collective-permute-start.10 = (bf16[576,512]{1,0:T(8,128)(2,1)}, bf16[576,512]{1,0:T(8,128)(2,1)}, u32[]{:S(2)}, u32[]{:S(2)}) collective-permute-start(bf16[576,512]{1,0:T(8,128)(2,1)} %collective-permute-done.5.b10), channel_id=1, source_target_pairs={{0,2},{2,0},{4,6},{6,4},{1,3},{3,1},{5,7},{7,5},{8,10},{10,8},{12,... | collective-permute-start | bytes 1769480 | tf_op jit(solution)/shard_map/ppermute | solution.py:31
  49.8 35.3 %collective-permute-start.12 = (bf16[288,576]{1,0:T(8,128)(2,1)S(1)}, bf16[288,576]{1,0:T(8,128)(2,1)S(1)}, u32[]{:S(2)}, u32[]{:S(2)}) collective-permute-start(bf16[288,576]{1,0:T(8,128)(2,1)S(1)} %copy-done.5), channel_id=1, source_target_pairs={{0,4},{2,6},{4,0},{6,2},{1,5},{3,7},{5,1},{7,3},{8,12},{10,14},{12... | collective-permute-start | bytes 995336 | tf_op jit(solution)/shard_map/ppermute | solution.py:27
  51.5 33.6 %collective-permute-start.11 = (bf16[288,576]{1,0:T(8,128)(2,1)S(1)}, bf16[288,576]{1,0:T(8,128)(2,1)S(1)}, u32[]{:S(2)}, u32[]{:S(2)}) collective-permute-start(bf16[288,576]{1,0:T(8,128)(2,1)S(1)} %copy-done.5), channel_id=1, source_target_pairs={{0,1},{1,0},{2,3},{3,2},{4,5},{5,4},{6,7},{7,6},{8,9},{9,8},{10,11... | collective-permute-start | bytes 995336 | tf_op jit(solution)/shard_map/ppermute | solution.py:35
  53.1 32.0 %collective-permute-start.13 = (bf16[576,256]{1,0:T(8,128)(2,1)}, bf16[576,256]{1,0:T(8,128)(2,1)}, u32[]{:S(2)}, u32[]{:S(2)}) collective-permute-start(bf16[576,256]{1,0:T(8,128)(2,1)} %get-tuple-element.201), channel_id=1, source_target_pairs={{0,1},{1,0},{2,3},{3,2},{4,5},{5,4},{6,7},{7,6},{8,9},{9,8},{10,11... | collective-permute-start | bytes 884744 | tf_op jit(solution)/shard_map/ppermute | solution.py:35
  53.6 31.5 %collective-permute-start.15 = (bf16[144,1076]{1,0:T(8,128)(2,1)}, bf16[144,1076]{1,0:T(8,128)(2,1)}, u32[]{:S(2)}, u32[]{:S(2)}) collective-permute-start(bf16[144,1076]{1,0:T(8,128)(2,1)} %dynamic-slice_bitcast_fusion), channel_id=1, source_target_pairs={{0,1},{1,0},{2,3},{3,2},{4,5},{5,4},{6,7},{7,6},{8,9},{9,8},{10,11... | collective-permute-start | bytes 929672 | tf_op jit(solution)/shard_map/ppermute | solution.py:35
  60.7 24.4 %collective-permute-start.14 = (bf16[576,256]{1,0:T(8,128)(2,1)S(1)}, bf16[576,256]{1,0:T(8,128)(2,1)}, u32[]{:S(2)}, u32[]{:S(2)}) collective-permute-start(bf16[576,256]{1,0:T(8,128)(2,1)S(1)} %get-tuple-element.203.oa.goa), channel_id=1, source_target_pairs={{0,4},{2,6},{4,0},{6,2},{1,5},{3,7},{5,1},{7,3},{8,12},{10,14},{12... | collective-permute-start | bytes 884744 | tf_op jit(solution)/shard_map/ppermute | solution.py:27
  85.2 17.5 %collective-permute-start.19 = (bf16[288,576]{1,0:T(8,128)(2,1)S(1)}, bf16[288,576]{1,0:T(8,128)(2,1)S(1)}, u32[]{:S(2)}, u32[]{:S(2)}) collective-permute-start(bf16[288,576]{1,0:T(8,128)(2,1)S(1)} %collective-permute-done.12.x_a), channel_id=1, source_target_pairs={{0,1},{1,0},{2,3},{3,2},{4,5},{5,4},{6,7},{7,6},{8,9},{9,8},{10,11... | collective-permute-start | bytes 995336 | tf_op jit(solution)/shard_map/ppermute | solution.py:35
  85.6 15.7 %collective-permute-start.16 = (bf16[288,512]{1,0:T(8,128)(2,1)S(1)}, bf16[288,512]{1,0:T(8,128)(2,1)}, u32[]{:S(2)}, u32[]{:S(2)}) collective-permute-start(bf16[288,512]{1,0:T(8,128)(2,1)S(1)} %get-tuple-element.274.o1), channel_id=1, source_target_pairs={{0,1},{1,0},{2,3},{3,2},{4,5},{5,4},{6,7},{7,6},{8,9},{9,8},{10,11... | collective-permute-start | bytes 884744 | tf_op jit(solution)/shard_map/ppermute | solution.py:35
  88.0 13.3 %collective-permute-start.20 = (bf16[576,256]{1,0:T(8,128)(2,1)}, bf16[576,256]{1,0:T(8,128)(2,1)S(1)}, u32[]{:S(2)}, u32[]{:S(2)}) collective-permute-start(bf16[576,256]{1,0:T(8,128)(2,1)} %collective-permute-done.13.ob.gob), channel_id=1, source_target_pairs={{0,4},{2,6},{4,0},{6,2},{1,5},{3,7},{5,1},{7,3},{8,12},{10,14},{12... | collective-permute-start | bytes 884744 | tf_op jit(solution)/shard_map/ppermute | solution.py:27
  89.5 12.4 %collective-permute-start.18 = (bf16[288,512]{1,0:T(8,128)(2,1)S(1)}, bf16[288,512]{1,0:T(8,128)(2,1)S(1)}, u32[]{:S(2)}, u32[]{:S(2)}) collective-permute-start(bf16[288,512]{1,0:T(8,128)(2,1)S(1)} %get-tuple-element.273.own.o0), channel_id=1, source_target_pairs={{0,2},{2,0},{4,6},{6,4},{1,3},{3,1},{5,7},{7,5},{8,10},{10,8},{12,... | collective-permute-start | bytes 884744 | tf_op jit(solution)/shard_map/ppermute | solution.py:31
  89.6 13.1 %collective-permute-start.17 = (bf16[288,512]{1,0:T(8,128)(2,1)S(1)}, bf16[288,512]{1,0:T(8,128)(2,1)}, u32[]{:S(2)}, u32[]{:S(2)}) collective-permute-start(bf16[288,512]{1,0:T(8,128)(2,1)S(1)} %get-tuple-element.273.own.o0), channel_id=1, source_target_pairs={{0,4},{2,6},{4,0},{6,2},{1,5},{3,7},{5,1},{7,3},{8,12},{10,14},{12... | collective-permute-start | bytes 884744 | tf_op jit(solution)/shard_map/ppermute | solution.py:27
  102.7 10.3 %collective-permute-start.24 = (bf16[576,1076]{1,0:T(8,128)(2,1)}, bf16[576,1076]{1,0:T(8,128)(2,1)S(1)}, u32[]{:S(2)}, u32[]{:S(2)}) collective-permute-start(bf16[576,1076]{1,0:T(8,128)(2,1)} %ua.1), channel_id=1, source_target_pairs={{0,2},{2,0},{4,6},{6,4},{1,3},{3,1},{5,7},{7,5},{8,10},{10,8},{12,... | collective-permute-start | bytes 3718664 | tf_op jit(solution)/shard_map/ppermute | solution.py:31
  103.2 3.9 collective-permute-start.22
  103.3 9.7 %collective-permute-start.21 = (bf16[288,512]{1,0:T(8,128)(2,1)}, bf16[288,512]{1,0:T(8,128)(2,1)}, u32[]{:S(2)}, u32[]{:S(2)}) collective-permute-start(bf16[288,512]{1,0:T(8,128)(2,1)} %collective-permute-done.16.y), channel_id=1, source_target_pairs={{0,4},{2,6},{4,0},{6,2},{1,5},{3,7},{5,1},{7,3},{8,12},{10,14},{12... | collective-permute-start | bytes 884744 | tf_op jit(solution)/shard_map/ppermute | solution.py:27
  117.2 7.5 %collective-permute-start.27 = (bf16[576,1152]{1,0:T(8,128)(2,1)S(1)}, bf16[576,1152]{1,0:T(8,128)(2,1)S(1)}, u32[]{:S(2)}, u32[]{:S(2)}) collective-permute-start(bf16[576,1152]{1,0:T(8,128)(2,1)S(1)} %out_weights.1.w), channel_id=1, source_target_pairs={{0,2},{2,0},{4,6},{6,4},{1,3},{3,1},{5,7},{7,5},{8,10},{10,8},{12,... | collective-permute-start | bytes 3981320 | tf_op jit(solution)/shard_map/ppermute | solution.py:31
  117.2 20.1 %collective-permute-start.28 = (bf16[576,1076]{1,0:T(8,128)(2,1)}, bf16[576,1076]{1,0:T(8,128)(2,1)S(1)}, u32[]{:S(2)}, u32[]{:S(2)}) collective-permute-start(bf16[576,1076]{1,0:T(8,128)(2,1)} %all-gather.3.cloned.1.call-done.ub), channel_id=1, source_target_pairs={{0,2},{2,0},{4,6},{6,4},{1,3},{3,1},{5,7},{7,5},{8,10},{10,8},{12,... | collective-permute-start | bytes 3718664 | tf_op jit(solution)/shard_map/ppermute | solution.py:31
  117.7 19.6 %collective-permute-start.29 = (bf16[576,1076]{1,0:T(8,128)(2,1)}, bf16[576,1076]{1,0:T(8,128)(2,1)S(1)}, u32[]{:S(2)}, u32[]{:S(2)}) collective-permute-start(bf16[576,1076]{1,0:T(8,128)(2,1)} %all-gather.5.cloned.1.call-done.db.dba), channel_id=1, source_target_pairs={{0,2},{2,0},{4,6},{6,4},{1,3},{3,1},{5,7},{7,5},{8,10},{10,8},{12,... | collective-permute-start | bytes 3718664 | tf_op jit(solution)/shard_map/ppermute | solution.py:31
  117.8 6.9 %collective-permute-start.26 = (bf16[288,512]{1,0:T(8,128)(2,1)}, bf16[288,512]{1,0:T(8,128)(2,1)S(1)}, u32[]{:S(2)}, u32[]{:S(2)}) collective-permute-start(bf16[288,512]{1,0:T(8,128)(2,1)} %collective-permute-done.21.xy), channel_id=1, source_target_pairs={{0,2},{2,0},{4,6},{6,4},{1,3},{3,1},{5,7},{7,5},{8,10},{10,8},{12,... | collective-permute-start | bytes 884744 | tf_op jit(solution)/shard_map/ppermute | solution.py:31
  148.0 5.0 %collective-permute-start.31 = (bf16[1152,1152]{1,0:T(8,128)(2,1)S(1)}, bf16[1152,1152]{1,0:T(8,128)(2,1)S(1)}, u32[]{:S(2)}, u32[]{:S(2)}) collective-permute-start(bf16[1152,1152]{1,0:T(8,128)(2,1)S(1)} %get-tuple-element.244), channel_id=1, source_target_pairs={{0,2},{2,0},{4,6},{6,4},{1,3},{3,1},{5,7},{7,5},{8,10},{10,8},{12,... | collective-permute-start | bytes 7962632 | tf_op jit(solution)/shard_map/ppermute | solution.py:31
  148.2 12.0 %collective-permute-start.32 = (bf16[1168,1152]{1,0:T(8,128)(2,1)S(1)}, bf16[1168,1152]{1,0:T(8,128)(2,1)S(1)}, u32[]{:S(2)}, u32[]{:S(2)}) collective-permute-start(bf16[1168,1152]{1,0:T(8,128)(2,1)S(1)} %get-tuple-element.248), channel_id=1, source_target_pairs={{0,2},{2,0},{4,6},{6,4},{1,3},{3,1},{5,7},{7,5},{8,10},{10,8},{12,... | collective-permute-start | bytes 8073224 | tf_op jit(solution)/shard_map/ppermute | solution.py:31
  157.3 39.9 %collective-permute-start.40 = (bf16[576,1152]{1,0:T(8,128)(2,1)}, bf16[576,1152]{1,0:T(8,128)(2,1)}, u32[]{:S(2)}, u32[]{:S(2)}) collective-permute-start(bf16[576,1152]{1,0:T(8,128)(2,1)} %get-tuple-element.245), channel_id=1, source_target_pairs={{0,1},{1,0},{2,3},{3,2},{4,5},{5,4},{6,7},{7,6},{8,9},{9,8},{10,11... | collective-permute-start | bytes 3981320 | tf_op jit(solution)/shard_map/ppermute | solution.py:35
  158.8 15.1 %collective-permute-start.30 = (bf16[1152,256]{1,0:T(8,128)(2,1)S(1)}, bf16[1152,256]{1,0:T(8,128)(2,1)S(1)}, u32[]{:S(2)}, u32[]{:S(2)}) collective-permute-start(bf16[1152,256]{1,0:T(8,128)(2,1)S(1)} %get-tuple-element.235), channel_id=1, source_target_pairs={{0,4},{2,6},{4,0},{6,2},{1,5},{3,7},{5,1},{7,3},{8,12},{10,14},{12... | collective-permute-start | bytes 1769480 | tf_op jit(solution)/shard_map/ppermute | solution.py:27
  181.1 6.4 %collective-permute-start.33 = (bf16[288,256]{1,0:T(8,128)(2,1)S(1)}, bf16[288,256]{1,0:T(8,128)(2,1)S(1)}, u32[]{:S(2)}, u32[]{:S(2)}) collective-permute-start(bf16[288,256]{1,0:T(8,128)(2,1)S(1)} %get-tuple-element.254), channel_id=1, source_target_pairs={{0,4},{2,6},{4,0},{6,2},{1,5},{3,7},{5,1},{7,3},{8,12},{10,14},{12... | collective-permute-start | bytes 442376 | tf_op jit(solution)/shard_map/ppermute | solution.py:27
  182.6 6.7 %collective-permute-start.34 = (bf16[288,256]{1,0:T(8,128)(2,1)S(1)}, bf16[288,256]{1,0:T(8,128)(2,1)}, u32[]{:S(2)}, u32[]{:S(2)}) collective-permute-start(bf16[288,256]{1,0:T(8,128)(2,1)S(1)} %get-tuple-element.255), channel_id=1, source_target_pairs={{0,4},{2,6},{4,0},{6,2},{1,5},{3,7},{5,1},{7,3},{8,12},{10,14},{12... | collective-permute-start | bytes 442376 | tf_op jit(solution)/shard_map/ppermute | solution.py:27
  183.1 8.7 %collective-permute-start.35 = (bf16[288,256]{1,0:T(8,128)(2,1)S(1)}, bf16[288,256]{1,0:T(8,128)(2,1)S(1)}, u32[]{:S(2)}, u32[]{:S(2)}) collective-permute-start(bf16[288,256]{1,0:T(8,128)(2,1)S(1)} %get-tuple-element.256), channel_id=1, source_target_pairs={{0,1},{1,0},{2,3},{3,2},{4,5},{5,4},{6,7},{7,6},{8,9},{9,8},{10,11... | collective-permute-start | bytes 442376 | tf_op jit(solution)/shard_map/ppermute | solution.py:35
  191.8 5.4 %collective-permute-start.37 = (bf16[288,256]{1,0:T(8,128)(2,1)}, bf16[288,256]{1,0:T(8,128)(2,1)S(1)}, u32[]{:S(2)}, u32[]{:S(2)}) collective-permute-start(bf16[288,256]{1,0:T(8,128)(2,1)} %collective-permute-done.34), channel_id=1, source_target_pairs={{0,1},{1,0},{2,3},{3,2},{4,5},{5,4},{6,7},{7,6},{8,9},{9,8},{10,11... | collective-permute-start | bytes 442376 | tf_op jit(solution)/shard_map/ppermute | solution.py:35
  193.3 3.9 collective-permute-start.38
  193.3 3.9 collective-permute-start.39
  199.8 34.3 %collective-permute-start.44 = (bf16[576,1152]{1,0:T(8,128)(2,1)S(1)}, bf16[576,1152]{1,0:T(8,128)(2,1)S(1)}, u32[]{:S(2)}, u32[]{:S(2)}) collective-permute-start(bf16[576,1152]{1,0:T(8,128)(2,1)S(1)} %add_convert_fusion.7), channel_id=1, source_target_pairs={{0,8},{24,16},{1,9},{25,17},{2,10},{26,18},{3,11},{27,19},{4,12},{... | collective-permute-start | bytes 3981320 | tf_op jit(solution)/shard_map/ppermute | solution.py:73
  202.7 31.4 %collective-permute-start.43 = (bf16[592,1152]{1,0:T(8,128)(2,1)S(1)}, bf16[592,1152]{1,0:T(8,128)(2,1)S(1)}, u32[]{:S(2)}, u32[]{:S(2)}) collective-permute-start(bf16[592,1152]{1,0:T(8,128)(2,1)S(1)} %copy-done.8), channel_id=1, source_target_pairs={{0,1},{1,0},{2,3},{3,2},{4,5},{5,4},{6,7},{7,6},{8,9},{9,8},{10,11... | collective-permute-start | bytes 4091912 | tf_op jit(solution)/shard_map/ppermute | solution.py:35
  204.5 26.7 %collective-permute-start.46 = (f32[8,1152]{1,0:T(8,128)S(1)}, f32[8,1152]{1,0:T(8,128)S(1)}, u32[]{:S(2)}, u32[]{:S(2)}) collective-permute-start(f32[8,1152]{1,0:T(8,128)S(1)} %copy-done.51), channel_id=1, source_target_pairs={{0,4},{2,6},{4,0},{6,2},{1,5},{3,7},{5,1},{7,3},{8,12},{10,14},{12... | collective-permute-start | bytes 110600 | tf_op jit(solution)/shard_map/ppermute | solution.py:27
  206.0 25.2 %collective-permute-start.42 = (bf16[1152,256]{1,0:T(8,128)(2,1)S(1)}, bf16[1152,256]{1,0:T(8,128)(2,1)S(1)}, u32[]{:S(2)}, u32[]{:S(2)}) collective-permute-start(bf16[1152,256]{1,0:T(8,128)(2,1)S(1)} %copy-done.22), channel_id=1, source_target_pairs={{0,4},{2,6},{4,0},{6,2},{1,5},{3,7},{5,1},{7,3},{8,12},{10,14},{12... | collective-permute-start | bytes 1769480 | tf_op jit(solution)/shard_map/ppermute | solution.py:27
  206.6 27.5 %collective-permute-start.45 = (bf16[1152,256]{1,0:T(8,128)(2,1)S(1)}, bf16[1152,256]{1,0:T(8,128)(2,1)S(1)}, u32[]{:S(2)}, u32[]{:S(2)}) collective-permute-start(bf16[1152,256]{1,0:T(8,128)(2,1)S(1)} %copy-done.24), channel_id=1, source_target_pairs={{0,4},{2,6},{4,0},{6,2},{1,5},{3,7},{5,1},{7,3},{8,12},{10,14},{12... | collective-permute-start | bytes 1769480 | tf_op jit(solution)/shard_map/ppermute | solution.py:27
  235.5 10.7 %collective-permute-start.48 = (bf16[1152,1024]{1,0:T(8,128)(2,1)S(1)}, bf16[1152,1024]{1,0:T(8,128)(2,1)S(1)}, u32[]{:S(2)}, u32[]{:S(2)}) collective-permute-start(bf16[1152,1024]{1,0:T(8,128)(2,1)S(1)} %part.1), channel_id=1, source_target_pairs={{0,2},{2,0},{4,6},{6,4},{1,3},{3,1},{5,7},{7,5},{8,10},{10,8},{12,... | collective-permute-start | bytes 7077896 | tf_op jit(solution)/shard_map/ppermute | solution.py:31
  236.0 31.6 %collective-permute-start.53 = (bf16[592,1152]{1,0:T(8,128)(2,1)S(1)}, bf16[592,1152]{1,0:T(8,128)(2,1)S(1)}, u32[]{:S(2)}, u32[]{:S(2)}) collective-permute-start(bf16[592,1152]{1,0:T(8,128)(2,1)S(1)} %add_convert_fusion.4), channel_id=1, source_target_pairs={{0,8},{24,16},{1,9},{25,17},{2,10},{26,18},{3,11},{27,19},{4,12},{... | collective-permute-start | bytes 4091912 | tf_op jit(solution)/shard_map/ppermute | solution.py:73
  241.2 9.1 %collective-permute-start.52 = (bf16[576,1152]{1,0:T(8,128)(2,1)S(1)}, bf16[576,1152]{1,0:T(8,128)(2,1)S(1)}, u32[]{:S(2)}, u32[]{:S(2)}) collective-permute-start(bf16[576,1152]{1,0:T(8,128)(2,1)S(1)} %add_convert_fusion.6), channel_id=1, source_target_pairs={{8,16},{16,8},{9,17},{17,9},{10,18},{18,10},{11,19},{19,11},{12,20... | collective-permute-start | bytes 3981320 | tf_op jit(solution)/shard_map/ppermute | solution.py:73
  245.6 23.8 %collective-permute-start.51 = (bf16[736,640]{1,0:T(8,128)(2,1)S(1)}, bf16[736,640]{1,0:T(8,128)(2,1)S(1)}, u32[]{:S(2)}, u32[]{:S(2)}) collective-permute-start(bf16[736,640]{1,0:T(8,128)(2,1)S(1)} %get-tuple-element.302), channel_id=1, source_target_pairs={{0,1},{1,0},{2,3},{3,2},{4,5},{5,4},{6,7},{7,6},{8,9},{9,8},{10,11... | collective-permute-start | bytes 2826248 | tf_op jit(solution)/shard_map/ppermute | solution.py:35
  247.7 21.7 %collective-permute-start.49 = (bf16[1152,256]{1,0:T(8,128)(2,1)S(1)}, bf16[1152,256]{1,0:T(8,128)(2,1)S(1)}, u32[]{:S(2)}, u32[]{:S(2)}) collective-permute-start(bf16[1152,256]{1,0:T(8,128)(2,1)S(1)} %get-tuple-element.304), channel_id=1, source_target_pairs={{0,4},{2,6},{4,0},{6,2},{1,5},{3,7},{5,1},{7,3},{8,12},{10,14},{12... | collective-permute-start | bytes 1769480 | tf_op jit(solution)/shard_map/ppermute | solution.py:27
  248.8 32.7 %collective-permute-start.50 = (bf16[576,512]{1,0:T(8,128)(2,1)S(1)}, bf16[576,512]{1,0:T(8,128)(2,1)S(1)}, u32[]{:S(2)}, u32[]{:S(2)}) collective-permute-start(bf16[576,512]{1,0:T(8,128)(2,1)S(1)} %get-tuple-element.305), channel_id=1, source_target_pairs={{0,1},{1,0},{2,3},{3,2},{4,5},{5,4},{6,7},{7,6},{8,9},{9,8},{10,11... | collective-permute-start | bytes 1769480 | tf_op jit(solution)/shard_map/ppermute | solution.py:35
  281.9 37.3 %collective-permute-start.55 = (bf16[592,1152]{1,0:T(8,128)(2,1)S(1)}, bf16[592,1152]{1,0:T(8,128)(2,1)S(1)}, u32[]{:S(2)}, u32[]{:S(2)}) collective-permute-start(bf16[592,1152]{1,0:T(8,128)(2,1)S(1)} %add_convert_fusion.3), channel_id=1, source_target_pairs={{8,16},{16,8},{9,17},{17,9},{10,18},{18,10},{11,19},{19,11},{12,20... | collective-permute-start | bytes 4091912 | tf_op jit(solution)/shard_map/ppermute | solution.py:73
  282.8 37.4 %collective-permute-start.56 = (bf16[1184,640]{1,0:T(8,128)(2,1)S(1)}, bf16[1184,640]{1,0:T(8,128)(2,1)S(1)}, u32[]{:S(2)}, u32[]{:S(2)}) collective-permute-start(bf16[1184,640]{1,0:T(8,128)(2,1)S(1)} %gather.1), channel_id=1, source_target_pairs={{0,8},{24,16},{1,9},{25,17},{2,10},{26,18},{3,11},{27,19},{4,12},{... | collective-permute-start | bytes 4546568 | tf_op jit(solution)/shard_map/ppermute | solution.py:73
  287.9 31.2 %collective-permute-start.54 = (bf16[576,1152]{1,0:T(8,128)(2,1)S(1)}, bf16[576,1152]{1,0:T(8,128)(2,1)S(1)}, u32[]{:S(2)}, u32[]{:S(2)}) collective-permute-start(bf16[576,1152]{1,0:T(8,128)(2,1)S(1)} %add_convert_fusion.5), channel_id=1, source_target_pairs={{8,0},{16,24},{9,1},{17,25},{10,2},{18,26},{11,3},{19,27},{12,4},{... | collective-permute-start | bytes 3981320 | tf_op jit(solution)/shard_map/ppermute | solution.py:73
  289.5 7.3 %collective-permute-start.57 = (bf16[576,256]{1,0:T(8,128)(2,1)S(1)}, bf16[576,256]{1,0:T(8,128)(2,1)S(1)}, u32[]{:S(2)}, u32[]{:S(2)}) collective-permute-start(bf16[576,256]{1,0:T(8,128)(2,1)S(1)} %get-tuple-element.318), channel_id=1, source_target_pairs={{0,4},{2,6},{4,0},{6,2},{1,5},{3,7},{5,1},{7,3},{8,12},{10,14},{12... | collective-permute-start | bytes 884744 | tf_op jit(solution)/shard_map/ppermute | solution.py:27
  290.7 6.9 %collective-permute-start.58 = (bf16[576,256]{1,0:T(8,128)(2,1)S(1)}, bf16[576,256]{1,0:T(8,128)(2,1)S(1)}, u32[]{:S(2)}, u32[]{:S(2)}) collective-permute-start(bf16[576,256]{1,0:T(8,128)(2,1)S(1)} %get-tuple-element.319), channel_id=1, source_target_pairs={{0,1},{1,0},{2,3},{3,2},{4,5},{5,4},{6,7},{7,6},{8,9},{9,8},{10,11... | collective-permute-start | bytes 884744 | tf_op jit(solution)/shard_map/ppermute | solution.py:35
  299.5 3.9 collective-permute-start.60
  303.3 8.5 %collective-permute-start.62 = (bf16[576,256]{1,0:T(8,128)(2,1)S(1)}, bf16[576,256]{1,0:T(8,128)(2,1)S(1)}, u32[]{:S(2)}, u32[]{:S(2)}) collective-permute-start(bf16[576,256]{1,0:T(8,128)(2,1)S(1)} %copy-done.43), channel_id=1, source_target_pairs={{0,1},{1,0},{2,3},{3,2},{4,5},{5,4},{6,7},{7,6},{8,9},{9,8},{10,11... | collective-permute-start | bytes 884744 | tf_op jit(solution)/shard_map/ppermute | solution.py:35
  321.8 35.0 %collective-permute-start.64 = (bf16[1184,640]{1,0:T(8,128)(2,1)}, bf16[1184,640]{1,0:T(8,128)(2,1)}, u32[]{:S(2)}, u32[]{:S(2)}) collective-permute-start(bf16[1184,640]{1,0:T(8,128)(2,1)} %add_convert_fusion.1), channel_id=1, source_target_pairs={{8,16},{16,8},{9,17},{17,9},{10,18},{18,10},{11,19},{19,11},{12,20... | collective-permute-start | bytes 4546568 | tf_op jit(solution)/shard_map/ppermute | solution.py:73
  325.1 31.8 %collective-permute-start.63 = (bf16[592,1152]{1,0:T(8,128)(2,1)}, bf16[592,1152]{1,0:T(8,128)(2,1)}, u32[]{:S(2)}, u32[]{:S(2)}) collective-permute-start(bf16[592,1152]{1,0:T(8,128)(2,1)} %add_convert_fusion.2), channel_id=1, source_target_pairs={{8,0},{16,24},{9,1},{17,25},{10,2},{18,26},{11,3},{19,27},{12,4},{... | collective-permute-start | bytes 4091912 | tf_op jit(solution)/shard_map/ppermute | solution.py:73
  326.4 30.4 %collective-permute-start.65 = (f32[8,576]{1,0:T(8,128)S(1)}, f32[8,576]{1,0:T(8,128)S(1)}, u32[]{:S(2)}, u32[]{:S(2)}) collective-permute-start(f32[8,576]{1,0:T(8,128)S(1)} %add.92), channel_id=1, source_target_pairs={{0,8},{8,0},{16,24},{24,16},{1,9},{9,1},{17,25},{25,17},{2,10},{10... | collective-permute-start | bytes 55304 | tf_op jit(solution)/shard_map/ppermute | solution.py:67
  330.1 26.7 %collective-permute-start.66 = (bf16[576,256]{1,0:T(8,128)(2,1)S(1)}, bf16[576,256]{1,0:T(8,128)(2,1)S(1)}, u32[]{:S(2)}, u32[]{:S(2)}) collective-permute-start(bf16[576,256]{1,0:T(8,128)(2,1)S(1)} %get-tuple-element.338), channel_id=1, source_target_pairs={{0,1},{1,0},{2,3},{3,2},{4,5},{5,4},{6,7},{7,6},{8,9},{9,8},{10,11... | collective-permute-start | bytes 884744 | tf_op jit(solution)/shard_map/ppermute | solution.py:35
  360.2 34.3 %collective-permute-start.67 = (bf16[1184,640]{1,0:T(8,128)(2,1)}, bf16[1184,640]{1,0:T(8,128)(2,1)}, u32[]{:S(2)}, u32[]{:S(2)}) collective-permute-start(bf16[1184,640]{1,0:T(8,128)(2,1)} %add_convert_fusion), channel_id=1, source_target_pairs={{8,0},{16,24},{9,1},{17,25},{10,2},{18,26},{11,3},{19,27},{12,4},{... | collective-permute-start | bytes 4546568 | tf_op jit(solution)/shard_map/ppermute | solution.py:73
  361.5 9.4 %collective-permute-start.68 = (f32[8,576]{1,0:T(8,128)S(1)}, f32[8,576]{1,0:T(8,128)S(1)}, u32[]{:S(2)}, u32[]{:S(2)}) collective-permute-start(f32[8,576]{1,0:T(8,128)S(1)} %add.94), channel_id=1, source_target_pairs={{0,16},{8,24},{16,0},{24,8},{1,17},{9,25},{17,1},{25,9},{2,18},{10... | collective-permute-start | bytes 55304 | tf_op jit(solution)/shard_map/ppermute | solution.py:67
  (85 other events, 610.5 us)
Sparse Core Ops, SparseCore 0:
  49.2 34.4 all-gather.2
  85.3 31.8 all-gather.4
